TPU v7x, 32 devices: a whole 2x2x4 slice. The times are simulated.
32 devices in a mesh: wide: 8 (over y, x, core), narrow: 4 (over z).
Axes of the slice: x: 2, y: 2, z: 4, core: 2. Of those that a mesh axis runs over, the one named last changes fastest.
Arguments:
- latents: bfloat16 [32, 1024, 768], P(('wide', 'narrow')), may hold values from -6 to 6
- condition: bfloat16 [32, 768], P(('wide', 'narrow')), may hold values from -6 to 6
- valid_mask: int32 [32, 1024], P(('wide', 'narrow')), may hold values from 0 to 1, as said below
- ada_weight: bfloat16 [768, 4608], P(('wide', 'narrow')), may hold values from -0.21875 to 0.21875
- ada_bias: bfloat16 [4608], P(('wide', 'narrow')), may hold values from -3 to 3
- dw1_kernel: bfloat16 [9, 768], P(None, ('wide', 'narrow')), may hold values from -2 to 2
- dw1_bias: bfloat16 [768], P(('wide', 'narrow')), may hold values from -3 to 3
- qkv_weight: bfloat16 [768, 2304], P(('wide', 'narrow')), may hold values from -0.21875 to 0.21875
- proj_weight: bfloat16 [768, 768], P(('wide', 'narrow')), may hold values from -1.25 to 1.25
- proj_bias: bfloat16 [768], P(('wide', 'narrow')), may hold values from -3 to 3
- fc1_weight: bfloat16 [768, 3072], P(('wide', 'narrow')), may hold values from -0.21875 to 0.21875
- fc1_bias: bfloat16 [3072], P(('wide', 'narrow')), may hold values from -3 to 3
- dw2_kernel: bfloat16 [9, 3072], P(None, ('wide', 'narrow')), may hold values from -2 to 2
- dw2_bias: bfloat16 [3072], P(('wide', 'narrow')), may hold values from -3 to 3
- fc2_weight: bfloat16 [3072, 768], P(('wide', 'narrow')), may hold values from -0.109375 to 0.109375
- fc2_bias: bfloat16 [768], P(('wide', 'narrow')), may hold values from -3 to 3
- out_cotangent: bfloat16 [32, 1024, 768], P(('wide', 'narrow')), may hold values from -6 to 6
Outputs:
- block_out: bfloat16 [32, 1024, 768], P(('wide', 'narrow'))
- input_grad: bfloat16 [32, 1024, 768], P(('wide', 'narrow'))
- cond_grad: float32 [32, 768], P(('wide', 'narrow'))
- ada_wgrad: float32 [768, 4608], P(('wide', 'narrow'))
- ada_bgrad: float32 [4608], P(('wide', 'narrow'))
- dw1_kgrad: float32 [9, 768], P(None, ('wide', 'narrow'))
- dw1_bgrad: float32 [768], P(('wide', 'narrow'))
- qkv_grad: float32 [768, 2304], P(('wide', 'narrow'))
- proj_wgrad: float32 [768, 768], P(('wide', 'narrow'))
- proj_bgrad: float32 [768], P(('wide', 'narrow'))
- fc1_wgrad: float32 [768, 3072], P(('wide', 'narrow'))
- fc1_bgrad: float32 [3072], P(('wide', 'narrow'))
- dw2_kgrad: float32 [9, 3072], P(None, ('wide', 'narrow'))
- dw2_bgrad: float32 [3072], P(('wide', 'narrow'))
- fc2_wgrad: float32 [3072, 768], P(('wide', 'narrow'))
- fc2_bgrad: float32 [768], P(('wide', 'narrow'))
Inputs may be any that keep to these rules, and one draw needn't show every extreme that they name: `valid_mask`: in each latent the valid tokens are those of the first h rows and first w columns of its 32 x 32 grid, h and w even and at least 16; at least one latent of every draw is wholly valid.
All inputs are finite; a program needn't handle non-finite values.
Results may differ from a plain program's by a relative error of at most 0.014.
The roundings to bfloat16 on the way count: a program that leaves them out, or rounds other values in their place, can miss the bound.
Values may be sent and summed in bfloat16 or wider, within the bound.
A program may use at most 384 MiB of HBM per device.

v0:
```python
import jax
import jax.numpy as jnp
from jax import lax
from jax.sharding import PartitionSpec as P

HEAD = 64
GRID = 32


def smooth_gate(values):
    return values * jax.nn.sigmoid(values)


def gelu_tanh(values):
    return (
        0.5
        * values
        * (1.0 + jnp.tanh(0.7978845608028654 * (values + 0.044715 * values * values * values)))
    )


def modulate(values, offsets, scales):
    centered = values - jnp.mean(values, axis=-1, keepdims=True)
    spread = jnp.mean(centered * centered, axis=-1, keepdims=True)
    return centered * lax.rsqrt(spread + 1e-06) * (1.0 + scales) + offsets


def depthwise(source, kernel, offsets):
    channels = source.shape[-1]
    square = source.reshape(GRID, GRID, channels)
    padded = jnp.pad(square, ((1, 1), (1, 1), (0, 0)))
    result = jnp.zeros_like(square) + offsets
    for offset_index in range(9):
        row_shift = offset_index // 3
        col_shift = offset_index % 3
        result = (
            result
            + kernel[offset_index]
            * padded[row_shift : row_shift + GRID, col_shift : col_shift + GRID]
        )
    return result.reshape(GRID * GRID, channels)


def regroup(tokens):
    channels = tokens.shape[-1]
    half_side = GRID // 2
    grid_view = tokens.reshape(half_side, 2, half_side, 2, channels).transpose(1, 3, 0, 2, 4)
    return grid_view.reshape(4, half_side * half_side, channels)


def ungroup(groups):
    channels = groups.shape[-1]
    half_side = GRID // 2
    grid_view = groups.reshape(2, 2, half_side, half_side, channels).transpose(2, 0, 3, 1, 4)
    return grid_view.reshape(GRID * GRID, channels)


def attend(triple, validity):
    model_width = triple.shape[1] // 3
    grouped = regroup(triple)
    queries = grouped[:, :, :model_width].reshape(4, -1, model_width // HEAD, HEAD)
    key_rows = grouped[:, :, model_width : 2 * model_width].reshape(
        4, -1, model_width // HEAD, HEAD
    )
    values = grouped[:, :, 2 * model_width :].reshape(4, -1, model_width // HEAD, HEAD)
    key_keep = regroup(validity[:, None])[:, :, 0]
    scores = (
        jnp.einsum("gqhd,gkhd->hgqk", queries, key_rows, preferred_element_type=jnp.float32) * 0.125
    )
    scores = jnp.where(key_keep[None, :, None, :] > 0.5, scores, -1e30)
    largest = jnp.max(scores, axis=-1, keepdims=True)
    exponent = jnp.exp(scores - largest)
    attention = exponent / jnp.sum(exponent, axis=-1, keepdims=True)
    attended = jnp.einsum(
        "hgqk,gkhd->gqhd",
        attention.astype(jnp.bfloat16),
        values,
        preferred_element_type=jnp.float32,
    ).astype(jnp.bfloat16)
    return (ungroup(attended.reshape(4, -1, model_width)), attention, (queries, key_rows, values))


def attend_back(grad_attended, attention, queries, key_rows, values):
    model_width = grad_attended.shape[1]
    grad_grouped = regroup(grad_attended).reshape(4, -1, model_width // HEAD, HEAD)
    attention_low = attention.astype(jnp.bfloat16)
    grad_values = jnp.einsum(
        "hgqk,gqhd->gkhd", attention_low, grad_grouped, preferred_element_type=jnp.float32
    )
    grad_attention = jnp.einsum(
        "gqhd,gkhd->hgqk", grad_grouped, values, preferred_element_type=jnp.float32
    )
    inner = jnp.sum(attention * grad_attention, axis=-1, keepdims=True)
    grad_scores = (attention * (grad_attention - inner)).astype(jnp.bfloat16)
    grad_queries = (
        jnp.einsum("hgqk,gkhd->gqhd", grad_scores, key_rows, preferred_element_type=jnp.float32)
        * 0.125
    )
    grad_keys = (
        jnp.einsum("hgqk,gqhd->gkhd", grad_scores, queries, preferred_element_type=jnp.float32)
        * 0.125
    )
    stacked = jnp.concatenate(
        [
            grad_queries.reshape(4, -1, model_width),
            grad_keys.reshape(4, -1, model_width),
            grad_values.reshape(4, -1, model_width),
        ],
        axis=-1,
    )
    return ungroup(stacked)


def latent_state(tokens, cond_row, validity, gathered):
    (
        ada_weight,
        ada_bias,
        dw1_kernel,
        dw1_bias,
        qkv_weight,
        proj_weight,
        proj_bias,
        fc1_weight,
        fc1_bias,
        dw2_kernel,
        dw2_bias,
        fc2_weight,
        fc2_bias,
    ) = gathered
    silu_cond, silu_back = jax.vjp(smooth_gate, cond_row)
    silu_low = silu_cond.astype(jnp.bfloat16)
    modulation = jnp.dot(silu_low[None, :], ada_weight, preferred_element_type=jnp.float32)[
        0
    ] + ada_bias.astype(jnp.float32)
    shifts = jnp.split(modulation, 6)
    normed, norm_back = jax.vjp(modulate, tokens, shifts[0], shifts[1])
    mixed_full, mix_back = jax.vjp(
        depthwise, normed, dw1_kernel.astype(jnp.float32), dw1_bias.astype(jnp.float32)
    )
    mixed_rows = mixed_full.astype(jnp.bfloat16)
    triple = jnp.dot(mixed_rows, qkv_weight, preferred_element_type=jnp.float32).astype(
        jnp.bfloat16
    )
    attended, attention, grouped = attend(triple, validity)
    branch = jnp.dot(attended, proj_weight, preferred_element_type=jnp.float32) + proj_bias.astype(
        jnp.float32
    )
    middle = tokens + shifts[2] * branch
    normed_two, norm_back_two = jax.vjp(modulate, middle, shifts[3], shifts[4])
    normed_low = normed_two.astype(jnp.bfloat16)
    hidden = jnp.dot(normed_low, fc1_weight, preferred_element_type=jnp.float32) + fc1_bias.astype(
        jnp.float32
    )
    convolved, conv_back = jax.vjp(
        depthwise, hidden, dw2_kernel.astype(jnp.float32), dw2_bias.astype(jnp.float32)
    )
    activated_full, gelu_back = jax.vjp(gelu_tanh, convolved)
    activated = activated_full.astype(jnp.bfloat16)
    branch_two = jnp.dot(
        activated, fc2_weight, preferred_element_type=jnp.float32
    ) + fc2_bias.astype(jnp.float32)
    output = middle + shifts[5] * branch_two
    saved = (
        silu_back,
        silu_low,
        shifts,
        norm_back,
        mix_back,
        mixed_rows,
        attended,
        attention,
        grouped,
        branch,
        norm_back_two,
        normed_low,
        conv_back,
        gelu_back,
        activated,
        branch_two,
    )
    return (output, saved)


def latent_backward(tokens, cond_row, validity, cotangent, gathered):
    (
        ada_weight,
        ada_bias,
        dw1_kernel,
        dw1_bias,
        qkv_weight,
        proj_weight,
        proj_bias,
        fc1_weight,
        fc1_bias,
        dw2_kernel,
        dw2_bias,
        fc2_weight,
        fc2_bias,
    ) = gathered
    output, saved = latent_state(tokens, cond_row, validity, gathered)
    (
        silu_back,
        silu_low,
        shifts,
        norm_back,
        mix_back,
        mixed_rows,
        attended,
        attention,
        grouped,
        branch,
        norm_back_two,
        normed_low,
        conv_back,
        gelu_back,
        activated,
        branch_two,
    ) = saved
    grad_out = cotangent * validity[:, None]
    gate_two_grad = jnp.sum(grad_out * branch_two, axis=0)
    grad_two = grad_out * shifts[5]
    fc2_bias_grad = jnp.sum(grad_two, axis=0)
    grad_two_low = grad_two.astype(jnp.bfloat16)
    fc2_weight_grad = jnp.einsum(
        "sf,sd->fd", activated, grad_two_low, preferred_element_type=jnp.float32
    )
    grad_activated = jnp.einsum(
        "sd,fd->sf", grad_two_low, fc2_weight, preferred_element_type=jnp.float32
    )
    (grad_convolved,) = gelu_back(grad_activated)
    grad_hidden, dw2_kernel_grad, dw2_bias_grad = conv_back(grad_convolved)
    fc1_bias_grad = jnp.sum(grad_hidden, axis=0)
    hidden_low = grad_hidden.astype(jnp.bfloat16)
    fc1_weight_grad = jnp.einsum(
        "sd,sf->df", normed_low, hidden_low, preferred_element_type=jnp.float32
    )
    grad_normed_two = jnp.einsum(
        "sf,df->sd", hidden_low, fc1_weight, preferred_element_type=jnp.float32
    )
    grad_middle, shift_two_grad, scale_two_grad = norm_back_two(grad_normed_two)
    grad_middle = grad_middle + grad_out
    gate_one_grad = jnp.sum(grad_middle * branch, axis=0)
    grad_branch = grad_middle * shifts[2]
    proj_bias_grad = jnp.sum(grad_branch, axis=0)
    branch_low = grad_branch.astype(jnp.bfloat16)
    proj_weight_grad = jnp.einsum(
        "sa,sd->ad", attended, branch_low, preferred_element_type=jnp.float32
    )
    grad_attended = jnp.einsum(
        "sd,ad->sa", branch_low, proj_weight, preferred_element_type=jnp.float32
    ).astype(jnp.bfloat16)
    grad_triple = attend_back(grad_attended, attention, grouped[0], grouped[1], grouped[2]).astype(
        jnp.bfloat16
    )
    qkv_weight_grad = jnp.einsum(
        "sa,sb->ab", mixed_rows, grad_triple, preferred_element_type=jnp.float32
    )
    grad_mixed = jnp.einsum(
        "sb,ab->sa", grad_triple, qkv_weight, preferred_element_type=jnp.float32
    )
    grad_normed, dw1_kernel_grad, dw1_bias_grad = mix_back(grad_mixed)
    grad_tokens, shift_one_grad, scale_one_grad = norm_back(grad_normed)
    grad_tokens = grad_tokens + grad_middle
    grad_modulation = jnp.concatenate(
        [
            shift_one_grad,
            scale_one_grad,
            gate_one_grad,
            shift_two_grad,
            scale_two_grad,
            gate_two_grad,
        ]
    )
    modulation_low = grad_modulation.astype(jnp.bfloat16)
    grad_silu = jnp.einsum(
        "e,de->d", modulation_low, ada_weight, preferred_element_type=jnp.float32
    )
    (cond_grad,) = silu_back(grad_silu)
    grads = (
        dw1_kernel_grad,
        dw1_bias_grad,
        qkv_weight_grad,
        proj_weight_grad,
        proj_bias_grad,
        fc1_weight_grad,
        fc1_bias_grad,
        dw2_kernel_grad,
        dw2_bias_grad,
        fc2_weight_grad,
        fc2_bias_grad,
    )
    return (grad_tokens, cond_grad, grads, silu_low, grad_modulation)


def pack_owned(members, dims, count):
    pieces = [jnp.moveaxis(member, dim, 0).reshape(count, -1) for member, dim in zip(members, dims)]
    return jnp.concatenate(pieces, axis=1)


def unpack_owned(flat_row, members, dims, count):
    results = []
    offset = 0
    for member, dim in zip(members, dims):
        moved = jnp.moveaxis(member, dim, 0)
        shape_owned = (moved.shape[0] // count,) + moved.shape[1:]
        length = moved.size // count
        piece = flat_row[offset : offset + length].reshape(shape_owned)
        results.append(jnp.moveaxis(piece, 0, dim))
        offset = offset + length
    return tuple(results)


def on_device(
    latents,
    condition,
    valid_mask,
    ada_weight,
    ada_bias,
    dw1_kernel,
    dw1_bias,
    qkv_weight,
    proj_weight,
    proj_bias,
    fc1_weight,
    fc1_bias,
    dw2_kernel,
    dw2_bias,
    fc2_weight,
    fc2_bias,
    out_cotangent,
):
    gathered = (
        lax.all_gather(ada_weight, ("wide", "narrow"), axis=0, tiled=True),
        lax.all_gather(ada_bias, ("wide", "narrow"), axis=0, tiled=True),
        lax.all_gather(dw1_kernel, ("wide", "narrow"), axis=1, tiled=True),
        lax.all_gather(dw1_bias, ("wide", "narrow"), axis=0, tiled=True),
        lax.all_gather(qkv_weight, ("wide", "narrow"), axis=0, tiled=True),
        lax.all_gather(proj_weight, ("wide", "narrow"), axis=0, tiled=True),
        lax.all_gather(proj_bias, ("wide", "narrow"), axis=0, tiled=True),
        lax.all_gather(fc1_weight, ("wide", "narrow"), axis=0, tiled=True),
        lax.all_gather(fc1_bias, ("wide", "narrow"), axis=0, tiled=True),
        lax.all_gather(dw2_kernel, ("wide", "narrow"), axis=1, tiled=True),
        lax.all_gather(dw2_bias, ("wide", "narrow"), axis=0, tiled=True),
        lax.all_gather(fc2_weight, ("wide", "narrow"), axis=0, tiled=True),
        lax.all_gather(fc2_bias, ("wide", "narrow"), axis=0, tiled=True),
    )
    validity = valid_mask.astype(jnp.float32)

    def forward_one(sample):
        output, saved = latent_state(
            sample[0].astype(jnp.float32), sample[1].astype(jnp.float32), sample[2], gathered
        )
        return output.astype(jnp.bfloat16)

    block_out = lax.map(forward_one, (latents, condition, validity))
    backward_set = (
        lax.all_gather(ada_weight, ("wide", "narrow"), axis=0, tiled=True),
        lax.all_gather(ada_bias, ("wide", "narrow"), axis=0, tiled=True),
        lax.all_gather(dw1_kernel, ("wide", "narrow"), axis=1, tiled=True),
        lax.all_gather(dw1_bias, ("wide", "narrow"), axis=0, tiled=True),
        lax.all_gather(qkv_weight, ("wide", "narrow"), axis=0, tiled=True),
        lax.all_gather(proj_weight, ("wide", "narrow"), axis=0, tiled=True),
        lax.all_gather(proj_bias, ("wide", "narrow"), axis=0, tiled=True),
        lax.all_gather(fc1_weight, ("wide", "narrow"), axis=0, tiled=True),
        lax.all_gather(fc1_bias, ("wide", "narrow"), axis=0, tiled=True),
        lax.all_gather(dw2_kernel, ("wide", "narrow"), axis=1, tiled=True),
        lax.all_gather(dw2_bias, ("wide", "narrow"), axis=0, tiled=True),
        lax.all_gather(fc2_weight, ("wide", "narrow"), axis=0, tiled=True),
        lax.all_gather(fc2_bias, ("wide", "narrow"), axis=0, tiled=True),
    )
    starting = tuple((jnp.zeros(member.shape, jnp.float32) for member in backward_set[2:]))

    def backward_one(running, sample):
        grad_tokens, cond_grad, grads, silu_low, grad_modulation = latent_backward(
            sample[0].astype(jnp.float32),
            sample[1].astype(jnp.float32),
            sample[2],
            sample[3].astype(jnp.float32),
            backward_set,
        )
        updated = tuple((total + extra for total, extra in zip(running, grads)))
        return (updated, (grad_tokens.astype(jnp.bfloat16), cond_grad, silu_low, grad_modulation))

    summed, (input_grad, cond_grad, silu_rows, mod_rows) = lax.scan(
        backward_one, starting, (latents, condition, validity, out_cotangent)
    )
    rest_dims = (1, 0, 0, 0, 0, 0, 0, 1, 0, 0, 0)
    count = lax.axis_size(("wide", "narrow"))
    ada_wsum = jnp.einsum(
        "bd,be->de", silu_rows, mod_rows.astype(jnp.bfloat16), preferred_element_type=jnp.float32
    )
    ada_bsum = jnp.sum(mod_rows, axis=0)
    members = (ada_wsum, ada_bsum) + summed
    dims = (0, 0) + rest_dims
    packed = pack_owned(members, dims, count)
    owned_flat = lax.psum_scatter(packed, ("wide", "narrow"), scatter_dimension=0, tiled=True)
    owned = unpack_owned(owned_flat[0], members, dims, count)
    return (
        block_out,
        input_grad,
        cond_grad,
        owned[0],
        owned[1],
        owned[2],
        owned[3],
        owned[4],
        owned[5],
        owned[6],
        owned[7],
        owned[8],
        owned[9],
        owned[10],
        owned[11],
        owned[12],
    )


def solution(mesh):
    in_specs = (
        P(("wide", "narrow"), None, None),
        P(("wide", "narrow"), None),
        P(("wide", "narrow"), None),
        P(("wide", "narrow"), None),
        P(("wide", "narrow")),
        P(None, ("wide", "narrow")),
        P(("wide", "narrow")),
        P(("wide", "narrow"), None),
        P(("wide", "narrow"), None),
        P(("wide", "narrow")),
        P(("wide", "narrow"), None),
        P(("wide", "narrow")),
        P(None, ("wide", "narrow")),
        P(("wide", "narrow")),
        P(("wide", "narrow"), None),
        P(("wide", "narrow")),
        P(("wide", "narrow"), None, None),
    )
    out_specs = (
        P(("wide", "narrow"), None, None),
        P(("wide", "narrow"), None, None),
        P(("wide", "narrow"), None),
        P(("wide", "narrow"), None),
        P(("wide", "narrow")),
        P(None, ("wide", "narrow")),
        P(("wide", "narrow")),
        P(("wide", "narrow"), None),
        P(("wide", "narrow"), None),
        P(("wide", "narrow")),
        P(("wide", "narrow"), None),
        P(("wide", "narrow")),
        P(None, ("wide", "narrow")),
        P(("wide", "narrow")),
        P(("wide", "narrow"), None),
        P(("wide", "narrow")),
    )
    return jax.shard_map(
        on_device, mesh=mesh, in_specs=in_specs, out_specs=out_specs, check_vma=False
    )
```

profile of v0, /device:TPU:0, one launch (start us, length us, event | category | flops | bytes accessed | tf_op | source)
XLA Modules:
  0.0 1531.2 jit_solution(7383951005282924041)
XLA Ops:
  19.6 42.8 %all-reduce.45 = (bf16[4608]{0:T(1024)(128)(2,1)}, bf16[768]{0:T(1024)(128)(2,1)S(1)}, bf16[768]{0:T(1024)(128)(2,1)S(1)}, bf16[3072]{0:T(1024)(128)(2,1)S(1)}, ...) all-reduce(bf16[4608]{0:T(1024)(128)(2,1)S(1)} %dynamic-update-slic, ...), channel_id=1, replica_groups=mesh['wide'=8,'narrow'=4] {'wide','narrow'}, use_global_device_ids=true, to_apply=%add.38 | all-reduce | flops 13056 | bytes 52224
  66.0 68.1 %all-gather = bf16[32,24,9]{1,2,0:T(8,128)(2,1)S(1)} all-gather(bf16[1,24,9]{1,2,0:T(8,128)(2,1)S(1)} %bitcast.238), channel_id=1, replica_groups=mesh['wide'=8,'narrow'=4] {'wide','narrow'}, dimensions={0}, use_global_device_ids=true | all-gather | bytes 14256 | tf_op jit(solution)/shard_map/all_gather | solution.py:335
  135.3 64.8 %all-gather.1 = bf16[32,96,9]{1,2,0:T(8,128)(2,1)S(1)} all-gather(bf16[1,96,9]{1,2,0:T(8,128)(2,1)S(1)} %bitcast.239), channel_id=1, replica_groups=mesh['wide'=8,'narrow'=4] {'wide','narrow'}, dimensions={0}, use_global_device_ids=true | all-gather | bytes 57024 | tf_op jit(solution)/shard_map/all_gather | solution.py:342
  213.3 8.0 convolution_convert_fusion
  221.3 10.2 reshape.550
  246.8 8.0 fusion.96
  254.8 9.1 fusion.87
  263.9 5.2 fusion.73
  269.1 6.0 copy.175
  275.1 6.1 reshape.555
  285.8 5.1 fusion.92
  293.0 11.5 broadcast_add_fusion
  304.5 46.6 %fusion.11 = (bf16[32,32,3072]{2,1,0:T(8,128)(2,1)}, f32[32,32,3072]{2,1,0:T(8,128)}) fusion(f32[3072]{0:T(1024)S(1)} %bitcast.212, f32[3072]{0:T(1024)S(1)} %bitcast.214, f32[3072]{0:T(1024)S(1)} %bitcast.216, f32[3072]{0:T(1024)S(1)} %bitcast.218, f32[32,32,3072]{2,1,0:T(8,128)} %bitcast.187, f32[3072]{0:T(1024)S(1)} %bitcast.220, f32[3072]{0:T(1024)S(1)} %bitcast.222, ...), kind=kLoop, calls=%fused_computation.25 | loop fusion | flops 84934656 | bytes 31580160 | tf_op jit(solution)/shard_map/while/body/eval_jaxpr/convert_element_type | solution.py:158
  351.1 10.0 multiply_convert_fusion.1
  361.1 63.2 %multiply_reduce_fusion.8 = (f32[3072]{0:T(1024)}, f32[3072]{0:T(1024)}, f32[3072]{0:T(1024)}, f32[3072]{0:T(1024)}, f32[3072]{0:T(1024)}, /*index=5*/f32[3072]{...) fusion(f32[32,32,3072]{2,1,0:T(8,128)} %bitcast.188, bf16[3072,768]{1,0:T(8,128)(2,1)} %all-gather.16.cloned.1.call-done, ...), kind=kOutput, calls=%fused_computation.44 | convolution fusion | flops 4957642752 | bytes 44145664 | tf_op jit(solution)/shard_map/while/body/eval_jaxpr/sd,fd->sf/dot_general | solution.py:227
  424.3 10.1 fusion.88
  436.2 35.0 %broadcast_multiply_fusion.1 = (f32[32,32,3072]{2,1,0:T(8,128)}, f32[32,32,3072]{2,1,0:T(8,128)}, f32[32,32,3072]{2,1,0:T(8,128)}, f32[32,32,3072]{2,1,0:T(8,128...) fusion(f32[32,32,3072]{2,1,0:T(8,128)S(1)} %bitcast.186, ...), kind=kLoop, calls=%fused_computation.55 | loop fusion | flops 28311552 | bytes 125939712 | tf_op jit(solution)/shard_map/while/body/eval_jaxpr/transpose(jvp())/mul | solution.py:38
  471.1 19.4 %pad_add_fusion = f32[34,34,3072]{2,1,0:T(8,128)} fusion(f32[32,32,3072]{2,1,0:T(8,128)} %get-tuple-element.316, f32[32,32,3072]{2,1,0:T(8,128)} %get-tuple-element.317, f32[32,32,3072]{2,1,0:T(8,128)} %get-tuple-element.309), kind=kLoop, calls=%fused_computation.15 | loop fusion | flops 7102464 | bytes 51953664 | tf_op jit(solution)/shard_map/while/body/eval_jaxpr/transpose(jvp())/add_any | solution.py:39
  490.6 33.6 %fusion.89 = (f32[3072]{0:T(1024)}, bf16[32,32,3072]{2,1,0:T(8,128)(2,1)}) fusion(f32[32,32,3072]{2,1,0:T(8,128)} %get-tuple-element.310, f32[32,32,3072]{2,1,0:T(8,128)} %get-tuple-element.311, f32[32,32,3072]{2,1,0:T(8,128)} %get-tuple-element.312, f32[32,32,3072]{2,1,0:T(8,128)} %get-tuple-element.313, f32[32,32,3072]{2,1,0:T(8,128)} %get-tuple-element.314, ...), kind=kLoop, calls=%fused_computation.235 | loop fusion | flops 25162752 | bytes 94384128 | tf_op jit(solution)/shard_map/while/body/eval_jaxpr/reduce_sum | solution.py:232
  524.2 10.9 fusion.86
  535.1 9.1 fusion.97
  552.0 13.2 fusion.35
  576.7 6.2 fusion.47
  583.0 6.9 fusion.45
  589.9 18.9 %multiply_convert_fusion = bf16[12,4,256,256]{2,3,1,0:T(8,128)(2,1)S(1)} fusion(f32[12,4,256,256]{2,3,1,0:T(8,128)} %fusion.45, f32[12,4,256,256]{2,3,1,0:T(8,128)} %get-tuple-element.351, f32[12,4,256]{2,1,0:T(4,128)S(1)} %copy-done.48), kind=kOutput, calls=%fused_computation.45 | output fusion | flops 18886912 | bytes 31506432 | tf_op jit(solution)/shard_map/while/body/eval_jaxpr/sub | solution.py:94
  618.0 5.4 concatenate.22
  628.1 5.2 concatenate.20
  633.3 6.1 copy.187
  639.4 6.1 concatenate.21
  648.9 9.4 copy.191
  658.2 10.5 convert_element_type.252
  668.8 10.7 convert_element_type.247
  679.6 16.9 %multiply_reduce_fusion.18 = (f32[768]{0:T(1024)S(1)}, f32[768]{0:T(1024)S(1)}, f32[768]{0:T(1024)S(1)}, f32[768]{0:T(1024)S(1)}, f32[768]{0:T(1024)S(1)}, /*ind...) fusion(f32[32,32,768]{2,1,0:T(8,128)S(1)} %copy-done.11, ...), kind=kOutput, calls=%fused_computation.127 | convolution fusion | flops 3645104640 | bytes 39770112 | tf_op jit(solution)/shard_map/while/body/eval_jaxpr/sb,ab->sa/dot_general | solution.py:258
  705.4 5.9 pad_add_fusion.8
  721.5 10.5 fusion.62
  732.1 8.2 reshape.574
  741.8 8.5 reshape.570
  753.5 8.2 fusion.98
  761.7 6.6 reshape.567
  768.9 6.9 broadcast_multiply_fusion
  775.8 10.8 reshape.563
  786.6 10.9 constant_dynamic-update-slice_fusion.3
  802.0 6.5 constant_dynamic-update-slice_fusion.2
  811.5 28.8 %dynamic-update-slice.13 = f32[32,333264]{1,0:T(8,128)} dynamic-update-slice(f32[32,333264]{1,0:T(8,128)} %dynamic-update-slice.12, f32[32,73728]{1,0:T(8,128)} %reshape.570, s32[]{} %constant.257, s32[]{} %constant.264) | dynamic-update-slice | bytes 18874372
  845.0 28.3 %dynamic-update-slice.17 = f32[32,333264]{1,0:T(8,128)} dynamic-update-slice(f32[32,333264]{1,0:T(8,128)} %dynamic-update-slice.16, f32[32,73728]{1,0:T(8,128)} %reshape.574, s32[]{} %constant.257, s32[]{} %constant.268) | dynamic-update-slice | bytes 18874372
  877.9 5.1 fusion.60
  884.7 5.1 convolution_reduce_fusion.1
  890.4 611.9 %all-reduce.48.cloned.1.call-done = f32[32,333264]{1,0:T(8,128)} async-done(((f32[32,333264]{1,0:T(8,128)}), f32[32,333264]{1,0:T(8,128)}) %all-reduce.48.cloned.1.call-update) | async-done | bytes 42657808
  (374 shorter events, 154.8 us)
Async XLA Ops:
  7.2 194.9 %all-gather.8.cloned.1.call-start = ((), (), s32[]{:S(2)}) async-start(), calls=%async_computation | async-start | bytes 7299072 | tf_op jit(solution)/shard_map/all_gather | solution.py:333
  7.9 205.3 %all-gather.10.cloned.1.call-start = ((), (), s32[]{:S(2)}) async-start(), calls=%async_computation.1 | async-start | bytes 3649536 | tf_op jit(solution)/shard_map/all_gather | solution.py:337
  8.7 277.1 %all-gather.12.cloned.1.call-start = ((), (), s32[]{:S(2)}) async-start(), calls=%async_computation.2 | async-start | bytes 1216512 | tf_op jit(solution)/shard_map/all_gather | solution.py:338
  9.4 283.5 %all-gather.14.cloned.1.call-start = ((), (), s32[]{:S(2)}) async-start(), calls=%async_computation.3 | async-start | bytes 4866048 | tf_op jit(solution)/shard_map/all_gather | solution.py:340
  10.0 351.1 %all-gather.16.cloned.1.call-start = ((), (), s32[]{:S(2)}) async-start(), calls=%async_computation.4 | async-start | bytes 4866048 | tf_op jit(solution)/shard_map/all_gather | solution.py:344
  10.6 1491.8 %all-reduce.48.cloned.1.call-start = ((), (), s32[]{:S(2)}) async-start(), calls=%async_computation.5 | async-start | bytes 85327872
  14.3 271.4 %copy-start = (bf16[1,1024,768]{1,2,0:T(8,128)(2,1)}, bf16[1,1024,768]{1,2,0:T(8,128)(2,1)S(1)}, u32[]{:S(2)}) copy-start(bf16[1,1024,768]{1,2,0:T(8,128)(2,1)S(1)} %copy.163) | copy-start | bytes 4718596
  14.7 51.3 %copy-start.93 = (bf16[9,24]{1,0:T(8,128)(2,1)S(1)}, bf16[9,24]{1,0:T(8,128)(2,1)}, u32[]{:S(2)}) copy-start(bf16[9,24]{1,0:T(8,128)(2,1)} %param.22) | copy-start | bytes 1300
  15.4 184.9 %copy-start.51 = (f32[1024]{0:T(1024)}, f32[1024]{0:T(1024)S(1)}, u32[]{:S(2)}) copy-start(f32[1024]{0:T(1024)S(1)} %multiply_reduce_fusion.25) | copy-start | bytes 12292
  15.4 119.8 %copy-start.94 = (bf16[9,96]{1,0:T(8,128)(2,1)S(1)}, bf16[9,96]{1,0:T(8,128)(2,1)}, u32[]{:S(2)}) copy-start(bf16[9,96]{1,0:T(8,128)(2,1)} %param.29) | copy-start | bytes 5188
  15.5 190.9 %copy-start.31 = (f32[32,32]{1,0:T(8,128)}, f32[32,32]{1,0:T(8,128)S(1)}, u32[]{:S(2)}) copy-start(f32[32,32]{1,0:T(8,128)S(1)} %div.94) | copy-start | bytes 12292
  15.5 184.9 %copy-start.23 = (bf16[1,1024,768]{2,1,0:T(8,128)(2,1)S(1)}, bf16[1,1024,768]{2,1,0:T(8,128)(2,1)}, u32[]{:S(2)}) copy-start(bf16[1,1024,768]{2,1,0:T(8,128)(2,1)} %param.33) | copy-start | bytes 4718596
  135.2 71.8 %copy-start.53 = (f32[768]{0:T(1024)}, f32[768]{0:T(1024)S(1)}, u32[]{:S(2)}) copy-start(f32[768]{0:T(1024)S(1)} %get-tuple-element.281) | copy-start | bytes 9220
  135.2 71.8 %copy-start.59 = (f32[768]{0:T(1024)}, f32[768]{0:T(1024)S(1)}, u32[]{:S(2)}) copy-start(f32[768]{0:T(1024)S(1)} %get-tuple-element.280) | copy-start | bytes 9220
  135.2 71.8 %copy-start.61 = (f32[768]{0:T(1024)}, f32[768]{0:T(1024)S(1)}, u32[]{:S(2)}) copy-start(f32[768]{0:T(1024)S(1)} %get-tuple-element.282) | copy-start | bytes 9220
  135.2 71.8 %copy-start.63 = (f32[768]{0:T(1024)}, f32[768]{0:T(1024)S(1)}, u32[]{:S(2)}) copy-start(f32[768]{0:T(1024)S(1)} %get-tuple-element.283) | copy-start | bytes 9220
  135.2 71.8 %copy-start.65 = (f32[768]{0:T(1024)}, f32[768]{0:T(1024)S(1)}, u32[]{:S(2)}) copy-start(f32[768]{0:T(1024)S(1)} %get-tuple-element.284) | copy-start | bytes 9220
  135.2 71.9 %copy-start.67 = (f32[768]{0:T(1024)}, f32[768]{0:T(1024)S(1)}, u32[]{:S(2)}) copy-start(f32[768]{0:T(1024)S(1)} %get-tuple-element.285) | copy-start | bytes 9220
  135.2 71.9 %copy-start.69 = (f32[768]{0:T(1024)}, f32[768]{0:T(1024)S(1)}, u32[]{:S(2)}) copy-start(f32[768]{0:T(1024)S(1)} %get-tuple-element.286) | copy-start | bytes 9220
  206.4 79.4 %copy-start.75 = (f32[768]{0:T(1024)}, f32[768]{0:T(1024)S(1)}, u32[]{:S(2)}) copy-start(f32[768]{0:T(1024)S(1)} %get-tuple-element.347) | copy-start | bytes 9220
  206.4 86.6 %copy-start.55 = (f32[768]{0:T(1024)}, f32[768]{0:T(1024)S(1)}, u32[]{:S(2)}) copy-start(f32[768]{0:T(1024)S(1)} %get-tuple-element.344) | copy-start | bytes 9220
  206.4 86.6 %copy-start.95 = (f32[768]{0:T(1024)}, f32[768]{0:T(1024)S(1)}, u32[]{:S(2)}) copy-start(f32[768]{0:T(1024)S(1)} %get-tuple-element.343) | copy-start | bytes 9220
  242.4 21.4 %copy-start.7 = (bf16[4,256,768]{1,2,0:T(8,128)(2,1)}, bf16[4,256,768]{1,2,0:T(8,128)(2,1)S(1)}, u32[]{:S(2)}) copy-start(bf16[4,256,768]{1,2,0:T(8,128)(2,1)S(1)} %copy.168) | copy-start | bytes 4718596
  254.8 9.1 copy-start.47
  290.9 13.7 copy-start.42
  292.9 11.6 copy-start.49
  292.9 11.6 copy-start.79
  351.1 10.0 copy-start.25
  351.1 10.0 copy-start.98
  424.3 11.9 copy-start.2
  490.6 33.6 %copy-start.4 = (f32[1024,768]{0,1:T(8,128)S(1)}, f32[1024,768]{0,1:T(8,128)}, u32[]{:S(2)}) copy-start(f32[1024,768]{0,1:T(8,128)} %copy-done.3) | copy-start | bytes 9437188
  490.6 33.6 %copy-start.43 = (f32[1024]{0:T(1024)S(1)}, f32[1024]{0:T(1024)}, u32[]{:S(2)}) copy-start(f32[1024]{0:T(1024)} %copy-done.42) | copy-start | bytes 12292
  490.6 33.6 %copy-start.56 = (f32[768]{0:T(1024)S(1)}, f32[768]{0:T(1024)}, u32[]{:S(2)}) copy-start(f32[768]{0:T(1024)} %copy-done.55) | copy-start | bytes 9220
  490.6 33.6 %copy-start.80 = (f32[1024]{0:T(1024)S(1)}, f32[1024]{0:T(1024)}, u32[]{:S(2)}) copy-start(f32[1024]{0:T(1024)} %copy-done.79) | copy-start | bytes 12292
  490.6 33.6 %copy-start.96 = (f32[768]{0:T(1024)S(1)}, f32[768]{0:T(1024)}, u32[]{:S(2)}) copy-start(f32[768]{0:T(1024)} %copy-done.95) | copy-start | bytes 9220
  524.2 10.9 copy-start.13
  552.0 13.2 copy-start.14
  589.9 19.0 %copy-start.15 = (bf16[4,256,768]{1,2,0:T(8,128)(2,1)S(1)}, bf16[4,256,768]{1,2,0:T(8,128)(2,1)}, u32[]{:S(2)}) copy-start(bf16[4,256,768]{1,2,0:T(8,128)(2,1)} %copy.170) | copy-start | bytes 4718596
  668.8 10.8 copy-start.11
  668.8 10.8 copy-start.60
  668.8 10.8 copy-start.62
  668.8 10.8 copy-start.64
  668.8 10.8 copy-start.66
  668.8 10.8 copy-start.68
  668.8 10.8 copy-start.70
  668.8 10.8 copy-start.72
  668.8 10.8 copy-start.74
  679.6 16.9 %copy-start.54 = (f32[768]{0:T(1024)S(1)}, f32[768]{0:T(1024)}, u32[]{:S(2)}) copy-start(f32[768]{0:T(1024)} %copy-done.53) | copy-start | bytes 9220
  (64 other events, 282.8 us)
Sparse Core Ops, SparseCore 0:
  10.8 75.5 all-gather.7
  89.2 59.2 all-gather.9
  151.3 52.9 all-gather.11
  207.0 62.5 all-gather.13
  272.2 62.3 all-gather.15
  874.9 627.3 all-reduce.47
where the time goes:
time: 1540 us; the launch traced here: 1530 us
  waiting for transfers between devices  615 us (40%)
  local copies, waits for them, and re-layouts  285 us (19%)
  other arithmetic  240 us (16%)
  matrix products  200 us (13%)
  blocking collectives  176 us (11%)
  between operations  15.8 us (1%)
    unnamed x7, waiting for transfers between devices  615 us
    unnamed x247, local copies, waits for them, and re-layouts  106 us
    all_gather x1, blocking collectives, on_device(): lax.all_gather(dw1_kernel, ('wide', 'narrow'), axis=1, tiled=True)  68.1 us
    all_gather x1, blocking collectives, on_device(): lax.all_gather(dw2_kernel, ('wide', 'narrow'), axis=1, tiled=True)  64.8 us
    dot_general x1, matrix products, latent_backward(): jnp.einsum('sd,fd->sf', grad_two_low, fc2_weight, preferred_element_type=...  63.2 us
    convert_element_type x2, other arithmetic, latent_state(): activated = activated_full.astype(jnp.bfloat16)  56.5 us
    unnamed x1, blocking collectives  42.8 us
    reshape x13, local copies, waits for them, and re-layouts, pack_owned(): jnp.moveaxis(member, dim, 0).reshape(count, -1)  38.3 us
  transfers between devices with their start and end apart: 6, of which 1 were waited for; matrix products, arithmetic and copies ran while one was open for 12% of the time, Pallas kernels for 0%

commit v1 on v0

v1 whole, which is shorter than its diff:
```python
import functools

import jax
import jax.numpy as jnp
from jax import lax
from jax.experimental import pallas as pl
from jax.experimental.pallas import tpu as pltpu
from jax.sharding import PartitionSpec as P

HEAD = 64
GRID = 32
HALF = 16
GROUP = 256
TOKENS = 1024
C0 = 0.7978845608028654
C1 = 0.044715
EPS = 1e-06
MIB = 1 << 20
AXES = ("wide", "narrow")
F32, BF16 = jnp.float32, jnp.bfloat16


def dot_nn(a, b):
    return lax.dot_general(a, b, (((1,), (0,)), ((), ())), preferred_element_type=F32)


def dot_nt(a, b):
    return lax.dot_general(a, b, (((1,), (1,)), ((), ())), preferred_element_type=F32)


def dot_tn(a, b):
    return lax.dot_general(a, b, (((0,), (0,)), ((), ())), preferred_element_type=F32)


def whole(shape):
    return pl.BlockSpec(shape, lambda *_: (0,) * len(shape))


def once(shape):
    return pl.BlockSpec(shape, lambda *_: (0,) * len(shape), pipeline_mode=pl.Buffered(1))


def like(shape, dtype):
    return jax.ShapeDtypeStruct(shape, dtype)


def shift_pair(pair, parity, first, last):
    low, high = pair
    zero = jnp.zeros_like(low)
    if parity == 0:
        low, high = pltpu.roll(low, 1, 0), pltpu.roll(high, 1, 0)
        return jnp.where(first, zero, low), jnp.where(first, low, high)
    low, high = pltpu.roll(low, 7, 0), pltpu.roll(high, 7, 0)
    return jnp.where(last, high, low), jnp.where(last, zero, high)


def row_sources(gi, r):
    if gi == 0:
        return ((1, r - 1), (0, r), (1, r))
    return ((0, r), (1, r), (0, r + 1))


def load_pair(ref, slab, gi, gj, r):
    tile = 2 + 2 * r
    group = 2 * gi + gj
    return ref[slab, group, tile], ref[slab, group, tile + 1]


def store_pair(ref, slab, gi, gj, r, pair):
    tile = 2 + 2 * r
    group = 2 * gi + gj
    ref[slab, group, tile] = pair[0]
    ref[slab, group, tile + 1] = pair[1]


def edge_masks():
    sub = lax.broadcasted_iota(jnp.int32, (8, 128), 0)
    return sub == 0, sub == 7


def clear_edges(ref):
    slabs = ref.shape[0]
    ref[:, :, 0:2] = jnp.zeros((slabs, 4, 2, 8, 128), F32)
    ref[:, :, 34:36] = jnp.zeros((slabs, 4, 2, 8, 128), F32)


def conv_cell(src, slab, gi, gj, r, k, bias, masks):
    sources = row_sources(gi, r)
    other = 1 - gj
    near = 2 if gj == 0 else 0
    far = 2 - near
    same = [load_pair(src, slab, p, gj, rr) for p, rr in sources]
    cross = [load_pair(src, slab, p, other, rr) for p, rr in sources]
    straight, moved = [], []
    for h in (0, 1):
        acc, off = bias, None
        for a in range(3):
            acc = acc + k[3 * a + 1] * same[a][h] + k[3 * a + near] * cross[a][h]
            term = k[3 * a + far] * cross[a][h]
            off = term if off is None else off + term
        straight.append(acc)
        moved.append(off)
    moved = shift_pair(moved, gj, *masks)
    return straight[0] + moved[0], straight[1] + moved[1]


def conv_back(slab, k, src, grad, grad_moved, put):
    def body(r, carry):
        kg, total = list(carry[:9]), carry[9]
        for gi in (0, 1):
            sources = row_sources(gi, r)
            for gj in (0, 1):
                other = 1 - gj
                near = 2 if gj == 0 else 0
                here = load_pair(src, slab, gi, gj, r)
                out = [None, None]
                for a in range(3):
                    p, rr = sources[2 - a]
                    trio = {
                        1: load_pair(grad, slab, p, gj, rr),
                        2 - near: load_pair(grad, slab, p, other, rr),
                        near: load_pair(grad_moved, slab, p, other, rr),
                    }
                    for b in range(3):
                        n = 3 * a + b
                        for h in (0, 1):
                            term = k[n] * trio[b][h]
                            out[h] = term if out[h] is None else out[h] + term
                            kg[n] = kg[n] + here[h] * trio[b][h]
                total = total + out[0] + out[1]
                put(gi, gj, r, out)
        return tuple(kg) + (total,)

    zero = jnp.zeros((8, 128), F32)
    return lax.fori_loop(0, HALF, body, (zero,) * 10)


def group_rows(gi, gj, r):
    return pl.ds(pl.multiple_of((2 * gi + gj) * GROUP + r * HALF, HALF), HALF)


def row_sum(values):
    rows, columns = values.shape
    return jnp.sum(values.reshape(rows // 8, 8, columns), axis=0)


def unit_rows(values):
    model = values.shape[-1]
    centered = values - jnp.sum(values, axis=-1, keepdims=True) * (1.0 / model)
    spread = jnp.sum(centered * centered, axis=-1, keepdims=True) * (1.0 / model)
    scale = lax.rsqrt(spread + EPS)
    return centered * scale, scale


def unit_back(grad, unit, scale):
    model = grad.shape[-1]
    mean = jnp.sum(grad, axis=-1, keepdims=True) * (1.0 / model)
    tilt = jnp.sum(grad * unit, axis=-1, keepdims=True) * (1.0 / model)
    return scale * (grad - mean - unit * tilt)


def order_matrix():
    d = jnp.arange(GROUP)
    group, position, column = d // 64, (d % 64) // HALF, d % HALF
    source = (2 * position + group // 2) * GRID + 2 * column + group % 2
    return (source[:, None] == jnp.arange(GROUP)[None, :]).astype(BF16)


def pre_kernel(x_ref, cot_ref, mask_ref, order_ref, mod_ref, kern_ref, bias_ref,
               lat_ref, gout_ref, g2_ref, normed_ref, mixed_ref, keep_ref, fc2b_ref):
    model = x_ref.shape[1]
    slabs = model // 128
    clear_edges(normed_ref)
    shift, scale, gate = mod_ref[0:1, :], mod_ref[1:2, :], mod_ref[5:6, :]
    total = jnp.zeros((8, model), F32)
    for t in range(4):
        rows = pl.ds(t * GROUP, GROUP)
        tokens = dot_nn(order_ref[...], x_ref[rows, :])
        unit, _ = unit_rows(tokens)
        normed = unit * (1.0 + scale) + shift
        kept = dot_nn(order_ref[...], mask_ref[rows, :])
        spread = jnp.concatenate([kept] * slabs, axis=1)
        gout = dot_nn(order_ref[...], cot_ref[rows, :]) * spread
        two = gout * gate
        total = total + row_sum(two)
        for g in range(4):
            src = slice(64 * g, 64 * g + 64)
            dst = pl.ds(g * GROUP + 64 * t, 64)
            lat_ref[dst, :] = tokens[src].astype(BF16)
            gout_ref[dst, :] = gout[src].astype(BF16)
            g2_ref[dst, :] = two[src].astype(BF16)
            keep_ref[dst, :] = (kept[src] - 1.0) * 1e30
            for s in range(slabs):
                tile = normed[src, s * 128 : s * 128 + 128].reshape(8, 8, 128)
                normed_ref[s, g, 2 + 8 * t : 10 + 8 * t] = tile
    fc2b_ref[...] = total
    masks = edge_masks()
    for s in range(slabs):
        lanes = pl.ds(s * 128, 128)
        k = [kern_ref[n, :, lanes] for n in range(9)]
        bias = bias_ref[:, lanes]

        def body(r, carry):
            for gi in (0, 1):
                for gj in (0, 1):
                    pair = conv_cell(normed_ref, s, gi, gj, r, k, bias, masks)
                    mixed_ref[group_rows(gi, gj, r), lanes] = jnp.concatenate(pair, 0).astype(BF16)
            return carry

        lax.fori_loop(0, HALF, body, 0)


def pre(x, cot, mask, order, mod, kern, bias):
    tokens, model = x.shape
    slabs = model // 128
    mask = jnp.broadcast_to(mask.astype(BF16)[:, None], (tokens, 128))
    kern = jnp.broadcast_to(kern.astype(F32)[:, None, :], (9, 8, model))
    bias = jnp.broadcast_to(bias.astype(F32)[None, :], (8, model))
    return pl.pallas_call(
        pre_kernel,
        out_shape=[
            like((tokens, model), BF16), like((tokens, model), BF16), like((tokens, model), BF16),
            like((slabs, 4, 36, 8, 128), F32), like((tokens, model), BF16),
            like((tokens, 128), F32), like((8, model), F32),
        ],
        compiler_params=pltpu.CompilerParams(vmem_limit_bytes=56 * MIB),
        name="norm_and_mix",
    )(x, cot, mask, order, mod, kern, bias)


def attend_kernel(mixed_ref, lat_ref, keep_ref, mod_ref, qkv_ref, proj_ref, projb_ref,
                  triple_ref, probs_ref, att_ref, branch_ref, middle_ref, n2_ref):
    model = lat_ref.shape[1]
    slabs = model // 128
    triple_ref[...] = dot_nn(mixed_ref[...], qkv_ref[...]).astype(BF16)
    lane = lax.broadcasted_iota(jnp.int32, (GROUP, 128), 1)
    left = lane < HEAD
    keep = jnp.concatenate([keep_ref[...]] * 2, axis=1)
    for s in range(slabs):
        q = triple_ref[:, s * 128 : s * 128 + 128]
        k = triple_ref[:, model + s * 128 : model + s * 128 + 128] * jnp.asarray(0.125, BF16)
        v = triple_ref[:, 2 * model + s * 128 : 2 * model + s * 128 + 128]
        outs = []
        for h in (0, 1):
            own = left if h == 0 else jnp.logical_not(left)
            scores = dot_nt(jnp.where(own, k, jnp.zeros_like(k)), q) + keep
            e = jnp.exp(scores - jnp.max(scores, axis=0, keepdims=True))
            p = (e * (1.0 / jnp.sum(e, axis=0, keepdims=True))).astype(BF16)
            probs_ref[2 * s + h] = p
            outs.append(dot_tn(p, v))
        att_ref[:, s * 128 : s * 128 + 128] = jnp.where(left, outs[0], outs[1]).astype(BF16)
    branch = dot_nn(att_ref[...], proj_ref[...]) + projb_ref[...]
    middle = lat_ref[...].astype(F32) + mod_ref[2:3, :] * branch
    unit, _ = unit_rows(middle)
    branch_ref[...] = branch
    middle_ref[...] = middle
    n2_ref[...] = (unit * (1.0 + mod_ref[4:5, :]) + mod_ref[3:4, :]).astype(BF16)


def attend(mixed, lat, keep, mod, qkv, proj, projb):
    tokens, model = lat.shape
    heads = model // HEAD
    by_group = lambda columns: pl.BlockSpec((GROUP, columns), lambda g: (g, 0))
    return pl.pallas_call(
        attend_kernel,
        grid=(4,),
        in_specs=[
            by_group(model), by_group(model), by_group(128), whole(mod.shape),
            once(qkv.shape), once(proj.shape), whole((1, model)),
        ],
        out_specs=[
            by_group(3 * model), pl.BlockSpec((heads, GROUP, GROUP), lambda g: (g, 0, 0)),
            by_group(model), by_group(model), by_group(model), by_group(model),
        ],
        out_shape=[
            like((tokens, 3 * model), BF16), like((4 * heads, GROUP, GROUP), BF16),
            like((tokens, model), BF16), like((tokens, model), F32),
            like((tokens, model), F32), like((tokens, model), BF16),
        ],
        compiler_params=pltpu.CompilerParams(vmem_limit_bytes=56 * MIB),
        name="attend",
    )(mixed, lat, keep, mod, qkv, proj, projb.astype(F32)[None, :])


def ff_kernel(n2_ref, n2t_ref, g2_ref, fc1_ref, fc1b_ref, kern_ref, dwb_ref, fc2_ref,
              branch_ref, gn2_ref, w1g_ref, w2g_ref, kg_ref, dwbg_ref, fc1bg_ref,
              hid, ga, gc, gcs, act, ghl):
    step = pl.program_id(0)
    slabs = hid.shape[0]

    @pl.when(step == 0)
    def _():
        branch_ref[...] = jnp.zeros_like(branch_ref)
        gn2_ref[...] = jnp.zeros_like(gn2_ref)
        for ref in (hid, gc, gcs):
            clear_edges(ref)

    for g in range(4):
        rows = pl.ds(g * GROUP, GROUP)
        full = dot_nn(n2_ref[rows, :], fc1_ref[...]) + fc1b_ref[...]
        back = dot_nt(g2_ref[rows, :], fc2_ref[...])
        for slab in range(slabs):
            lanes = slice(slab * 128, slab * 128 + 128)
            hid[slab, g, 2:34] = full[:, lanes].reshape(32, 8, 128)
            ga[slab, g] = back[:, lanes].reshape(32, 8, 128)

    masks = edge_masks()
    for slab in range(slabs):
        lanes = pl.ds(slab * 128, 128)
        k = [kern_ref[n, :, lanes] for n in range(9)]
        bias = dwb_ref[:, lanes]

        def forward(r, total):
            for gi in (0, 1):
                for gj in (0, 1):
                    pair = conv_cell(hid, slab, gi, gj, r, k, bias, masks)
                    acts, grads = [], []
                    for h in (0, 1):
                        x = pair[h]
                        x2 = x * x
                        half = 0.5 * jnp.tanh(x * (C0 + (C0 * C1) * x2)) + 0.5
                        value = x * half
                        slope = half + (value - value * half) * (2.0 * C0 + (6.0 * C0 * C1) * x2)
                        acts.append(value)
                        grads.append(ga[slab, 2 * gi + gj, 2 * r + h] * slope)
                        total = total + grads[-1]
                    act[group_rows(gi, gj, r), lanes] = jnp.concatenate(acts, 0).astype(BF16)
                    store_pair(gc, slab, gi, gj, r, grads)
                    store_pair(gcs, slab, gi, gj, r, shift_pair(grads, 1 - gj, *masks))
            return total

        dwbg_ref[:, lanes] = lax.fori_loop(0, HALF, forward, jnp.zeros((8, 128), F32))

        def put(gi, gj, r, pair):
            ghl[group_rows(gi, gj, r), lanes] = jnp.concatenate(pair, 0).astype(BF16)

        sums = conv_back(slab, k, hid, gc, gcs, put)
        for n in range(9):
            kg_ref[n, :, lanes] = sums[n]
        fc1bg_ref[:, lanes] = sums[9]

    branch_ref[...] += dot_nn(act[...], fc2_ref[...])
    gn2_ref[...] += dot_nt(ghl[...], fc1_ref[...])
    w2g_ref[...] = dot_tn(act[...], g2_ref[...]).astype(w2g_ref.dtype)
    w1g_ref[...] = dot_nn(n2t_ref[...], ghl[...]).astype(w1g_ref.dtype)


def feed_forward(n2, g2, fc1, fc1_bias, kern, dw_bias, fc2, width=256):
    tokens, model = n2.shape
    hidden = fc1.shape[1]
    slabs = width // 128
    fc1b = fc1_bias.astype(F32)[None, :]
    kern8 = jnp.broadcast_to(kern.astype(F32)[:, None, :], (9, 8, hidden))
    dwb8 = jnp.broadcast_to(dw_bias.astype(F32)[None, :], (8, hidden))
    padded = pltpu.VMEM((slabs, 4, 36, 8, 128), F32)
    columns = lambda rows: pl.BlockSpec((rows, width), lambda s: (0, s))
    out = pl.pallas_call(
        ff_kernel,
        grid=(hidden // width,),
        in_specs=[
            once((tokens, model)), once((model, tokens)), once((tokens, model)),
            columns(model), columns(1), pl.BlockSpec((9, 8, width), lambda s: (0, 0, s)),
            columns(8), pl.BlockSpec((width, model), lambda s: (s, 0)),
        ],
        out_specs=[
            whole((tokens, model)), whole((tokens, model)), columns(model),
            pl.BlockSpec((width, model), lambda s: (s, 0)),
            pl.BlockSpec((9, 8, width), lambda s: (0, 0, s)), columns(8), columns(8),
        ],
        out_shape=[
            like((tokens, model), F32), like((tokens, model), F32),
            like((model, hidden), BF16), like((hidden, model), BF16),
            like((9, 8, hidden), F32), like((8, hidden), F32), like((8, hidden), F32),
        ],
        scratch_shapes=[
            padded, pltpu.VMEM((slabs, 4, 32, 8, 128), F32), padded, padded,
            pltpu.VMEM((tokens, width), BF16), pltpu.VMEM((tokens, width), BF16),
        ],
        compiler_params=pltpu.CompilerParams(vmem_limit_bytes=56 * MIB),
        name="feed_forward",
    )(n2, n2.T, g2, fc1, fc1b, kern8, dwb8, fc2)
    branch, gn2, w1g, w2g, kg, dwbg, fc1bg = out
    return branch, gn2, w1g, w2g, kg.sum(1), dwbg.sum(0), fc1bg.sum(0)


def post_kernel(gn2_ref, two_ref, middle_ref, branch_ref, gout_ref, att_ref, triple_ref, probs_ref,
                mixed_ref, lat_ref, mod_ref, fc2b_ref, proj_ref, qkv_ref, normed_ref, kern_ref,
                order_ref,
                out_ref, xg_ref, sums_ref, qkvg_ref, projg_ref, kg_ref,
                gmid, gmix, gmoved, gnorm, out_rows, ga, gt, qkv_sum, proj_sum):
    step = pl.program_id(0)
    model = lat_ref.shape[1]
    slabs = model // 128

    @pl.when(step == 0)
    def _():
        clear_edges(gmix)
        clear_edges(gmoved)
        sums_ref[...] = jnp.zeros_like(sums_ref)
        qkv_sum[...] = jnp.zeros_like(qkv_sum)
        proj_sum[...] = jnp.zeros_like(proj_sum)

    @pl.when(step < 4)
    def _():
        rows = pl.ds(pl.multiple_of(step * GROUP, GROUP), GROUP)
        middle = middle_ref[...]
        two = two_ref[...] + fc2b_ref[...]
        gout = gout_ref[...].astype(F32)
        out_rows[rows, :] = (middle + mod_ref[5:6, :] * two).astype(BF16)
        sums_ref[5] += row_sum(gout * two)
        unit, scale = unit_rows(middle)
        gn2 = gn2_ref[...]
        sums_ref[3] += row_sum(gn2)
        sums_ref[4] += row_sum(gn2 * unit)
        gm = gout + unit_back(gn2 * (1.0 + mod_ref[4:5, :]), unit, scale)
        gmid[rows, :] = gm
        sums_ref[2] += row_sum(gm * branch_ref[...])
        gb = gm * mod_ref[2:3, :]
        sums_ref[6] += row_sum(gb)
        gbl = gb.astype(BF16)
        proj_sum[...] += dot_tn(att_ref[...], gbl)
        ga[...] = dot_nt(gbl, proj_ref[...]).astype(BF16)
        lane = lax.broadcasted_iota(jnp.int32, (GROUP, 128), 1)
        left = lane < HEAD
        for s in range(slabs):
            lanes = slice(s * 128, s * 128 + 128)
            q = triple_ref[:, s * 128 : s * 128 + 128] * jnp.asarray(0.125, BF16)
            k = triple_ref[:, model + s * 128 : model + s * 128 + 128] * jnp.asarray(0.125, BF16)
            v = triple_ref[:, 2 * model + s * 128 : 2 * model + s * 128 + 128]
            g = ga[:, lanes]
            gq = gk = gv = None
            for h in (0, 1):
                own = left if h == 0 else jnp.logical_not(left)
                mine = lambda value: jnp.where(own, value, jnp.zeros_like(value))
                p_low = probs_ref[2 * s + h]
                p = p_low.astype(F32)
                gh = mine(g)
                gp = dot_nt(v, gh)
                inner = jnp.sum(p * gp, axis=0, keepdims=True)
                gs = (p * (gp - inner)).astype(BF16)
                parts = (dot_tn(gs, mine(k)), dot_nn(gs, mine(q)), dot_nn(p_low, gh))
                if h == 0:
                    gq, gk, gv = parts
                else:
                    gq, gk, gv = gq + parts[0], gk + parts[1], gv + parts[2]
            gt[:, s * 128 : s * 128 + 128] = gq.astype(BF16)
            gt[:, model + s * 128 : model + s * 128 + 128] = gk.astype(BF16)
            gt[:, 2 * model + s * 128 : 2 * model + s * 128 + 128] = gv.astype(BF16)
        qkv_sum[...] += dot_tn(mixed_ref[...], gt[...])
        gmixed = dot_nt(gt[...], qkv_ref[...])
        for s in range(slabs):
            gmix[s, step, 2:34] = gmixed[:, s * 128 : s * 128 + 128].reshape(32, 8, 128)

    @pl.when(step == 4)
    def _():
        qkvg_ref[...] = qkv_sum[...].astype(BF16)
        projg_ref[...] = proj_sum[...].astype(BF16)
        masks = edge_masks()
        for s in range(slabs):
            lanes = pl.ds(s * 128, 128)
            k = [kern_ref[n, :, lanes] for n in range(9)]

            def move(r, total):
                for gi in (0, 1):
                    for gj in (0, 1):
                        pair = load_pair(gmix, s, gi, gj, r)
                        total = total + pair[0] + pair[1]
                        store_pair(gmoved, s, gi, gj, r, shift_pair(pair, 1 - gj, *masks))
                return total

            sums_ref[7, :, lanes] = lax.fori_loop(0, HALF, move, jnp.zeros((8, 128), F32))

            def put(gi, gj, r, pair):
                gnorm[group_rows(gi, gj, r), lanes] = jnp.concatenate(pair, 0)

            sums = conv_back(s, k, normed_ref, gmix, gmoved, put)
            for n in range(9):
                kg_ref[n, :, lanes] = sums[n]
            sums_ref[0, :, lanes] = sums[9]
        scale_sum = jnp.zeros((8, model), F32)
        for g in range(4):
            rows = pl.ds(g * GROUP, GROUP)
            unit, scale = unit_rows(lat_ref[rows, :].astype(F32))
            gn = gnorm[rows, :]
            scale_sum = scale_sum + row_sum(gn * unit)
            grad = gmid[rows, :] + unit_back(gn * (1.0 + mod_ref[1:2, :]), unit, scale)
            gnorm[rows, :] = grad
        sums_ref[1] = scale_sum
        for t in range(4):
            parts = [pl.ds(g * GROUP + 64 * t, 64) for g in range(4)]
            block = jnp.concatenate([out_rows[p, :] for p in parts], axis=0)
            out_ref[t * GROUP : t * GROUP + GROUP, :] = dot_tn(order_ref[...], block).astype(BF16)
            block = jnp.concatenate([gnorm[p, :].astype(BF16) for p in parts], axis=0)
            xg_ref[t * GROUP : t * GROUP + GROUP, :] = dot_tn(order_ref[...], block).astype(BF16)


def post(gn2, two, middle, branch, gout, att, triple, probs, mixed, lat, mod, fc2b, proj, qkv,
         normed, kern, order):
    tokens, model = lat.shape
    heads, slabs = model // HEAD, model // 128
    kern = jnp.broadcast_to(kern.astype(F32)[:, None, :], (9, 8, model))
    at = lambda g: jnp.minimum(g, 3)
    by_group = lambda columns: pl.BlockSpec((GROUP, columns), lambda g: (at(g), 0))
    padded = pltpu.VMEM((slabs, 4, 36, 8, 128), F32)
    return pl.pallas_call(
        post_kernel,
        grid=(5,),
        in_specs=[
            by_group(model), by_group(model), by_group(model), by_group(model), by_group(model),
            by_group(model), by_group(3 * model),
            pl.BlockSpec((heads, GROUP, GROUP), lambda g: (at(g), 0, 0)),
            by_group(model), once((tokens, model)), once(mod.shape), once((1, model)),
            once(proj.shape), once(qkv.shape), once(normed.shape), once(kern.shape),
            once(order.shape),
        ],
        out_specs=[
            once((tokens, model)), once((tokens, model)), once((8, 8, model)),
            once(qkv.shape), once(proj.shape), once(kern.shape),
        ],
        out_shape=[
            like((tokens, model), BF16), like((tokens, model), BF16), like((8, 8, model), F32),
            like(qkv.shape, BF16), like(proj.shape, BF16), like(kern.shape, F32),
        ],
        scratch_shapes=[
            pltpu.VMEM((tokens, model), F32), padded, padded, pltpu.VMEM((tokens, model), F32),
            pltpu.VMEM((tokens, model), BF16), pltpu.VMEM((GROUP, model), BF16),
            pltpu.VMEM((GROUP, 3 * model), BF16), pltpu.VMEM(qkv.shape, F32),
            pltpu.VMEM(proj.shape, F32),
        ],
        compiler_params=pltpu.CompilerParams(vmem_limit_bytes=62 * MIB),
        name="attend_back",
    )(gn2, two, middle, branch, gout, att, triple, probs, mixed, lat, mod,
      fc2b.astype(F32)[None, :], proj, qkv, normed, kern, order)


def flip(index, bit):
    return index + bit - 2 * bit * lax.rem(index // bit, 2)


def bits_of(count):
    return [1 << b for b in range(count.bit_length() - 1)]


def at(w, n):
    return {"wide": w, "narrow": n}


def greet(places):
    barrier = pltpu.get_barrier_semaphore()
    for place in places:
        pl.semaphore_signal(barrier, inc=1, device_id=place, device_id_type=pl.DeviceIdType.MESH)
    pl.semaphore_wait(barrier, len(places))


def greet_all(me, total, narrow):
    barrier = pltpu.get_barrier_semaphore()

    def body(k, carry):
        d = lax.rem(me + k, total)
        pl.semaphore_signal(
            barrier, inc=1, device_id=at(d // narrow, lax.rem(d, narrow)),
            device_id_type=pl.DeviceIdType.MESH,
        )
        return carry

    lax.fori_loop(1, total, body, 0)
    pl.semaphore_wait(barrier, total - 1)


def remote(src, dst, send_sem, recv_sem, place):
    return pltpu.make_async_remote_copy(
        src_ref=src, dst_ref=dst, send_sem=send_sem, recv_sem=recv_sem, device_id=place,
        device_id_type=pl.DeviceIdType.MESH,
    )


def sends_to_all(me, total, narrow, src_of, dst, send_sems, recv_sems):
    def copy(k):
        d = lax.rem(me + k, total)
        return remote(src_of(d), dst.at[me], send_sems.at[k], recv_sems.at[k],
                      at(d // narrow, lax.rem(d, narrow)))

    def start(k, carry):
        copy(k).start()
        return carry

    def wait(k, carry):
        copy(k).wait()
        return carry

    lax.fori_loop(1, total, start, 0)
    return lambda: lax.fori_loop(1, total, wait, 0)


def modulation_kernel(wide, narrow, sil_ref, weight_ref, bias_ref, mod_ref, sils_ref,
                      got, part, rows, send_a, recv_a, send_b, recv_b):
    total = wide * narrow
    me = lax.axis_index("wide") * narrow + lax.axis_index("narrow")
    greet_all(me, total, narrow)
    got[me] = sil_ref[me]
    sends_to_all(me, total, narrow, lambda d: sil_ref.at[d], got, send_a, recv_a)()
    sil = got[...].reshape(total, 128)
    sils_ref[...] = sil
    product = dot_nn(sil.astype(BF16), weight_ref[...]) + bias_ref[...]
    for d in range(total):
        part[d] = product[d : d + 1, :]
    rows[me] = part[me]
    sends_to_all(me, total, narrow, lambda d: part.at[d], rows, send_b, recv_b)()
    mod_ref[...] = jnp.sum(rows[...], axis=0)


def modulation(wide, narrow, sil, weight, bias):
    total, columns = wide * narrow, weight.shape[1]
    sems = pltpu.SemaphoreType.DMA((total,))
    return pl.pallas_call(
        functools.partial(modulation_kernel, wide, narrow),
        out_shape=[like((1, columns), F32), like((total, 128), F32)],
        scratch_shapes=[
            pltpu.VMEM((total, 1, 128), F32), pltpu.VMEM((total, 1, columns), F32),
            pltpu.VMEM((total, 1, columns), F32), sems, sems, sems, sems,
        ],
        compiler_params=pltpu.CompilerParams(
            vmem_limit_bytes=56 * MIB, collective_id=0, has_side_effects=True
        ),
        name="modulation",
    )(sil, weight, bias)


def modulation_back_kernel(wide, narrow, grad_ref, small_ref, sils_ref, weight_ref,
                           wgrad_ref, bgrad_ref, cond_ref, small_out,
                           rows, part, smalls, send_a, recv_a, send_b, recv_b, send_c, recv_c):
    total = wide * narrow
    me = lax.axis_index("wide") * narrow + lax.axis_index("narrow")
    greet_all(me, total, narrow)
    rows[me] = grad_ref[0]
    smalls[me] = small_ref[me]
    wait = sends_to_all(me, total, narrow, lambda d: grad_ref.at[0], rows, send_a, recv_a)
    wait_small = sends_to_all(me, total, narrow, lambda d: small_ref.at[d], smalls, send_c, recv_c)
    wait()
    grads = rows[...]
    bgrad_ref[...] = jnp.sum(grads, axis=0)
    low = grads.reshape(total, grads.shape[2]).astype(BF16)
    cond = dot_nt(low, weight_ref[...])
    for d in range(total):
        part[d] = cond[d : d + 1, :]
    cond_ref[me] = part[me]
    wait = sends_to_all(me, total, narrow, lambda d: part.at[d], cond_ref, send_b, recv_b)
    wgrad_ref[...] = dot_tn(sils_ref[...].astype(BF16), low)[: wgrad_ref.shape[0]]
    wait_small()
    small_out[...] = jnp.sum(smalls[...], axis=0)
    wait()


def modulation_back(wide, narrow, grad, small, sils, weight, owned):
    total, columns = wide * narrow, weight.shape[1]
    sems = pltpu.SemaphoreType.DMA((total,))
    return pl.pallas_call(
        functools.partial(modulation_back_kernel, wide, narrow),
        out_shape=[
            like((owned, columns), F32), like((1, columns), F32), like((total, 1, 128), F32),
            like(small.shape[1:], F32),
        ],
        scratch_shapes=[
            pltpu.VMEM((total, 1, columns), F32), pltpu.VMEM((total, 1, 128), F32),
            pltpu.VMEM(small.shape, F32), sems, sems, sems, sems, sems, sems,
        ],
        compiler_params=pltpu.CompilerParams(
            vmem_limit_bytes=56 * MIB, collective_id=1, has_side_effects=True
        ),
        name="modulation_back",
    )(grad, small, sils, weight)


def partners(wide, narrow, w, n):
    places = [at(w, lax.rem(n + k, narrow)) for k in range(1, narrow)]
    return places + [at(flip(w, bit), n) for bit in bits_of(wide)]


class Gather:
    def __init__(self, wide, narrow, src, dst, sends, recvs, chunk, turn, columns):
        self.w, self.n = lax.axis_index("wide"), lax.axis_index("narrow")
        self.wide, self.narrow = wide, narrow
        self.src, self.dst = src, dst
        self.sends, self.recvs, self.chunk = sends, recvs, chunk
        self.columns = columns
        far = bits_of(wide)[1:]
        cut = turn % len(far) if far else 0
        self.order = far[cut:] + far[:cut] + bits_of(wide)[:1]
        self.stages = 1 + len(self.order)

    def copies(self, stage):
        place = lambda ref, *index: ref.at[(*index, slice(None), self.columns)]
        if stage == 0:
            return [
                remote(place(self.src), place(self.dst, self.w, self.n),
                       self.sends.at[self.chunk, k - 1], self.recvs.at[self.chunk, k - 1],
                       at(self.w, lax.rem(self.n + k, self.narrow)))
                for k in range(1, self.narrow)
            ]
        held = [self.w]
        for bit in self.order[: stage - 1]:
            held = held + [flip(h, bit) for h in held]
        base = self.narrow - 2 + len(held)
        place = lambda h: self.dst.at[h, :, :, self.columns]
        return [
            remote(place(h), place(h), self.sends.at[self.chunk, base + i],
                   self.recvs.at[self.chunk, base + i], at(flip(self.w, self.order[stage - 1]), self.n))
            for i, h in enumerate(held)
        ]

    def start(self, stage):
        for copy in self.copies(stage):
            copy.start()

    def wait(self, stage):
        for copy in self.copies(stage):
            copy.wait_recv()

    def finish(self):
        for stage in range(self.stages):
            for copy in self.copies(stage):
                copy.wait_send()


def gather_kernel(wide, narrow, chunks, count, *refs):
    srcs, dsts = refs[:count], refs[count : 2 * count]
    sends, recvs, locals_ = refs[2 * count :]
    w, n = lax.axis_index("wide"), lax.axis_index("narrow")
    own = [pltpu.make_async_copy(srcs[i], dsts[i].at[w, n], locals_.at[i]) for i in range(count)]
    for copy in own:
        copy.start()
    greet(partners(wide, narrow, w, n))
    jobs = [
        Gather(wide, narrow, srcs[i], dsts[i], sends, recvs, c, c, pl.ds(at_, size))
        for c, (i, at_, size) in enumerate(chunks)
    ]
    stages = jobs[0].stages
    for wave in range(len(jobs) + stages):
        for c, job in enumerate(jobs):
            stage = wave - c
            if stage == 1 and c == 0:
                for copy in own:
                    copy.wait()
            if 1 <= stage <= stages:
                job.wait(stage - 1)
            if 0 <= stage < stages:
                job.start(stage)
    for job in jobs:
        job.finish()


def gather(wide, narrow, blocks, chunks):
    count = len(blocks)
    sems = pltpu.SemaphoreType.DMA((len(chunks), narrow + wide - 2))
    anywhere = pl.BlockSpec(memory_space=pl.ANY)
    return pl.pallas_call(
        functools.partial(gather_kernel, wide, narrow, chunks, count),
        in_specs=[anywhere] * count,
        out_specs=[anywhere] * count,
        out_shape=[like((wide, narrow) + b.shape, b.dtype) for b in blocks],
        scratch_shapes=[sems, sems, pltpu.SemaphoreType.DMA((count,))],
        compiler_params=pltpu.CompilerParams(collective_id=2, has_side_effects=True),
        name="gather",
    )(*blocks)


def insert_bit(index, position, value):
    low = index % (1 << position)
    return ((index // (1 << position)) * 2 + value) * (1 << position) + low


class Scatter:
    def __init__(self, wide, narrow, src, halves, line, got, sends, recvs, chunk, turn, columns):
        self.w, self.n = lax.axis_index("wide"), lax.axis_index("narrow")
        self.wide, self.narrow = wide, narrow
        self.src, self.halves, self.line, self.got = src, halves, line, got
        self.sends, self.recvs, self.chunk = sends, recvs, chunk
        self.columns = columns
        far = bits_of(wide)[1:]
        cut = turn % len(far) if far else 0
        self.order = bits_of(wide)[:1] + far[cut:] + far[:cut]
        self.stages = 1 + len(self.order)
        self.rows = line.shape[1]

    def level(self, stage):
        source = self.src if stage == 0 else self.halves[stage - 1]
        bit = self.order[stage]
        position = sum(1 for b in bits_of(self.wide) if b < bit and b not in self.order[:stage])
        return source, bit, position, self.wide >> (stage + 1)

    def copies(self, stage):
        if stage == len(self.order):
            base = self.wide - 1
            return [
                remote(self.line.at[lax.rem(self.n + k, self.narrow), :, self.columns],
                       self.got.at[k - 1, :, self.columns],
                       self.sends.at[self.chunk, base + k - 1], self.recvs.at[self.chunk, base + k - 1],
                       at(self.w, lax.rem(self.n + k, self.narrow)))
                for k in range(1, self.narrow)
            ]
        source, bit, position, size = self.level(stage)
        theirs = 1 - lax.rem(self.w // bit, 2)
        base = self.wide - 2 * size
        return [
            remote(source.at[insert_bit(j, position, theirs), :, self.columns],
                   self.halves[stage].at[j, :, self.columns],
                   self.sends.at[self.chunk, base + j], self.recvs.at[self.chunk, base + j],
                   at(flip(self.w, bit), self.n))
            for j in range(size)
        ]

    def start(self, stage):
        for copy in self.copies(stage):
            copy.start()

    def wait(self, stage):
        for copy in self.copies(stage):
            copy.wait()

    def add(self, stage):
        if stage == len(self.order):
            return
        source, bit, position, size = self.level(stage)
        mine = lax.rem(self.w // bit, 2)
        into = self.halves[stage]
        last = stage == len(self.order) - 1
        for j in range(size):
            index = insert_bit(j, position, mine)
            if last:
                both = (source[index, :, self.columns].astype(F32)
                        + into[j, :, self.columns].astype(F32))
                for m in range(self.narrow):
                    self.line[m, :, self.columns] = both[m * self.rows : (m + 1) * self.rows].astype(BF16)
            else:
                def body(i, carry):
                    rows = pl.ds(pl.multiple_of(i * 16, 16), 16)
                    into[j, rows, self.columns] = (
                        source[index, rows, self.columns].astype(F32)
                        + into[j, rows, self.columns].astype(F32)
                    ).astype(BF16)
                    return carry

                lax.fori_loop(0, into.shape[1] // 16, body, 0)

    def result(self, out):
        value = self.line[self.n, :, self.columns].astype(F32)
        for k in range(1, self.narrow):
            value = value + self.got[k - 1, :, self.columns].astype(F32)
        out[:, self.columns] = value


def scatter_kernel(wide, narrow, chunks, count, levels, *refs):
    srcs, outs = refs[:count], refs[count : 2 * count]
    rest = refs[2 * count :]
    sends, recvs = rest[-2:]
    per = levels + 2
    w, n = lax.axis_index("wide"), lax.axis_index("narrow")
    greet(partners(wide, narrow, w, n))
    jobs = []
    for c, (i, start, size) in enumerate(chunks):
        own = rest[i * per : (i + 1) * per]
        jobs.append(Scatter(wide, narrow, srcs[i], own[:levels], own[levels], own[levels + 1],
                            sends, recvs, c, c, pl.ds(start, size)))
    stages = jobs[0].stages
    for wave in range(len(jobs) + stages):
        for c, job in enumerate(jobs):
            stage = wave - c
            if 1 <= stage <= stages:
                job.wait(stage - 1)
                job.add(stage - 1)
            if 0 <= stage < stages:
                job.start(stage)
            if stage == stages:
                job.result(outs[chunks[c][0]])


def scatter(wide, narrow, arrays, chunks):
    count, levels = len(arrays), len(bits_of(wide))
    sems = pltpu.SemaphoreType.DMA((len(chunks), narrow + wide - 2))
    scratch, outs = [], []
    for a in arrays:
        _, height, columns = a.shape
        rows = height // narrow
        for stage in range(levels):
            scratch.append(pltpu.VMEM((wide >> (stage + 1), height, columns), BF16))
        scratch.append(pltpu.VMEM((narrow, rows, columns), BF16))
        scratch.append(pltpu.VMEM((narrow - 1, rows, columns), BF16))
        outs.append(like((rows, columns), F32))
    return pl.pallas_call(
        functools.partial(scatter_kernel, wide, narrow, chunks, count, levels),
        out_shape=outs,
        scratch_shapes=scratch + [sems, sems],
        compiler_params=pltpu.CompilerParams(
            vmem_limit_bytes=60 * MIB, collective_id=3, has_side_effects=True
        ),
        name="scatter",
    )(*arrays)


def smooth_gate(values):
    return values * jax.nn.sigmoid(values)


def on_device(wide, narrow, latents, condition, valid_mask, ada_weight, ada_bias, dw1_kernel, dw1_bias,
              qkv_weight, proj_weight, proj_bias, fc1_weight, fc1_bias, dw2_kernel, dw2_bias,
              fc2_weight, fc2_bias, out_cotangent):
    total = wide * narrow
    me = lax.axis_index("wide") * narrow + lax.axis_index("narrow")
    model = latents.shape[2]
    hidden = fc1_weight.shape[1]
    own, own_ff = model // total, hidden // total

    sil, silu_back = jax.vjp(smooth_gate, condition[0].astype(F32))
    sil = sil.astype(BF16).astype(F32).reshape(total, 1, own)
    sil = jnp.pad(sil, ((0, 0), (0, 0), (0, 128 - own)))
    ada_rows = jnp.pad(ada_weight, ((0, 128 - own), (0, 0)))
    bias_at = lax.dynamic_update_slice(
        jnp.zeros((1, 6 * model), F32), ada_bias.astype(F32)[None, :], (0, me * ada_bias.shape[0])
    )
    mod, sils = modulation(wide, narrow, sil, ada_rows, bias_at)
    mod = mod.reshape(6, model)

    small = jnp.concatenate([
        jnp.concatenate([dw1_kernel, dw1_bias[None], proj_bias[None], fc2_bias[None]]).reshape(-1),
        jnp.concatenate([dw2_kernel, dw2_bias[None], fc1_bias[None]]).reshape(-1),
    ])
    lines = -(-small.shape[0] // 2048) * 16
    small = jnp.pad(small, (0, lines * 128 - small.shape[0])).reshape(lines, 128)
    blocks = [small, qkv_weight, proj_weight, fc1_weight, fc2_weight]
    chunks = [(0, 0, 128), (1, 0, 1152), (1, 1152, 1152), (2, 0, 768), (3, 0, 1536), (4, 0, 384),
              (3, 1536, 1536), (4, 384, 384)]
    small, qkv, proj, fc1, fc2 = gather(wide, narrow, blocks, chunks)
    qkv, proj = qkv.reshape(model, 3 * model), proj.reshape(model, model)
    fc1, fc2 = fc1.reshape(model, hidden), fc2.reshape(hidden, model)
    small = small.reshape(total, lines * 128)
    narrow_part = small[:, : 12 * own].reshape(total, 12, own).transpose(1, 0, 2).reshape(12, model)
    wide_part = small[:, 12 * own : 12 * own + 11 * own_ff]
    wide_part = wide_part.reshape(total, 11, own_ff).transpose(1, 0, 2).reshape(11, hidden)
    dw1k, dw1b, projb, fc2b = narrow_part[:9], narrow_part[9], narrow_part[10], narrow_part[11]
    dw2k, dw2b, fc1b = wide_part[:9], wide_part[9], wide_part[10]

    order = order_matrix()
    lat, gout, g2, normed, mixed, keep, fc2bg = pre(
        latents[0], out_cotangent[0], valid_mask[0], order, mod, dw1k, dw1b
    )
    triple, probs, att, branch, middle, n2 = attend(mixed, lat, keep, mod, qkv, proj, projb)
    two, gn2, w1g, w2g, kg2, dwb2, fc1bg = feed_forward(n2, g2, fc1, fc1b, dw2k, dw2b, fc2)
    out, xg, sums, qkvg, projg, kg1 = post(
        gn2, two, middle, branch, gout, att, triple, probs, mixed, lat, mod, fc2b, proj, qkv,
        normed, dw1k, order
    )
    sums = sums.sum(1)
    grad_mod = sums[:6].reshape(1, 1, 6 * model)
    narrow_part = jnp.concatenate([kg1.sum(1), sums[7][None], sums[6][None], fc2bg.sum(0)[None]])
    wide_part = jnp.concatenate([kg2, dwb2[None], fc1bg[None]])
    small = jnp.concatenate([
        narrow_part.reshape(12, total, own).transpose(1, 0, 2).reshape(total, 12 * own),
        wide_part.reshape(11, total, own_ff).transpose(1, 0, 2).reshape(total, 11 * own_ff),
    ], axis=1)
    small = jnp.pad(small, ((0, 0), (0, -small.shape[1] % 128)))
    ada_wgrad, ada_bsum, cond, small = modulation_back(
        wide, narrow, grad_mod, small[:, None], sils, ada_rows, own
    )
    ada_bgrad = lax.dynamic_slice(ada_bsum[0], (me * ada_bias.shape[0],), ada_bias.shape)
    (cond_grad,) = silu_back(cond[:, 0, :own].reshape(model))

    narrow_part = small[0, : 12 * own].reshape(12, own)
    wide_part = small[0, 12 * own : 12 * own + 11 * own_ff].reshape(11, own_ff)

    as_lines = lambda grad: grad.reshape(wide, grad.shape[0] // wide, grad.shape[1])
    chunks = [(0, 0, 384), (1, 0, 1536), (0, 384, 384), (1, 1536, 1536), (3, 0, 768), (2, 0, 1152),
              (2, 1152, 1152)]
    fc2g, fc1g, qkvg, projg = scatter(
        wide, narrow, [as_lines(w2g), as_lines(w1g), as_lines(qkvg), as_lines(projg)], chunks
    )
    return (
        out[None], xg[None], cond_grad[None], ada_wgrad, ada_bgrad,
        narrow_part[:9], narrow_part[9], qkvg, projg, narrow_part[10], fc1g, wide_part[10],
        wide_part[:9], wide_part[9], fc2g, narrow_part[11],
    )


def solution(mesh):
    wide, narrow = mesh.shape["wide"], mesh.shape["narrow"]
    rows = lambda rank: P(AXES, *(None,) * (rank - 1))
    lanes = P(None, AXES)
    in_specs = (
        rows(3), rows(2), rows(2), rows(2), rows(1), lanes, rows(1), rows(2), rows(2), rows(1),
        rows(2), rows(1), lanes, rows(1), rows(2), rows(1), rows(3),
    )
    out_specs = (
        rows(3), rows(3), rows(2), rows(2), rows(1), lanes, rows(1), rows(2), rows(2), rows(1),
        rows(2), rows(1), lanes, rows(1), rows(2), rows(1),
    )
    return jax.shard_map(
        functools.partial(on_device, wide, narrow), mesh=mesh, in_specs=in_specs,
        out_specs=out_specs, check_vma=False,
    )
```

time: 1540 us -> 524 us (0.34)
  waiting for transfers between devices: 615 us -> 0 us
  Pallas kernels: 0 us -> 486 us
  local copies, waits for them, and re-layouts: 285 us -> 28.2 us
  other arithmetic: 240 us -> 8.36 us
  matrix products: 200 us -> 0 us
  blocking collectives: 176 us -> 0 us
    unnamed x7 -> x0, waiting for transfers between devices: 615 us -> none
    pallas_call x0 -> x8, Pallas kernels: none -> 486 us  [the longest x1 140 us: scatter(): pl.pallas_call(functools.partial(scatter_kernel, wide, narrow, chunks, co...]
    dot_general x20 -> x0, matrix products: 200 us -> none  [the longest x1 63.2 us: latent_backward(): jnp.einsum('sd,fd->sf', grad_two_low, fc2_weight, preferred_element_type=...]
    all_gather x2 -> x0, blocking collectives: 133 us -> none  [the longest x1 68.1 us: on_device(): lax.all_gather(dw1_kernel, ('wide', 'narrow'), axis=1, tiled=True)]
    unnamed x247 -> x29, local copies, waits for them, and re-layouts: 106 us -> 5.67 us
    convert_element_type x14 -> x8, other arithmetic: 77.3 us -> 2.24 us  [the longest x1 0.76 us: order_matrix(): return (source[:, None] == jnp.arange(GROUP)[None, :]).astype(BF16)]
    reshape x28 -> x8, local copies, waits for them, and re-layouts: 71.5 us -> 1.81 us  [the longest x1 0.63 us: on_device(): grad_mod = sums[:6].reshape(1, 1, 6 * model)]
    reduce_sum x9 -> x6, other arithmetic: 54.8 us -> 1.13 us  [the longest x1 0.75 us: on_device(): fc2bg.sum(0)[None]]
  transfers between devices with their start and end apart: 6 -> 0, of which waited for: 1 -> 0; matrix products, arithmetic and copies ran while one was open for 12% -> 0% of each run, Pallas kernels for 0% -> 0%
where the time goes in v1:
time: 524 us
  Pallas kernels  486 us (93%)
  local copies, waits for them, and re-layouts  28.2 us (5%)
  other arithmetic  8.36 us (2%)
    pallas_call x1, Pallas kernels, scatter(): pl.pallas_call(functools.partial(scatter_kernel, wide, narrow, chunks, co...  140 us
    pallas_call x1, Pallas kernels, gather(): pl.pallas_call(functools.partial(gather_kernel, wide, narrow, chunks, cou...  134 us
    pallas_call x1, Pallas kernels, feed_forward(): pl.pallas_call(ff_kernel, grid=(hidden // width,), in_specs=[once((tokens...  79.5 us
    pallas_call x1, Pallas kernels, post(): pl.pallas_call(post_kernel, grid=(5,), in_specs=[by_group(model), by_grou...  45.2 us
    pallas_call x1, Pallas kernels, modulation_back(): pl.pallas_call(functools.partial(modulation_back_kernel, wide, narrow), o...  30.8 us
    pallas_call x1, Pallas kernels, modulation(): pl.pallas_call(functools.partial(modulation_kernel, wide, narrow), out_sh...  28.7 us
    pallas_call x1, Pallas kernels, attend(): pl.pallas_call(attend_kernel, grid=(4,), in_specs=[by_group(model), by_gr...  17.7 us
    pallas_call x1, Pallas kernels, pre(): pl.pallas_call(pre_kernel, out_shape=[like((tokens, model), BF16), like((...  10.8 us

profile of v1, /device:TPU:0, one launch (start us, length us, event | category | flops | bytes accessed | tf_op | source)
XLA Modules:
  0.0 523.7 jit_solution(10768770528134537789)
XLA Ops:
  0.7 0.7 broadcast_in_dim.92
  1.3 0.7 convert_reduce_fusion
  2.0 0.7 pad_maximum_fusion
  2.9 0.7 pad_maximum_fusion.1
  3.7 0.7 fusion.5.refs_0_
  4.4 0.7 convert_reduce_fusion.1
  5.2 0.6 pad_convert_fusion.sil_ref
  5.9 0.2 dynamic_update_slice.3.bias_ref
  6.0 0.8 fusion.order_ref
  6.8 0.9 broadcast_in_dim.33.mask_ref
  7.7 2.0 pad.20.weight_ref
  9.7 28.7 %modulation.1 = (f32[1,4608]{1,0:T(1,128)}, f32[32,128]{1,0:T(8,128)}) custom-call(f32[32,1,128]{2,1,0:T(1,128)} %pad_convert_fusion.sil_ref, bf16[128,4608]{1,0:T(8,128)(2,1)} %pad.20.weight_ref, f32[1,4608]{1,0:T(1,128)} %copy-done.9), custom_call_target="tpu_custom_call" | custom-call | tf_op jit(solution)/shard_map/modulation/pallas_call | solution.py:615
  38.4 0.8 reduce.2
  39.2 0.6 reshape.304.mod_ref
  39.8 133.7 %gather.1 = (bf16[8,4,16,128]{3,2,1,0:T(8,128)(2,1)}, bf16[8,4,24,2304]{3,2,1,0:T(8,128)(2,1)}, bf16[8,4,24,768]{3,2,1,0:T(8,128)(2,1)}, bf16[8,4,24,3072]{3,2,1,0:T(8,128)(2,1)}, bf16[8,4,96,768]{3,2,1,0:T(8,128)(2,1)}) custom-call(bf16[16,128]{1,0:T(8,128)(2,1)} %fusion.5.refs_0_, bf16[24,2304]{1,0:T(8,128)(2,1)} %refs_1_.1, bf16[24,768]{1,0:T(8,128)(2,1)} %refs_2_.1, ...), custom_call_target="tpu_custom_call" | custom-call | tf_op jit(solution)/shard_map/gather/pallas_call | solution.py:756
  173.5 0.9 copy.75
  174.8 0.7 reshape.330.fc2b_ref
  175.5 0.7 reshape.326.projb_ref
  176.4 0.6 broadcast_in_dim.86.bias_ref
  177.5 0.7 reshape.327.fc1b_ref
  178.3 0.6 broadcast_in_dim.88.dwb_ref
  179.0 0.7 broadcast_in_dim.42.kern_ref
  179.7 1.0 broadcast_in_dim.87.kern_ref
  180.7 10.8 %norm_and_mix.1 = (bf16[1024,768]{1,0:T(8,128)(2,1)}, bf16[1024,768]{1,0:T(8,128)(2,1)}, bf16[1024,768]{1,0:T(8,128)(2,1)}, f32[6,4,36,8,128]{4,3,2,1,0:T(8,128)...) custom-call(bf16[1024,768]{1,0:T(8,128)(2,1)} %bitcast.60, bf16[1024,768]{1,0:T(8,128)(2,1)} %bitcast.61, ...), custom_call_target="tpu_custom_call" | custom-call | tf_op jit(solution)/shard_map/norm_and_mix/pallas_call | solution.py:219
  191.5 0.7 reduce_sum.56
  192.3 17.7 %attend.1 = (bf16[1024,2304]{1,0:T(8,128)(2,1)}, bf16[48,256,256]{2,1,0:T(8,128)(2,1)}, bf16[1024,768]{1,0:T(8,128)(2,1)}, f32[1024,768]{1,0:T(8,128)}, f32[1024,768]{1,0:T(8,128)}, /*index=5*/bf16[1024,768]{1,0:T(8,128)(2,1)}) custom-call(bf16[1024,768]{1,0:T(8,128)(2,1)} %get-tuple-element.59.mixed_ref, bf16[1024,768]{1,0:T(8,128)(2,1)} %get-tuple-element.60.lat_ref, ...), custom_call_target="tpu_custom_call" | custom-call | tf_op jit(solution)/shard_map/attend/pallas_call | solution.py:264
  210.0 2.6 copy.65
  212.7 79.5 %feed_forward.1 = (f32[1024,768]{1,0:T(8,128)}, f32[1024,768]{1,0:T(8,128)}, bf16[768,3072]{1,0:T(8,128)(2,1)}, bf16[3072,768]{1,0:T(8,128)(2,1)}, f32[9,8,3072]...) custom-call(bf16[1024,768]{1,0:T(8,128)(2,1)} %get-tuple-element.64.n2_ref, bf16[768,1024]{1,0:T(8,128)(2,1)} %bitcast.52, ...), custom_call_target="tpu_custom_call" | custom-call | tf_op jit(solution)/shard_map/feed_forward/pallas_call | solution.py:357
  292.1 45.2 %attend_back.1 = (bf16[1024,768]{1,0:T(8,128)(2,1)}, bf16[1024,768]{1,0:T(8,128)(2,1)}, f32[8,8,768]{2,1,0:T(8,128)}, bf16[768,2304]{1,0:T(8,128)(2,1)}, bf16[768,768]{1,0:T(8,128)(2,1)}, /*index=5*/f32[9,8,768]{2,1,0:T(8,128)}) custom-call(f32[1024,768]{1,0:T(8,128)} %get-tuple-element.68.gn2_ref, f32[1024,768]{1,0:T(8,128)} %get-tuple-element.69.two_ref, ...), custom_call_target="tpu_custom_call" | custom-call | tf_op jit(solution)/shard_map/attend_back/pallas_call | solution.py:505
  337.4 139.8 %scatter.1 = (f32[96,768]{1,0:T(8,128)}, f32[24,3072]{1,0:T(8,128)}, f32[24,2304]{1,0:T(8,128)}, f32[24,768]{1,0:T(8,128)}) custom-call(bf16[8,384,768]{2,1,0:T(8,128)(2,1)} %bitcast.54, bf16[8,96,3072]{2,1,0:T(8,128)(2,1)} %bitcast.53, bf16[8,96,2304]{2,1,0:T(8,128)(2,1)} %bitcast.59, bf16[8,96,768]{2,1,0:T(8,128)(2,1)} %bitcast.62), custom_call_target="tpu_custom_call" | custom-call | tf_op jit(solution)/shard_map/scatter/pallas_call | solution.py:889
  477.7 0.6 reshape.315.grad_ref
  478.4 0.2 reduce_sum.57
  479.5 0.8 broadcast_in_dim.91.small_ref
  480.3 30.8 %modulation_back.1 = (f32[24,4608]{1,0:T(8,128)}, f32[1,4608]{1,0:T(1,128)}, f32[32,1,128]{2,1,0:T(1,128)}, f32[1,1408]{1,0:T(1,128)}) custom-call(f32[1,1,4608]{2,1,0:T(1,128)} %reshape.315.grad_ref, f32[32,1,1408]{2,1,0:T(1,128)} %broadcast_in_dim.91.small_ref, f32[32,128]{1,0:T(8,128)} %get-tuple-element.85.sils_ref, bf16[128,4608]{1,0:T(8,128)(2,1)} %pad.20.weight_ref), custom_call_target="tpu_custom_call" | custom-call | tf_op jit(solution)/shard_map/modulation_back/pallas_call | solution.py:657
  511.0 0.8 slice_reduce_fusion
  511.9 0.6 fusion.7
  512.5 1.3 constant_dynamic-slice_fusion
  513.8 0.7 slice_reduce_fusion.4
  514.5 1.3 slice_bitcast_fusion.1
  515.8 1.3 slice_bitcast_fusion
  517.1 0.8 slice_reduce_fusion.1
  517.8 0.7 slice.106
  518.5 0.7 slice.101
  519.2 1.8 copy.83
  521.0 0.7 copy.84
  521.7 0.6 copy.85
  522.3 0.7 copy.86
  523.0 0.7 copy.87
  (65 shorter events, 3.0 us)
Async XLA Ops:
  6.0 3.7 copy-start.9
  337.4 139.8 %copy-start.7 = (f32[8,3072]{1,0:T(8,128)S(1)}, f32[8,3072]{1,0:T(8,128)}, u32[]{:S(2)}) copy-start(f32[8,3072]{1,0:T(8,128)} %get-tuple-element.83) | copy-start | bytes 294916
  337.4 139.9 %copy-start.6 = (f32[8,3072]{1,0:T(8,128)S(1)}, f32[8,3072]{1,0:T(8,128)}, u32[]{:S(2)}) copy-start(f32[8,3072]{1,0:T(8,128)} %get-tuple-element.84) | copy-start | bytes 294916
  337.4 140.0 %copy-start.5 = (f32[8,8,768]{2,1,0:T(8,128)S(1)}, f32[8,8,768]{2,1,0:T(8,128)}, u32[]{:S(2)}) copy-start(f32[8,8,768]{2,1,0:T(8,128)} %get-tuple-element.79) | copy-start | bytes 589828
  337.4 140.9 %copy-start.4 = (f32[9,8,768]{2,1,0:T(8,128)S(1)}, f32[9,8,768]{2,1,0:T(8,128)}, u32[]{:S(2)}) copy-start(f32[9,8,768]{2,1,0:T(8,128)} %get-tuple-element.80) | copy-start | bytes 663556
  337.4 141.0 %copy-start = (f32[9,8,3072]{2,1,0:T(8,128)S(1)}, f32[9,8,3072]{2,1,0:T(8,128)}, u32[]{:S(2)}) copy-start(f32[9,8,3072]{2,1,0:T(8,128)} %get-tuple-element.82) | copy-start | bytes 2654212
  479.1 32.8 %copy-start.10 = (bf16[1,768]{1,0:T(2,128)(2,1)S(1)}, bf16[1,768]{1,0:T(2,128)(2,1)}, u32[]{:S(2)}) copy-start(bf16[1,768]{1,0:T(2,128)(2,1)} %param.18) | copy-start | bytes 4612
  479.3 41.7 %copy-start.3 = (f32[24,2304]{1,0:T(8,128)S(1)}, f32[24,2304]{1,0:T(8,128)}, u32[]{:S(2)}) copy-start(f32[24,2304]{1,0:T(8,128)} %get-tuple-element.133) | copy-start | bytes 663556
  479.5 42.2 %copy-start.8 = (f32[24,768]{1,0:T(8,128)S(1)}, f32[24,768]{1,0:T(8,128)}, u32[]{:S(2)}) copy-start(f32[24,768]{1,0:T(8,128)} %get-tuple-element.134) | copy-start | bytes 221188
  480.3 42.0 %copy-start.2 = (f32[24,3072]{1,0:T(8,128)S(1)}, f32[24,3072]{1,0:T(8,128)}, u32[]{:S(2)}) copy-start(f32[24,3072]{1,0:T(8,128)} %get-tuple-element.136) | copy-start | bytes 884740
  480.3 42.8 %copy-start.1 = (f32[96,768]{1,0:T(8,128)S(1)}, f32[96,768]{1,0:T(8,128)}, u32[]{:S(2)}) copy-start(f32[96,768]{1,0:T(8,128)} %get-tuple-element.140) | copy-start | bytes 884740

commit v2 on v1

v2 whole, which is shorter than its diff:
```python
import functools

import jax
import jax.numpy as jnp
from jax import lax
from jax.experimental import pallas as pl
from jax.experimental.pallas import tpu as pltpu
from jax.sharding import PartitionSpec as P

HEAD = 64
GRID = 32
HALF = 16
GROUP = 256
TOKENS = 1024
C0 = 0.7978845608028654
C1 = 0.044715
EPS = 1e-06
MIB = 1 << 20
AXES = ("wide", "narrow")
F32, BF16 = jnp.float32, jnp.bfloat16


def dot_nn(a, b):
    return lax.dot_general(a, b, (((1,), (0,)), ((), ())), preferred_element_type=F32)


def dot_nt(a, b):
    return lax.dot_general(a, b, (((1,), (1,)), ((), ())), preferred_element_type=F32)


def dot_tn(a, b):
    return lax.dot_general(a, b, (((0,), (0,)), ((), ())), preferred_element_type=F32)


def whole(shape):
    return pl.BlockSpec(shape, lambda *_: (0,) * len(shape))


def once(shape):
    return pl.BlockSpec(shape, lambda *_: (0,) * len(shape), pipeline_mode=pl.Buffered(1))


def like(shape, dtype):
    return jax.ShapeDtypeStruct(shape, dtype)


def shift_pair(pair, parity, first, last):
    low, high = pair
    zero = jnp.zeros_like(low)
    if parity == 0:
        low, high = pltpu.roll(low, 1, 0), pltpu.roll(high, 1, 0)
        return jnp.where(first, zero, low), jnp.where(first, low, high)
    low, high = pltpu.roll(low, 7, 0), pltpu.roll(high, 7, 0)
    return jnp.where(last, high, low), jnp.where(last, zero, high)


def row_sources(gi, r):
    if gi == 0:
        return ((1, r - 1), (0, r), (1, r))
    return ((0, r), (1, r), (0, r + 1))


def load_pair(ref, slab, gi, gj, r):
    tile = 2 + 2 * r
    group = 2 * gi + gj
    return ref[slab, group, tile], ref[slab, group, tile + 1]


def store_pair(ref, slab, gi, gj, r, pair):
    tile = 2 + 2 * r
    group = 2 * gi + gj
    ref[slab, group, tile] = pair[0]
    ref[slab, group, tile + 1] = pair[1]


def edge_masks():
    sub = lax.broadcasted_iota(jnp.int32, (8, 128), 0)
    return sub == 0, sub == 7


def clear_edges(ref):
    slabs = ref.shape[0]
    ref[:, :, 0:2] = jnp.zeros((slabs, 4, 2, 8, 128), F32)
    ref[:, :, 34:36] = jnp.zeros((slabs, 4, 2, 8, 128), F32)


def conv_cell(src, slab, gi, gj, r, k, bias, masks):
    sources = row_sources(gi, r)
    other = 1 - gj
    near = 2 if gj == 0 else 0
    far = 2 - near
    same = [load_pair(src, slab, p, gj, rr) for p, rr in sources]
    cross = [load_pair(src, slab, p, other, rr) for p, rr in sources]
    straight, moved = [], []
    for h in (0, 1):
        acc, off = bias, None
        for a in range(3):
            acc = acc + k[3 * a + 1] * same[a][h] + k[3 * a + near] * cross[a][h]
            term = k[3 * a + far] * cross[a][h]
            off = term if off is None else off + term
        straight.append(acc)
        moved.append(off)
    moved = shift_pair(moved, gj, *masks)
    return straight[0] + moved[0], straight[1] + moved[1]


def conv_back_row(slab, k, src, grad, grad_moved, put, r, carry):
    kg, total = list(carry[:9]), carry[9]
    for gi in (0, 1):
        sources = row_sources(gi, r)
        for gj in (0, 1):
            other = 1 - gj
            near = 2 if gj == 0 else 0
            here = load_pair(src, slab, gi, gj, r)
            out = [None, None]
            for a in range(3):
                p, rr = sources[2 - a]
                trio = {
                    1: load_pair(grad, slab, p, gj, rr),
                    2 - near: load_pair(grad, slab, p, other, rr),
                    near: load_pair(grad_moved, slab, p, other, rr),
                }
                for b in range(3):
                    n = 3 * a + b
                    for h in (0, 1):
                        term = k[n] * trio[b][h]
                        out[h] = term if out[h] is None else out[h] + term
                        kg[n] = kg[n] + here[h] * trio[b][h]
            total = total + out[0] + out[1]
            put(gi, gj, r, out)
    return tuple(kg) + (total,)


def conv_back(slab, k, src, grad, grad_moved, put):
    body = lambda r, carry: conv_back_row(slab, k, src, grad, grad_moved, put, r, carry)
    return lax.fori_loop(0, HALF, body, (jnp.zeros((8, 128), F32),) * 10)


def group_rows(gi, gj, r):
    return pl.ds(pl.multiple_of((2 * gi + gj) * GROUP + r * HALF, HALF), HALF)


def row_sum(values):
    rows, columns = values.shape
    return jnp.sum(values.reshape(rows // 8, 8, columns), axis=0)


def unit_rows(values):
    model = values.shape[-1]
    centered = values - jnp.sum(values, axis=-1, keepdims=True) * (1.0 / model)
    spread = jnp.sum(centered * centered, axis=-1, keepdims=True) * (1.0 / model)
    scale = lax.rsqrt(spread + EPS)
    return centered * scale, scale


def unit_back(grad, unit, scale):
    model = grad.shape[-1]
    mean = jnp.sum(grad, axis=-1, keepdims=True) * (1.0 / model)
    tilt = jnp.sum(grad * unit, axis=-1, keepdims=True) * (1.0 / model)
    return scale * (grad - mean - unit * tilt)


def order_matrix():
    d = jnp.arange(GROUP)
    group, position, column = d // 64, (d % 64) // HALF, d % HALF
    source = (2 * position + group // 2) * GRID + 2 * column + group % 2
    return (source[:, None] == jnp.arange(GROUP)[None, :]).astype(BF16)


def ff_kernel(n2_ref, n2t_ref, g2_ref, fc1_ref, small_ref, fc2_ref,
              branch_ref, gn2_ref, w1g_ref, w2g_ref, sums_ref,
              hid, ga, gc, gcs, act, ghl):
    step = pl.program_id(0)
    slabs = hid.shape[0]

    @pl.when(step == 0)
    def _():
        branch_ref[...] = jnp.zeros_like(branch_ref)
        gn2_ref[...] = jnp.zeros_like(gn2_ref)
        for ref in (hid, gc, gcs):
            clear_edges(ref)

    for g in range(4):
        rows = pl.ds(g * GROUP, GROUP)
        full = dot_nn(n2_ref[rows, :], fc1_ref[...]) + small_ref[10:11, :]
        back = dot_nt(g2_ref[rows, :], fc2_ref[...])
        for slab in range(slabs):
            lanes = slice(slab * 128, slab * 128 + 128)
            hid[slab, g, 2:34] = full[:, lanes].reshape(32, 8, 128)
            ga[slab, g] = back[:, lanes].reshape(32, 8, 128)

    masks = edge_masks()
    for slab in range(slabs):
        lanes = pl.ds(slab * 128, 128)
        k = [jnp.broadcast_to(small_ref[n : n + 1, lanes], (8, 128)) for n in range(9)]
        bias = jnp.broadcast_to(small_ref[9:10, lanes], (8, 128))

        def forward(r, total):
            for gi in (0, 1):
                for gj in (0, 1):
                    pair = conv_cell(hid, slab, gi, gj, r, k, bias, masks)
                    acts, grads = [], []
                    for h in (0, 1):
                        x = pair[h]
                        x2 = x * x
                        half = 0.5 * jnp.tanh(x * (C0 + (C0 * C1) * x2)) + 0.5
                        value = x * half
                        slope = half + (value - value * half) * (2.0 * C0 + (6.0 * C0 * C1) * x2)
                        acts.append(value)
                        grads.append(ga[slab, 2 * gi + gj, 2 * r + h] * slope)
                        total = total + grads[-1]
                    act[group_rows(gi, gj, r), lanes] = jnp.concatenate(acts, 0).astype(BF16)
                    store_pair(gc, slab, gi, gj, r, grads)
                    store_pair(gcs, slab, gi, gj, r, shift_pair(grads, 1 - gj, *masks))
            return total

        total = lax.fori_loop(0, HALF, forward, jnp.zeros((8, 128), F32))

        def put(gi, gj, r, pair):
            ghl[group_rows(gi, gj, r), lanes] = jnp.concatenate(pair, 0).astype(BF16)

        sums = conv_back(slab, k, hid, gc, gcs, put)
        for n, value in enumerate([*sums[:9], total, sums[9]]):
            sums_ref[n : n + 1, lanes] = jnp.sum(value, axis=0, keepdims=True)
        sums_ref[11:16, lanes] = jnp.zeros((5, 128), F32)

    branch_ref[...] += dot_nn(act[...], fc2_ref[...])
    gn2_ref[...] += dot_nt(ghl[...], fc1_ref[...])
    w2g_ref[...] = dot_tn(act[...], g2_ref[...]).astype(w2g_ref.dtype)
    w1g_ref[...] = dot_nn(n2t_ref[...], ghl[...]).astype(w1g_ref.dtype)


def feed_forward(n2, g2, fc1, small, fc2, width=256):
    tokens, model = n2.shape
    hidden = fc1.shape[1]
    slabs = width // 128
    padded = pltpu.VMEM((slabs, 4, 36, 8, 128), F32)
    columns = lambda rows: pl.BlockSpec((rows, width), lambda s: (0, s))
    lines = pl.BlockSpec((width, model), lambda s: (s, 0))
    return pl.pallas_call(
        ff_kernel,
        grid=(hidden // width,),
        in_specs=[
            once((tokens, model)), once((model, tokens)), once((tokens, model)),
            columns(model), columns(16), lines,
        ],
        out_specs=[whole((tokens, model)), whole((tokens, model)), columns(model), lines, columns(16)],
        out_shape=[
            like((tokens, model), F32), like((tokens, model), F32),
            like((model, hidden), BF16), like((hidden, model), BF16), like((16, hidden), F32),
        ],
        scratch_shapes=[
            padded, pltpu.VMEM((slabs, 4, 32, 8, 128), F32), padded, padded,
            pltpu.VMEM((tokens, width), BF16), pltpu.VMEM((tokens, width), BF16),
        ],
        compiler_params=pltpu.CompilerParams(vmem_limit_bytes=56 * MIB),
        name="feed_forward",
    )(n2, n2.T, g2, fc1, small, fc2)


def flip(index, bit):
    return index + bit - 2 * bit * lax.rem(index // bit, 2)


def bits_of(count):
    return [1 << b for b in range(count.bit_length() - 1)]


def at(w, n):
    return {"wide": w, "narrow": n}


def greet(places):
    barrier = pltpu.get_barrier_semaphore()
    for place in places:
        pl.semaphore_signal(barrier, inc=1, device_id=place, device_id_type=pl.DeviceIdType.MESH)
    pl.semaphore_wait(barrier, len(places))


def greet_all(place):
    barrier = pltpu.get_barrier_semaphore()
    total = place.total

    def body(k, carry):
        pl.semaphore_signal(
            barrier, inc=1, device_id=place.device(lax.rem(place.sid + k, total)),
            device_id_type=pl.DeviceIdType.MESH,
        )
        return carry

    lax.fori_loop(1, total, body, 0)
    pl.semaphore_wait(barrier, total - 1)


def remote(src, dst, send_sem, recv_sem, place):
    return pltpu.make_async_remote_copy(
        src_ref=src, dst_ref=dst, send_sem=send_sem, recv_sem=recv_sem, device_id=place,
        device_id_type=pl.DeviceIdType.MESH,
    )


class Place:
    def __init__(self, wide, narrow):
        self.wide, self.narrow = wide, narrow
        self.w, self.n = lax.axis_index("wide"), lax.axis_index("narrow")
        self.total, self.half = wide * narrow, wide * narrow // 2
        self.me = self.w * narrow + self.n
        self.core = lax.rem(self.w, 2)
        self.slot = (self.w // 2) * narrow + self.n
        self.sid = self.core * self.half + self.slot
        self.sibling = at(flip(self.w, 1), self.n)

    def device(self, sid):
        core, slot = sid // self.half, lax.rem(sid, self.half)
        return at(2 * (slot // self.narrow) + core, lax.rem(slot, self.narrow))

    def partners(self):
        places = [at(self.w, lax.rem(self.n + k, self.narrow)) for k in range(1, self.narrow)]
        return places + [at(flip(self.w, bit), self.n) for bit in bits_of(self.wide)]

    def to_all(self, src_of, dst, sends, recvs):
        def copy(k):
            sid = lax.rem(self.sid + k, self.total)
            return remote(src_of(sid), dst, sends.at[k], recvs.at[k], self.device(sid))

        return exchange(copy, self.total)

    def to_kin(self, src_of, dst, sends, recvs):
        def copy(k):
            slot = lax.rem(self.slot + k, self.half)
            return remote(src_of(slot), dst, sends.at[k], recvs.at[k],
                          self.device(self.core * self.half + slot))

        return exchange(copy, self.half)


def exchange(copy, count):
    def start(k, carry):
        copy(k).start()
        return carry

    def wait(k, carry):
        copy(k).wait()
        return carry

    lax.fori_loop(1, count, start, 0)
    return lambda: lax.fori_loop(1, count, wait, 0)


class Gather:
    def __init__(self, place, src, dst, sends, recvs, chunk, turn, columns):
        self.p = place
        self.src, self.dst = src, dst
        self.sends, self.recvs, self.chunk = sends, recvs, chunk
        self.columns = columns
        far = bits_of(place.wide)[1:]
        cut = turn % len(far) if far else 0
        self.order = far[cut:] + far[:cut] + bits_of(place.wide)[:1]
        self.stages = 1 + len(self.order)

    def copies(self, stage):
        w, n, narrow = self.p.w, self.p.n, self.p.narrow
        if stage == 0:
            return [
                remote(self.src.at[:, self.columns], self.dst.at[w, n, :, self.columns],
                       self.sends.at[self.chunk, k - 1], self.recvs.at[self.chunk, k - 1],
                       at(w, lax.rem(n + k, narrow)))
                for k in range(1, narrow)
            ]
        held = [w]
        for bit in self.order[: stage - 1]:
            held = held + [flip(h, bit) for h in held]
        base = narrow - 2 + len(held)
        part = lambda h: self.dst.at[h, :, :, self.columns]
        return [
            remote(part(h), part(h), self.sends.at[self.chunk, base + i],
                   self.recvs.at[self.chunk, base + i], at(flip(w, self.order[stage - 1]), n))
            for i, h in enumerate(held)
        ]

    def start(self, stage):
        for copy in self.copies(stage):
            copy.start()

    def wait(self, stage):
        for copy in self.copies(stage):
            copy.wait_recv()

    def finish(self):
        for stage in range(self.stages):
            for copy in self.copies(stage):
                copy.wait_send()


class Waves:
    def __init__(self, chunks):
        self.chunks, self.wave = chunks, 0
        self.stages = chunks[0][0].stages
        self.count = len(chunks) + self.stages

    def run(self, wave):
        for c, jobs in enumerate(self.chunks):
            stage = wave - c
            for job in jobs:
                if 1 <= stage <= self.stages:
                    job.wait(stage - 1)
                if 0 <= stage < self.stages:
                    job.start(stage)

    def tick(self, times=1):
        for _ in range(times):
            if self.wave < self.count:
                self.run(self.wave)
                self.wave += 1

    def at_hook(self, hook, hooks):
        left = self.count - 1
        for wave in range(1 + hook * left // hooks, 1 + (hook + 1) * left // hooks):
            self.run(wave)

    def finish(self):
        for jobs in self.chunks:
            for job in jobs:
                job.finish()

    def end(self):
        self.tick(self.count)
        self.finish()


def slots_of(chunks):
    return sum(len(chunk) for chunk in chunks)


def job_sems(wide, narrow, chunks):
    return [pltpu.SemaphoreType.DMA((slots_of(chunks), narrow + wide - 2))] * 2


def gather_jobs(place, srcs, dsts, sends, recvs, chunks):
    jobs, slot = [], 0
    for chunk in chunks:
        jobs.append([])
        for i, start, size, turn in chunk:
            jobs[-1].append(
                Gather(place, srcs[i], dsts[i], sends, recvs, slot, turn, pl.ds(start, size))
            )
            slot += 1
    return Waves(jobs)


def both(i, start, size):
    return [(i, start + turn * (size // 2), size // 2, turn) for turn in (0, 1)]


def insert_bit(index, position, value):
    low = index % (1 << position)
    return ((index // (1 << position)) * 2 + value) * (1 << position) + low


class Scatter:
    def __init__(self, place, src, buffers, out, sends, recvs, chunk, turn, columns):
        self.p = place
        self.src, self.out = src, out
        self.halves, self.line, self.got = buffers[:-2], buffers[-2], buffers[-1]
        self.sends, self.recvs, self.chunk = sends, recvs, chunk
        self.columns = columns
        far = bits_of(place.wide)[1:]
        cut = turn % len(far) if far else 0
        self.order = bits_of(place.wide)[:1] + far[cut:] + far[:cut]
        self.stages = 1 + len(self.order)
        self.rows = self.line.shape[1]

    def level(self, stage):
        source = self.src if stage == 0 else self.halves[stage - 1]
        bit = self.order[stage]
        wide = self.p.wide
        position = sum(1 for b in bits_of(wide) if b < bit and b not in self.order[:stage])
        return source, bit, position, wide >> (stage + 1)

    def copies(self, stage):
        w, n, narrow = self.p.w, self.p.n, self.p.narrow
        if stage == len(self.order):
            base = self.p.wide - 1
            return [
                remote(self.line.at[lax.rem(n + k, narrow), :, self.columns],
                       self.got.at[k - 1, :, self.columns],
                       self.sends.at[self.chunk, base + k - 1], self.recvs.at[self.chunk, base + k - 1],
                       at(w, lax.rem(n + k, narrow)))
                for k in range(1, narrow)
            ]
        source, bit, position, size = self.level(stage)
        theirs = 1 - lax.rem(w // bit, 2)
        base = self.p.wide - 2 * size
        return [
            remote(source.at[insert_bit(j, position, theirs), :, self.columns],
                   self.halves[stage].at[j, :, self.columns],
                   self.sends.at[self.chunk, base + j], self.recvs.at[self.chunk, base + j],
                   at(flip(w, bit), n))
            for j in range(size)
        ]

    def start(self, stage):
        for copy in self.copies(stage):
            copy.start()

    def wait(self, stage):
        for copy in self.copies(stage):
            copy.wait()
        if stage == len(self.order):
            value = self.line[self.p.n, :, self.columns].astype(F32)
            for k in range(1, self.p.narrow):
                value = value + self.got[k - 1, :, self.columns].astype(F32)
            self.out[:, self.columns] = value
        else:
            self.add(stage)

    def add(self, stage):
        source, bit, position, size = self.level(stage)
        mine = lax.rem(self.p.w // bit, 2)
        into = self.halves[stage]
        for j in range(size):
            index = insert_bit(j, position, mine)
            if stage == len(self.order) - 1:
                total = (source[index, :, self.columns].astype(F32)
                         + into[j, :, self.columns].astype(F32))
                for m in range(self.p.narrow):
                    rows = slice(m * self.rows, (m + 1) * self.rows)
                    self.line[m, :, self.columns] = total[rows].astype(BF16)
                continue

            def body(i, carry):
                rows = pl.ds(pl.multiple_of(i * 16, 16), 16)
                into[j, rows, self.columns] = (
                    source[index, rows, self.columns].astype(F32)
                    + into[j, rows, self.columns].astype(F32)
                ).astype(BF16)
                return carry

            lax.fori_loop(0, into.shape[1] // 16, body, 0)

    def finish(self):
        pass


def scatter_scratch(wide, narrow, shapes):
    scratch = []
    for _, height, columns in shapes:
        for stage in range(len(bits_of(wide))):
            scratch.append(pltpu.VMEM((wide >> (stage + 1), height, columns), BF16))
        scratch.append(pltpu.VMEM((narrow, height // narrow, columns), BF16))
        scratch.append(pltpu.VMEM((narrow - 1, height // narrow, columns), BF16))
    return scratch


def scatter_jobs(place, srcs, outs, buffers, sends, recvs, chunks):
    per = len(buffers) // len(srcs)
    jobs, slot = [], 0
    for chunk in chunks:
        jobs.append([])
        for i, start, size, turn in chunk:
            own = buffers[i * per : (i + 1) * per]
            jobs[-1].append(
                Scatter(place, srcs[i], own, outs[i], sends, recvs, slot, turn, pl.ds(start, size))
            )
            slot += 1
    return Waves(jobs)


def owned_shape(shape, narrow):
    return like((shape[1] // narrow, shape[2]), F32)


def spread_pieces(pieces, own):
    total, rows, _ = pieces.shape
    used = lax.broadcasted_iota(jnp.int32, (rows, 128), 1) < own
    tiles = [None] * (total * own // 128 + 1)
    for d in range(total):
        piece = jnp.where(used, pieces[d], 0.0)
        tile, shift = divmod(d * own, 128)
        if shift:
            piece = pltpu.roll(piece, shift, 1)
        lane = lax.broadcasted_iota(jnp.int32, (rows, 128), 1)
        parts = [(tile, jnp.where(lane >= shift, piece, 0.0))]
        if shift + own > 128:
            parts.append((tile + 1, jnp.where(lane < shift, piece, 0.0)))
        for t, part in parts:
            tiles[t] = part if tiles[t] is None else tiles[t] + part
    return jnp.concatenate(tiles[: total * own // 128], axis=1)


def cut_piece(values, d, own):
    tile, shift = divmod(d * own, 128)
    piece = values[:, tile * 128 : tile * 128 + 128]
    if not shift:
        return piece
    piece = pltpu.roll(piece, 128 - shift, 1)
    if shift + own > 128:
        after = pltpu.roll(values[:, tile * 128 + 128 : tile * 128 + 256], 128 - shift, 1)
        lane = lax.broadcasted_iota(jnp.int32, piece.shape, 1)
        piece = jnp.where(lane < 128 - shift, piece, after)
    return piece


def front_kernel(wide, narrow, chunks, count, own, own_ff, *refs):
    (x_ref, cot_ref, mask_ref, order_ref, sil_ref, ada_ref, bias_ref, small_ref) = refs[:8]
    srcs = refs[8 : 8 + count]
    (mod_ref, sils_ref, model_ref, hidden_ref, lat_ref, gout_ref, g2_ref, normed_ref, mixed_ref,
     keep_ref, fc2b_ref) = refs[8 + count : 19 + count]
    dsts = refs[19 + count : 19 + 2 * count]
    (got, part, sib, rows_in, smalls, send_a, recv_a, send_b, recv_b, send_c, recv_c,
     sends, recvs, local) = refs[19 + 2 * count :]
    p = Place(wide, narrow)
    model = x_ref.shape[1]
    slabs = model // 128
    own_copies = [
        pltpu.make_async_copy(srcs[i], dsts[i].at[p.w, p.n], local.at[i]) for i in range(count)
    ]
    for copy in own_copies:
        copy.start()
    smalls[p.w, p.n] = small_ref[...]
    greet_all(p)
    got[p.sid] = sil_ref[p.sid]
    wait_sil = p.to_all(lambda sid: sil_ref.at[sid], got.at[p.sid], send_a, recv_a)
    waves = gather_jobs(p, [small_ref, *srcs], [smalls, *dsts], sends, recvs, chunks)
    waves.tick()

    clear_edges(normed_ref)

    def arrange(t):
        rows = pl.ds(t * GROUP, GROUP)
        tokens = dot_nn(order_ref[...], x_ref[rows, :])
        unit, _ = unit_rows(tokens)
        kept = dot_nn(order_ref[...], mask_ref[rows, :])
        gout = dot_nn(order_ref[...], cot_ref[rows, :]) * jnp.concatenate([kept] * slabs, axis=1)
        for g in range(4):
            src = slice(64 * g, 64 * g + 64)
            dst = pl.ds(g * GROUP + 64 * t, 64)
            lat_ref[dst, :] = tokens[src].astype(BF16)
            gout_ref[dst, :] = gout[src].astype(BF16)
            keep_ref[dst, :] = (kept[src] - 1.0) * 1e30
            for s in range(slabs):
                tile = unit[src, s * 128 : s * 128 + 128].reshape(8, 8, 128)
                normed_ref[s, g, 2 + 8 * t : 10 + 8 * t] = tile

    arrange(0)
    for copy in own_copies:
        copy.wait()
    waves.tick()
    wait_sil()
    sil = got[...].reshape(p.total, 128)
    sils_ref[...] = sil
    product = dot_nn(sil[:, :own].astype(BF16), ada_ref[...]) + bias_ref[...]
    for d in range(p.total):
        part[d // p.half, d % p.half] = product[d : d + 1, :]
    to_sibling = remote(part.at[1 - p.core], sib, send_b, recv_b, p.sibling)
    to_sibling.start()
    arrange(1)
    to_sibling.wait()
    part[p.core] = part[p.core] + sib[...]
    rows_in[p.slot] = part[p.core, p.slot]
    wait_rows = p.to_kin(lambda slot: part.at[p.core, slot], rows_in.at[p.slot], send_c, recv_c)
    waves.tick()
    arrange(2)
    waves.tick()
    arrange(3)
    waves.tick()
    small = smalls[...].reshape(p.total, 32, 128).astype(F32)
    model_ref[...] = spread_pieces(small[:, :16], own)
    hidden_ref[...] = spread_pieces(small[:, 16:], own_ff)
    wait_rows()
    mod = jnp.sum(rows_in[...], axis=0)
    for i in range(6):
        mod_ref[i : i + 1, :] = mod[:, i * model : (i + 1) * model]
    waves.tick()

    shift, scale, gate = mod_ref[0:1, :], mod_ref[1:2, :], mod_ref[5:6, :]
    total = jnp.zeros((8, model), F32)
    for g in range(4):
        rows = pl.ds(g * GROUP, GROUP)
        two = gout_ref[rows, :].astype(F32) * gate
        total = total + row_sum(two)
        g2_ref[rows, :] = two.astype(BF16)
    fc2b_ref[...] = total
    masks = edge_masks()
    for s in range(slabs):
        lanes = pl.ds(s * 128, 128)
        at_s = slice(s * 128, s * 128 + 128)
        shift8 = jnp.broadcast_to(shift[:, at_s], (8, 128))
        scale8 = jnp.broadcast_to(1.0 + scale[:, at_s], (8, 128))
        normed_ref[s, :, 2:34] = normed_ref[s, :, 2:34] * scale8 + shift8
        k = [jnp.broadcast_to(model_ref[n : n + 1, at_s], (8, 128)) for n in range(9)]
        bias = jnp.broadcast_to(model_ref[9:10, at_s], (8, 128))

        def body(r, carry):
            for gi in (0, 1):
                for gj in (0, 1):
                    pair = conv_cell(normed_ref, s, gi, gj, r, k, bias, masks)
                    mixed_ref[group_rows(gi, gj, r), lanes] = jnp.concatenate(pair, 0).astype(BF16)
            return carry

        lax.fori_loop(0, HALF, body, 0)
        waves.tick()
    waves.end()


def front(wide, narrow, x, cot, mask, order, sil, ada, bias, small, blocks, chunks, hidden):
    total = wide * narrow
    tokens, model = x.shape
    slabs, count, columns = model // 128, len(blocks), ada.shape[1]
    own, own_ff = model // total, hidden // total
    inside = pl.BlockSpec(memory_space=pltpu.VMEM)
    anywhere = pl.BlockSpec(memory_space=pl.ANY)
    all_sems = pltpu.SemaphoreType.DMA((total,))
    one_sem = pltpu.SemaphoreType.DMA
    kin_sems = pltpu.SemaphoreType.DMA((total // 2,))
    return pl.pallas_call(
        functools.partial(front_kernel, wide, narrow, chunks, count, own, own_ff),
        in_specs=[inside] * 8 + [anywhere] * count,
        out_specs=[inside] * 11 + [anywhere] * count,
        out_shape=[
            like((8, model), F32), like((total, 128), F32), like((16, model), F32),
            like((16, hidden), F32), like((tokens, model), BF16), like((tokens, model), BF16),
            like((tokens, model), BF16), like((slabs, 4, 36, 8, 128), F32),
            like((tokens, model), BF16), like((tokens, 128), F32), like((8, model), F32),
        ] + [like((wide, narrow) + b.shape, BF16) for b in blocks],
        scratch_shapes=[
            pltpu.VMEM((total, 1, 128), F32), pltpu.VMEM((2, total // 2, 1, columns), F32),
            pltpu.VMEM((total // 2, 1, columns), F32), pltpu.VMEM((total // 2, 1, columns), F32),
            pltpu.VMEM((wide, narrow, 32, 128), BF16),
            all_sems, all_sems, one_sem, one_sem, kin_sems, kin_sems,
            *job_sems(wide, narrow, chunks), pltpu.SemaphoreType.DMA((count,)),
        ],
        compiler_params=pltpu.CompilerParams(
            vmem_limit_bytes=56 * MIB, collective_id=0, has_side_effects=True
        ),
        name="front",
    )(x, cot, mask, order, sil, ada, bias, small, *blocks)


def attend_kernel(wide, narrow, chunks, count, *refs):
    mixed_ref, lat_ref, keep_ref, mod_ref, small_ref, qkv_ref, proj_ref = refs[:7]
    srcs = refs[7 : 7 + count]
    triple_ref, probs_ref, att_ref, branch_ref, middle_ref, n2_ref = refs[7 + count : 13 + count]
    dsts = refs[13 + count : 13 + 2 * count]
    sends, recvs, local = refs[13 + 2 * count :]
    step = pl.program_id(0)
    p = Place(wide, narrow)
    waves = gather_jobs(p, srcs, dsts, sends, recvs, chunks)
    own_copies = [
        pltpu.make_async_copy(srcs[i], dsts[i].at[p.w, p.n], local.at[i]) for i in range(count)
    ]

    def on(when, work):
        pl.when(step == when)(work)

    def first():
        for copy in own_copies:
            copy.start()
        greet(p.partners())
        waves.run(0)
        for copy in own_copies:
            copy.wait()

    def hook(position):
        for when in range(4):
            on(when, lambda: waves.at_hook(2 * when + position, 8))

    on(0, first)
    model = lat_ref.shape[1]
    slabs = model // 128
    triple_ref[...] = dot_nn(mixed_ref[...], qkv_ref[...]).astype(BF16)
    lane = lax.broadcasted_iota(jnp.int32, (GROUP, 128), 1)
    left = lane < HEAD
    keep = jnp.concatenate([keep_ref[...]] * 2, axis=1)
    for s in range(slabs):
        q = triple_ref[:, s * 128 : s * 128 + 128]
        k = triple_ref[:, model + s * 128 : model + s * 128 + 128] * jnp.asarray(0.125, BF16)
        v = triple_ref[:, 2 * model + s * 128 : 2 * model + s * 128 + 128]
        outs = []
        for h in (0, 1):
            mine = left if h == 0 else jnp.logical_not(left)
            scores = dot_nt(jnp.where(mine, k, jnp.zeros_like(k)), q) + keep
            e = jnp.exp(scores - jnp.max(scores, axis=0, keepdims=True))
            prob = (e * (1.0 / jnp.sum(e, axis=0, keepdims=True))).astype(BF16)
            probs_ref[2 * s + h] = prob
            outs.append(dot_tn(prob, v))
        att_ref[:, s * 128 : s * 128 + 128] = jnp.where(left, outs[0], outs[1]).astype(BF16)
        if s == slabs // 2 - 1:
            hook(0)
    branch = dot_nn(att_ref[...], proj_ref[...]) + small_ref[10:11, :]
    middle = lat_ref[...].astype(F32) + mod_ref[2:3, :] * branch
    unit, _ = unit_rows(middle)
    branch_ref[...] = branch
    middle_ref[...] = middle
    n2_ref[...] = (unit * (1.0 + mod_ref[4:5, :]) + mod_ref[3:4, :]).astype(BF16)
    hook(1)
    on(3, waves.finish)


def attend(wide, narrow, mixed, lat, keep, mod, small, qkv, proj, blocks, chunks):
    tokens, model = lat.shape
    heads, count = model // HEAD, len(blocks)
    by_group = lambda columns: pl.BlockSpec((GROUP, columns), lambda g: (g, 0))
    anywhere = pl.BlockSpec(memory_space=pl.ANY)
    return pl.pallas_call(
        functools.partial(attend_kernel, wide, narrow, chunks, count),
        grid=(4,),
        in_specs=[
            by_group(model), by_group(model), by_group(128), whole(mod.shape),
            whole(small.shape), once(qkv.shape), once(proj.shape),
        ] + [anywhere] * count,
        out_specs=[
            by_group(3 * model), pl.BlockSpec((heads, GROUP, GROUP), lambda g: (g, 0, 0)),
            by_group(model), by_group(model), by_group(model), by_group(model),
        ] + [anywhere] * count,
        out_shape=[
            like((tokens, 3 * model), BF16), like((4 * heads, GROUP, GROUP), BF16),
            like((tokens, model), BF16), like((tokens, model), F32),
            like((tokens, model), F32), like((tokens, model), BF16),
        ] + [like((wide, narrow) + b.shape, BF16) for b in blocks],
        scratch_shapes=[*job_sems(wide, narrow, chunks), pltpu.SemaphoreType.DMA((count,))],
        compiler_params=pltpu.CompilerParams(
            vmem_limit_bytes=56 * MIB, collective_id=1, has_side_effects=True
        ),
        name="attend",
    )(mixed, lat, keep, mod, small, qkv, proj, *blocks)


def back_kernel(wide, narrow, chunks, count, *refs):
    (gn2_ref, two_ref, middle_ref, branch_ref, gout_ref, att_ref, triple_ref, probs_ref, mixed_ref,
     mod_ref, small_ref, proj_ref, qkv_ref) = refs[:13]
    srcs = refs[13 : 13 + count]
    out_ref, gmid_ref, gmix_ref, sums_ref, qkvg_ref, projg_ref = refs[13 + count : 19 + count]
    outs = refs[19 + count : 19 + 2 * count]
    ga, gt, qkv_sum, proj_sum = refs[19 + 2 * count : 23 + 2 * count]
    buffers, (sends, recvs) = refs[23 + 2 * count : -2], refs[-2:]
    step = pl.program_id(0)
    model = gn2_ref.shape[1]
    slabs = model // 128
    p = Place(wide, narrow)
    waves = scatter_jobs(p, srcs, outs, buffers, sends, recvs, chunks)

    def hook(position):
        for when in range(4):
            pl.when(step == when)(lambda: waves.at_hook(4 * when + position, 16))

    @pl.when(step == 0)
    def _():
        greet(p.partners())
        waves.run(0)
        sums_ref[...] = jnp.zeros_like(sums_ref)
        qkv_sum[...] = jnp.zeros_like(qkv_sum)
        proj_sum[...] = jnp.zeros_like(proj_sum)

    middle = middle_ref[...]
    two = two_ref[...] + small_ref[11:12, :]
    gout = gout_ref[...].astype(F32)
    out_ref[...] = (middle + mod_ref[5:6, :] * two).astype(BF16)
    sums_ref[3] += row_sum(gout * two)
    unit, scale = unit_rows(middle)
    gn2 = gn2_ref[...]
    sums_ref[1] += row_sum(gn2)
    sums_ref[2] += row_sum(gn2 * unit)
    gm = gout + unit_back(gn2 * (1.0 + mod_ref[4:5, :]), unit, scale)
    gmid_ref[...] = gm
    sums_ref[0] += row_sum(gm * branch_ref[...])
    gb = gm * mod_ref[2:3, :]
    sums_ref[4] += row_sum(gb)
    gbl = gb.astype(BF16)
    proj_sum[...] += dot_tn(att_ref[...], gbl)
    ga[...] = dot_nt(gbl, proj_ref[...]).astype(BF16)
    hook(0)
    lane = lax.broadcasted_iota(jnp.int32, (GROUP, 128), 1)
    left = lane < HEAD
    for s in range(slabs):
        lanes = slice(s * 128, s * 128 + 128)
        q = triple_ref[:, s * 128 : s * 128 + 128] * jnp.asarray(0.125, BF16)
        k = triple_ref[:, model + s * 128 : model + s * 128 + 128] * jnp.asarray(0.125, BF16)
        v = triple_ref[:, 2 * model + s * 128 : 2 * model + s * 128 + 128]
        g = ga[:, lanes]
        gq = gk = gv = None
        for h in (0, 1):
            own = left if h == 0 else jnp.logical_not(left)
            mine = lambda value: jnp.where(own, value, jnp.zeros_like(value))
            p_low = probs_ref[2 * s + h]
            prob = p_low.astype(F32)
            gh = mine(g)
            gp = dot_nt(v, gh)
            inner = jnp.sum(prob * gp, axis=0, keepdims=True)
            gs = (prob * (gp - inner)).astype(BF16)
            parts = (dot_tn(gs, mine(k)), dot_nn(gs, mine(q)), dot_nn(p_low, gh))
            if h == 0:
                gq, gk, gv = parts
            else:
                gq, gk, gv = gq + parts[0], gk + parts[1], gv + parts[2]
        gt[:, s * 128 : s * 128 + 128] = gq.astype(BF16)
        gt[:, model + s * 128 : model + s * 128 + 128] = gk.astype(BF16)
        gt[:, 2 * model + s * 128 : 2 * model + s * 128 + 128] = gv.astype(BF16)
        if s in (1, 3):
            hook(1 + s // 2)
    qkv_sum[...] += dot_tn(mixed_ref[...], gt[...])
    gmixed = dot_nt(gt[...], qkv_ref[...])
    zero = jnp.zeros((slabs, 1, 2, 8, 128), F32)
    gmix_ref[:, :, 0:2] = zero
    gmix_ref[:, :, 34:36] = zero
    for s in range(slabs):
        gmix_ref[s, 0, 2:34] = gmixed[:, s * 128 : s * 128 + 128].reshape(32, 8, 128)
    hook(3)

    @pl.when(step == 3)
    def _():
        qkvg_ref[...] = qkv_sum[...].astype(BF16)
        projg_ref[...] = proj_sum[...].astype(BF16)
        waves.finish()


def back(wide, narrow, gn2, two, middle, branch, gout, att, triple, probs, mixed, mod, small, proj,
         qkv, arrays, chunks):
    tokens, model = middle.shape
    heads, slabs, count = model // HEAD, model // 128, len(arrays)
    by_group = lambda columns: pl.BlockSpec((GROUP, columns), lambda g: (g, 0))
    shapes = [a.shape for a in arrays]
    return pl.pallas_call(
        functools.partial(back_kernel, wide, narrow, chunks, count),
        grid=(4,),
        in_specs=[by_group(model)] * 6 + [
            by_group(3 * model), pl.BlockSpec((heads, GROUP, GROUP), lambda g: (g, 0, 0)),
            by_group(model), once(mod.shape), once(small.shape), once(proj.shape), once(qkv.shape),
        ] + [once(s) for s in shapes],
        out_specs=[
            by_group(model), by_group(model),
            pl.BlockSpec((slabs, 1, 36, 8, 128), lambda g: (0, g, 0, 0, 0)), once((5, 8, model)),
            once(qkv.shape), once(proj.shape),
        ] + [once(owned_shape(s, narrow).shape) for s in shapes],
        out_shape=[
            like((tokens, model), BF16), like((tokens, model), F32),
            like((slabs, 4, 36, 8, 128), F32), like((5, 8, model), F32),
            like(qkv.shape, BF16), like(proj.shape, BF16),
        ] + [owned_shape(s, narrow) for s in shapes],
        scratch_shapes=[
            pltpu.VMEM((GROUP, model), BF16), pltpu.VMEM((GROUP, 3 * model), BF16),
            pltpu.VMEM(qkv.shape, F32), pltpu.VMEM(proj.shape, F32),
            *scatter_scratch(wide, narrow, shapes), *job_sems(wide, narrow, chunks),
        ],
        compiler_params=pltpu.CompilerParams(
            vmem_limit_bytes=62 * MIB, collective_id=2, has_side_effects=True
        ),
        name="attend_back",
    )(gn2, two, middle, branch, gout, att, triple, probs, mixed, mod, small, proj, qkv, *arrays)


def tail_kernel(wide, narrow, chunks, count, own, own_ff, *refs):
    (lat_ref, gmid_ref, rows_ref, gmix_ref, normed_ref, mod_ref, small_ref, sums_ref, fc2b_ref,
     hidden_ref, sils_ref, ada_ref, order_ref) = refs[:13]
    srcs = refs[13 : 13 + count]
    out_ref, xg_ref, wgrad_ref, bgrad_ref, cond_ref, small_out = refs[13 + count : 19 + count]
    outs = refs[19 + count : 19 + 2 * count]
    (gmoved, gnorm, early, late, cuts, cuts_in, part, send_a, recv_a, send_b, recv_b, send_c, recv_c,
     send_d, recv_d, send_e, recv_e, send_f, recv_f) = refs[19 + 2 * count : 38 + 2 * count]
    buffers, (sends, recvs) = refs[38 + 2 * count : -2], refs[-2:]
    p = Place(wide, narrow)
    model = lat_ref.shape[1]
    slabs = model // 128
    greet_all(p)
    waves = scatter_jobs(p, srcs, outs, buffers, sends, recvs, chunks)
    waves.tick()

    gates = jnp.sum(sums_ref[...], axis=1)
    for i, row in enumerate((0, 1, 2, 3)):
        early[p.core, p.slot, :, i * model : (i + 1) * model] = gates[row : row + 1]
    mine = lambda ref: ref.at[p.core, p.slot]
    wait_early = p.to_kin(lambda slot: mine(early), mine(early), send_a, recv_a)

    clear_edges(gmoved)
    masks = edge_masks()
    rows_out = []
    for s in range(slabs):
        lanes = pl.ds(s * 128, 128)
        at_s = slice(s * 128, s * 128 + 128)
        k = [jnp.broadcast_to(small_ref[n : n + 1, at_s], (8, 128)) for n in range(9)]

        def move(r, total):
            for gi in (0, 1):
                for gj in (0, 1):
                    pair = load_pair(gmix_ref, s, gi, gj, r)
                    total = total + pair[0] + pair[1]
                    store_pair(gmoved, s, gi, gj, r, shift_pair(pair, 1 - gj, *masks))
            return total

        total = lax.fori_loop(0, HALF, move, jnp.zeros((8, 128), F32))

        def put(gi, gj, r, pair):
            gnorm[group_rows(gi, gj, r), lanes] = jnp.concatenate(pair, 0)

        sums = conv_back(s, k, normed_ref, gmix_ref, gmoved, put)
        late[p.core, p.slot, :, at_s] = jnp.sum(sums[9], axis=0, keepdims=True)
        column = [jnp.sum(v, axis=0, keepdims=True) for v in (*sums[:9], total)]
        column.append(jnp.sum(sums_ref[4, :, at_s], axis=0, keepdims=True))
        column.append(jnp.sum(fc2b_ref[:, at_s], axis=0, keepdims=True))
        rows_out.append(jnp.concatenate(column + [jnp.zeros((4, 128), F32)], axis=0))
        if s % 2:
            waves.tick()
    narrow_rows = jnp.concatenate(rows_out, axis=1)
    for sid in range(p.total):
        core, slot = divmod(sid, p.half)
        d = (2 * (slot // narrow) + core) * narrow + slot % narrow
        cuts[sid, :16] = cut_piece(narrow_rows, d, own)
        cuts[sid, 16:] = cut_piece(hidden_ref[...], d, own_ff)
    cuts_in[p.sid] = cuts[p.sid]
    wait_cuts = p.to_all(lambda sid: cuts.at[sid], cuts_in.at[p.sid], send_b, recv_b)
    waves.tick()
    scale_sum = jnp.zeros((8, model), F32)
    for g in range(4):
        rows = pl.ds(g * GROUP, GROUP)
        unit, scale = unit_rows(lat_ref[rows, :].astype(F32))
        gn = gnorm[rows, :]
        scale_sum = scale_sum + row_sum(gn * unit)
        grad = gmid_ref[rows, :] + unit_back(gn * (1.0 + mod_ref[1:2, :]), unit, scale)
        gnorm[rows, :] = grad
    late[p.core, p.slot, :, model:] = jnp.sum(scale_sum, axis=0, keepdims=True)
    wait_late = p.to_kin(lambda slot: mine(late), mine(late), send_c, recv_c)
    wait_early()
    swap_early = remote(early.at[p.core], early.at[p.core], send_d, recv_d, p.sibling)
    swap_early.start()
    waves.tick()
    for t in range(4):
        parts = [pl.ds(g * GROUP + 64 * t, 64) for g in range(4)]
        block = jnp.concatenate([rows_ref[q, :] for q in parts], axis=0)
        out_ref[t * GROUP : t * GROUP + GROUP, :] = dot_tn(order_ref[...], block).astype(BF16)
        block = jnp.concatenate([gnorm[q, :].astype(BF16) for q in parts], axis=0)
        xg_ref[t * GROUP : t * GROUP + GROUP, :] = dot_tn(order_ref[...], block).astype(BF16)
    wait_late()
    swap_late = remote(late.at[p.core], late.at[p.core], send_e, recv_e, p.sibling)
    swap_late.start()
    waves.tick()
    swap_early.wait()
    swap_late.wait()
    sil = sils_ref[:, :own].astype(BF16)
    cond = None
    for ref, start in ((late, 0), (early, 2 * model)):
        size = ref.shape[-1]
        span = slice(start, start + size)
        grads = ref[...].reshape(p.total, size)
        bgrad_ref[:, span] = jnp.sum(grads, axis=0, keepdims=True)
        low = grads.astype(BF16)
        wgrad_ref[:, span] = dot_tn(sil, low)
        term = dot_nt(low, ada_ref[:, span])
        cond = term if cond is None else cond + term
    cond = jnp.concatenate([cond, jnp.zeros((p.total, 128 - own), F32)], axis=1)
    for sid in range(p.total):
        part[sid] = cond[sid : sid + 1, :]
    cond_ref[p.me] = part[p.sid]
    wait_cond = p.to_all(lambda sid: part.at[sid], cond_ref.at[p.me], send_f, recv_f)
    wait_cuts()
    small_out[...] = jnp.sum(cuts_in[...], axis=0)
    waves.end()
    wait_cond()


def tail(wide, narrow, lat, gmid, rows, gmix, normed, mod, small, sums, fc2b, hidden_sums, sils, ada,
         order, arrays, chunks):
    total = wide * narrow
    tokens, model = lat.shape
    slabs, count, columns = model // 128, len(arrays), ada.shape[1]
    own, own_ff = ada.shape[0], hidden_sums.shape[1] // total
    shapes = [a.shape for a in arrays]
    all_sems, kin_sems = (pltpu.SemaphoreType.DMA((n,)) for n in (total, total // 2))
    one_sem = pltpu.SemaphoreType.DMA
    return pl.pallas_call(
        functools.partial(tail_kernel, wide, narrow, chunks, count, own, own_ff),
        out_shape=[
            like((tokens, model), BF16), like((tokens, model), BF16), like((own, columns), F32),
            like((1, columns), F32), like((total, 1, 128), F32), like((32, 128), F32),
        ] + [owned_shape(s, narrow) for s in shapes],
        scratch_shapes=[
            pltpu.VMEM((slabs, 4, 36, 8, 128), F32), pltpu.VMEM((tokens, model), F32),
            pltpu.VMEM((2, total // 2, 1, 4 * model), F32),
            pltpu.VMEM((2, total // 2, 1, 2 * model), F32),
            pltpu.VMEM((total, 32, 128), F32), pltpu.VMEM((total, 32, 128), F32),
            pltpu.VMEM((total, 1, 128), F32),
            kin_sems, kin_sems, all_sems, all_sems, kin_sems, kin_sems, one_sem, one_sem,
            one_sem, one_sem, all_sems, all_sems,
            *scatter_scratch(wide, narrow, shapes), *job_sems(wide, narrow, chunks),
        ],
        compiler_params=pltpu.CompilerParams(
            vmem_limit_bytes=60 * MIB, collective_id=3, has_side_effects=True
        ),
        name="tail",
    )(lat, gmid, rows, gmix, normed, mod, small, sums, fc2b, hidden_sums, sils, ada, order, *arrays)


def smooth_gate(values):
    return values * jax.nn.sigmoid(values)


def on_device(wide, narrow, latents, condition, valid_mask, ada_weight, ada_bias, dw1_kernel, dw1_bias,
              qkv_weight, proj_weight, proj_bias, fc1_weight, fc1_bias, dw2_kernel, dw2_bias,
              fc2_weight, fc2_bias, out_cotangent):
    total = wide * narrow
    w, n = lax.axis_index("wide"), lax.axis_index("narrow")
    me = w * narrow + n
    model, hidden = latents.shape[2], fc1_weight.shape[1]
    own, own_ff = model // total, hidden // total

    sil, silu_back = jax.vjp(smooth_gate, condition[0].astype(F32))
    sil = sil.astype(BF16).astype(F32).reshape(wide // 2, 2, narrow, 1, own)
    sil = jnp.pad(sil.transpose(1, 0, 2, 3, 4).reshape(total, 1, own), ((0, 0), (0, 0), (0, 128 - own)))
    bias_at = lax.dynamic_update_slice(
        jnp.zeros((1, 6 * model), F32), ada_bias.astype(F32)[None, :], (0, me * ada_bias.shape[0])
    )
    lanes = lambda rows: jnp.pad(rows, ((0, 0), (0, 128 - rows.shape[1])))
    small = jnp.concatenate([
        lanes(dw1_kernel), lanes(dw1_bias[None]), lanes(proj_bias[None]), lanes(fc2_bias[None]),
        jnp.zeros((4, 128), BF16), lanes(dw2_kernel), lanes(dw2_bias[None]), lanes(fc1_bias[None]),
        jnp.zeros((5, 128), BF16),
    ])
    mask = jnp.broadcast_to(valid_mask[0].astype(BF16)[:, None], (latents.shape[1], 128))
    order = order_matrix()

    chunks = [[(0, 0, 128, 0)], both(1, 0, 3 * model), both(2, 0, model)]
    (mod, sils, model_small, hidden_small, lat, gout, g2, normed, mixed, keep, fc2b, qkv, proj) = front(
        wide, narrow, latents[0], out_cotangent[0], mask, order, sil, ada_weight, bias_at, small,
        [qkv_weight, proj_weight], chunks, hidden,
    )
    qkv, proj = qkv.reshape(model, 3 * model), proj.reshape(model, model)
    chunks = [both(0, 0, hidden), both(1, 0, model)]
    triple, probs, att, branch, middle, n2, fc1, fc2 = attend(
        wide, narrow, mixed, lat, keep, mod, model_small, qkv, proj, [fc1_weight, fc2_weight], chunks
    )
    fc1, fc2 = fc1.reshape(model, hidden), fc2.reshape(hidden, model)
    two, gn2, fc1g, fc2g, hidden_sums = feed_forward(n2, g2, fc1, hidden_small, fc2)
    as_lines = lambda grad: grad.reshape(wide, grad.shape[0] // wide, grad.shape[1])
    chunks = [both(0, 0, hidden), both(1, 0, model)]
    rows, gmid, gmix, sums, qkvg, projg, fc1g, fc2g = back(
        wide, narrow, gn2, two, middle, branch, gout, att, triple, probs, mixed, mod, model_small,
        proj, qkv, [as_lines(fc1g), as_lines(fc2g)], chunks,
    )
    chunks = [both(1, 0, model), both(0, 0, 3 * model)]
    out, xg, ada_wgrad, ada_bsum, cond, small, qkvg, projg = tail(
        wide, narrow, lat, gmid, rows, gmix, normed, mod, model_small, sums, fc2b, hidden_sums, sils,
        ada_weight, order, [as_lines(qkvg), as_lines(projg)], chunks,
    )
    ada_bgrad = lax.dynamic_slice(ada_bsum[0], (me * ada_bias.shape[0],), ada_bias.shape)
    (cond_grad,) = silu_back(cond[:, 0, :own].reshape(model))
    return (
        out[None], xg[None], cond_grad[None], ada_wgrad, ada_bgrad,
        small[:9, :own], small[9, :own], qkvg, projg, small[10, :own], fc1g, small[26, :own_ff],
        small[16:25, :own_ff], small[25, :own_ff], fc2g, small[11, :own],
    )


def solution(mesh):
    wide, narrow = mesh.shape["wide"], mesh.shape["narrow"]
    rows = lambda rank: P(AXES, *(None,) * (rank - 1))
    lanes = P(None, AXES)
    in_specs = (
        rows(3), rows(2), rows(2), rows(2), rows(1), lanes, rows(1), rows(2), rows(2), rows(1),
        rows(2), rows(1), lanes, rows(1), rows(2), rows(1), rows(3),
    )
    out_specs = (
        rows(3), rows(3), rows(2), rows(2), rows(1), lanes, rows(1), rows(2), rows(2), rows(1),
        rows(2), rows(1), lanes, rows(1), rows(2), rows(1),
    )
    return jax.shard_map(
        functools.partial(on_device, wide, narrow), mesh=mesh, in_specs=in_specs,
        out_specs=out_specs, check_vma=False,
    )
```

time: 524 us -> 390 us (0.74)
  Pallas kernels: 486 us -> 357 us
    pallas_call x7 -> x4, Pallas kernels: 407 us -> 278 us  [the longest x1 77.8 us: back(): pl.pallas_call(functools.partial(back_kernel, wide, narrow, chunks, count...]
where the time goes in v2:
time: 390 us; the launch traced here: 389 us
  Pallas kernels  357 us (92%)
  local copies, waits for them, and re-layouts  27.1 us (7%)
  other arithmetic  4.08 us (1%)
    pallas_call x1, Pallas kernels, feed_forward(): pl.pallas_call(ff_kernel, grid=(hidden // width,), in_specs=[once((tokens...  79.6 us
    pallas_call x1, Pallas kernels, back(): pl.pallas_call(functools.partial(back_kernel, wide, narrow, chunks, count...  77.8 us
    pallas_call x1, Pallas kernels, attend(): pl.pallas_call(functools.partial(attend_kernel, wide, narrow, chunks, cou...  72.3 us
    pallas_call x1, Pallas kernels, tail(): pl.pallas_call(functools.partial(tail_kernel, wide, narrow, chunks, count...  69.5 us
    pallas_call x1, Pallas kernels, front(): pl.pallas_call(functools.partial(front_kernel, wide, narrow, chunks, coun...  58.1 us

profile of v2, /device:TPU:0, one launch (start us, length us, event | category | flops | bytes accessed | tf_op | source)
XLA Modules:
  0.0 389.2 jit_solution(9240875103172036422)
XLA Ops:
  0.7 0.7 pad.34
  1.3 0.7 pad.35
  2.0 0.7 pad.39
  2.6 0.7 pad.38
  3.3 0.7 pad.36
  4.0 0.7 broadcast_in_dim.58
  4.6 0.7 convert_reduce_fusion
  5.3 0.7 pad.33
  6.0 0.7 pad.37
  6.7 3.8 concatenate.3.refs_7_
  10.5 0.7 convert_reduce_fusion.1
  11.2 0.1 reshape.185
  11.3 0.6 pad_convert_fusion.refs_4_
  12.0 0.2 dynamic_update_slice.3.refs_6_
  12.2 0.0 copy-start.5
  12.2 0.8 fusion.refs_3_.refs_12_
  12.9 0.9 broadcast_in_dim.45.refs_2_
  13.8 0.0 copy-done.5
  13.8 58.1 %front.1 = (f32[8,768]{1,0:T(8,128)}, f32[32,128]{1,0:T(8,128)}, f32[16,768]{1,0:T(8,128)}, f32[16,3072]{1,0:T(8,128)}, bf16[1024,768]{1,0:T(8,128)(2,1)}, /*ind...) custom-call(bf16[1024,768]{1,0:T(8,128)(2,1)} %bitcast.43, ...), custom_call_target="tpu_custom_call" | custom-call | tf_op jit(solution)/shard_map/front/pallas_call | solution.py:716
  71.9 72.3 %attend.1 = (bf16[1024,2304]{1,0:T(8,128)(2,1)}, bf16[48,256,256]{2,1,0:T(8,128)(2,1)}, bf16[1024,768]{1,0:T(8,128)(2,1)}, f32[1024,768]{1,0:T(8,128)}, f32[1024...) custom-call(bf16[1024,768]{1,0:T(8,128)(2,1)} %get-tuple-element.59., ...), custom_call_target="tpu_custom_call" | custom-call | tf_op jit(solution)/shard_map/attend/pallas_call | solution.py:805
  144.2 2.6 copy.39
  146.8 79.6 %feed_forward.1 = (f32[1024,768]{1,0:T(8,128)}, f32[1024,768]{1,0:T(8,128)}, bf16[768,3072]{1,0:T(8,128)(2,1)}, bf16[3072,768]{1,0:T(8,128)(2,1)}, f32[16,3072]{1,0:T(8,128)}) custom-call(bf16[1024,768]{1,0:T(8,128)(2,1)} %get-tuple-element.65.n2_ref, bf16[768,1024]{1,0:T(8,128)(2,1)} %bitcast.35, bf16[1024,768]{1,0:T(8,128)(2,1)} %get-tuple-element.66.g2_ref, ...), custom_call_target="tpu_custom_call" | custom-call | tf_op jit(solution)/shard_map/feed_forward/pallas_call | solution.py:240
  226.4 77.8 %attend_back.1 = (bf16[1024,768]{1,0:T(8,128)(2,1)}, f32[1024,768]{1,0:T(8,128)}, f32[6,4,36,8,128]{4,3,2,1,0:T(8,128)}, f32[5,8,768]{2,1,0:T(8,128)}, bf16[768,...) custom-call(f32[1024,768]{1,0:T(8,128)} %get-tuple-element.70.refs_0_, ...), custom_call_target="tpu_custom_call" | custom-call | tf_op jit(solution)/shard_map/attend_back/pallas_call | solution.py:923
  304.2 0.0 copy-start.7
  304.2 69.5 %tail.1 = (bf16[1024,768]{1,0:T(8,128)(2,1)}, bf16[1024,768]{1,0:T(8,128)(2,1)}, f32[24,4608]{1,0:T(8,128)}, f32[1,4608]{1,0:T(1,128)}, f32[32,1,128]{2,1,0:T(1,...) custom-call(bf16[1024,768]{1,0:T(8,128)(2,1)} %get-tuple-element.58.refs_1_.refs_0_, ...), custom_call_target="tpu_custom_call" | custom-call | tf_op jit(solution)/shard_map/tail/pallas_call | solution.py:1069
  373.7 1.3 constant_dynamic-slice_fusion
  375.0 1.3 slice_bitcast_fusion.1
  376.3 1.3 slice_bitcast_fusion
  377.6 1.3 slice.29
  378.9 1.3 slice.25
  380.2 0.8 slice_reduce_fusion
  380.9 0.1 reshape_squeeze.3
  381.0 0.0 copy-done.7
  381.0 0.6 fusion.3
  381.6 2.8 copy.51
  384.4 0.0 copy-done
  384.4 0.0 copy-start.3
  384.4 1.1 copy.52
  385.6 0.1 copy-done.1
  385.7 0.8 copy.53
  386.4 0.0 copy-done.4
  386.4 0.7 copy.54
  387.1 0.0 copy-done.6
  387.1 0.6 copy.55
  387.8 0.0 copy-done.3
  387.8 0.7 copy.56
  388.5 0.0 copy-done.2
  388.5 0.7 copy.57
  (11 shorter events, 0.1 us)
Async XLA Ops:
  12.2 1.7 copy-start.5
  304.2 76.9 %copy-start.7 = (bf16[1,768]{1,0:T(2,128)(2,1)S(1)}, bf16[1,768]{1,0:T(2,128)(2,1)}, u32[]{:S(2)}) copy-start(bf16[1,768]{1,0:T(2,128)(2,1)} %param.18) | copy-start | bytes 4612
  381.6 2.8 copy-start
  384.4 1.3 copy-start.1
  384.4 2.0 copy-start.4
  384.4 2.7 copy-start.6
  384.4 3.3 copy-start.3
  385.7 2.8 copy-start.2

commit v3 on v2

v3 whole, which is shorter than its diff:
```python
import functools

import jax
import jax.numpy as jnp
from jax import lax
from jax.experimental import pallas as pl
from jax.experimental.pallas import tpu as pltpu
from jax.sharding import PartitionSpec as P

HEAD = 64
GRID = 32
HALF = 16
GROUP = 256
TOKENS = 1024
C0 = 0.7978845608028654
C1 = 0.044715
EPS = 1e-06
MIB = 1 << 20
AXES = ("wide", "narrow")
F32, BF16 = jnp.float32, jnp.bfloat16


def dot_nn(a, b):
    return lax.dot_general(a, b, (((1,), (0,)), ((), ())), preferred_element_type=F32)


def dot_nt(a, b):
    return lax.dot_general(a, b, (((1,), (1,)), ((), ())), preferred_element_type=F32)


def dot_tn(a, b):
    return lax.dot_general(a, b, (((0,), (0,)), ((), ())), preferred_element_type=F32)


def whole(shape):
    return pl.BlockSpec(shape, lambda *_: (0,) * len(shape))


def once(shape):
    return pl.BlockSpec(shape, lambda *_: (0,) * len(shape), pipeline_mode=pl.Buffered(1))


def like(shape, dtype):
    return jax.ShapeDtypeStruct(shape, dtype)


def shift_pair(pair, parity, first, last):
    low, high = pair
    zero = jnp.zeros_like(low)
    if parity == 0:
        low, high = pltpu.roll(low, 1, 0), pltpu.roll(high, 1, 0)
        return jnp.where(first, zero, low), jnp.where(first, low, high)
    low, high = pltpu.roll(low, 7, 0), pltpu.roll(high, 7, 0)
    return jnp.where(last, high, low), jnp.where(last, zero, high)


def row_sources(gi, r):
    if gi == 0:
        return ((1, r - 1), (0, r), (1, r))
    return ((0, r), (1, r), (0, r + 1))


def load_pair(ref, slab, gi, gj, r):
    tile = 2 + 2 * r
    group = 2 * gi + gj
    return ref[slab, group, tile], ref[slab, group, tile + 1]


def store_pair(ref, slab, gi, gj, r, pair):
    tile = 2 + 2 * r
    group = 2 * gi + gj
    ref[slab, group, tile] = pair[0]
    ref[slab, group, tile + 1] = pair[1]


def edge_masks():
    sub = lax.broadcasted_iota(jnp.int32, (8, 128), 0)
    return sub == 0, sub == 7


def clear_edges(ref):
    slabs = ref.shape[0]
    ref[:, :, 0:2] = jnp.zeros((slabs, 4, 2, 8, 128), F32)
    ref[:, :, 34:36] = jnp.zeros((slabs, 4, 2, 8, 128), F32)


def conv_cell(src, slab, gi, gj, r, k, bias, masks):
    sources = row_sources(gi, r)
    other = 1 - gj
    near = 2 if gj == 0 else 0
    far = 2 - near
    same = [load_pair(src, slab, p, gj, rr) for p, rr in sources]
    cross = [load_pair(src, slab, p, other, rr) for p, rr in sources]
    straight, moved = [], []
    for h in (0, 1):
        acc, off = bias, None
        for a in range(3):
            acc = acc + k[3 * a + 1] * same[a][h] + k[3 * a + near] * cross[a][h]
            term = k[3 * a + far] * cross[a][h]
            off = term if off is None else off + term
        straight.append(acc)
        moved.append(off)
    moved = shift_pair(moved, gj, *masks)
    return straight[0] + moved[0], straight[1] + moved[1]


def conv_back_row(slab, k, src, grad, grad_moved, put, r, carry):
    kg, total = list(carry[:9]), carry[9]
    for gi in (0, 1):
        sources = row_sources(gi, r)
        for gj in (0, 1):
            other = 1 - gj
            near = 2 if gj == 0 else 0
            here = load_pair(src, slab, gi, gj, r)
            out = [None, None]
            for a in range(3):
                p, rr = sources[2 - a]
                trio = {
                    1: load_pair(grad, slab, p, gj, rr),
                    2 - near: load_pair(grad, slab, p, other, rr),
                    near: load_pair(grad_moved, slab, p, other, rr),
                }
                for b in range(3):
                    n = 3 * a + b
                    for h in (0, 1):
                        term = k[n] * trio[b][h]
                        out[h] = term if out[h] is None else out[h] + term
                        kg[n] = kg[n] + here[h] * trio[b][h]
            total = total + out[0] + out[1]
            put(gi, gj, r, out)
    return tuple(kg) + (total,)


def conv_back(slab, k, src, grad, grad_moved, put):
    body = lambda r, carry: conv_back_row(slab, k, src, grad, grad_moved, put, r, carry)
    return lax.fori_loop(0, HALF, body, (jnp.zeros((8, 128), F32),) * 10)


def group_rows(gi, gj, r):
    return pl.ds(pl.multiple_of((2 * gi + gj) * GROUP + r * HALF, HALF), HALF)


def row_sum(values):
    rows, columns = values.shape
    return jnp.sum(values.reshape(rows // 8, 8, columns), axis=0)


def unit_rows(values):
    model = values.shape[-1]
    centered = values - jnp.sum(values, axis=-1, keepdims=True) * (1.0 / model)
    spread = jnp.sum(centered * centered, axis=-1, keepdims=True) * (1.0 / model)
    scale = lax.rsqrt(spread + EPS)
    return centered * scale, scale


def unit_back(grad, unit, scale):
    model = grad.shape[-1]
    mean = jnp.sum(grad, axis=-1, keepdims=True) * (1.0 / model)
    tilt = jnp.sum(grad * unit, axis=-1, keepdims=True) * (1.0 / model)
    return scale * (grad - mean - unit * tilt)


def order_matrix():
    d = jnp.arange(GROUP)
    group, position, column = d // 64, (d % 64) // HALF, d % HALF
    source = (2 * position + group // 2) * GRID + 2 * column + group % 2
    return (source[:, None] == jnp.arange(GROUP)[None, :]).astype(BF16)


def ff_kernel(wide, narrow, chunks, count, steps, sums_over, *refs):
    n2_ref, n2t_ref, g2_ref, fc1_ref, small_ref, fc2_ref = refs[:6]
    srcs = refs[6 : 6 + count]
    branch_ref, gn2_ref, w1g_ref, w2g_ref, sums_ref = refs[6 + count : 11 + count]
    dsts = refs[11 + count : 11 + 2 * count]
    hid, ga, gc, gcs, act, ghl = refs[11 + 2 * count : 17 + 2 * count]
    step = pl.program_id(0)
    slabs = hid.shape[0]
    p = Place(wide, narrow)
    if sums_over:
        buffers, (sends, recvs) = refs[17 + 2 * count : -2], refs[-2:]
        waves = scatter_jobs(p, srcs, dsts, buffers, sends, recvs, chunks)
        own_copies = []
    else:
        sends, recvs, local = refs[17 + 2 * count :]
        waves = gather_jobs(p, srcs, dsts, sends, recvs, chunks)
        own_copies = [
            pltpu.make_async_copy(
                srcs[i], dsts[i].at[(*digits_of(p.w, wide), p.n)], local.at[i]
            )
            for i in range(count)
        ]

    def hook(position):
        for when in range(steps):
            pl.when(step == when)(lambda: waves.at_hook(3 * when + position, 3 * steps))

    @pl.when(step == 0)
    def _():
        for copy in own_copies:
            copy.start()
        greet(p.partners())
        waves.run(0)
        for copy in own_copies:
            copy.wait()
        branch_ref[...] = jnp.zeros_like(branch_ref)
        gn2_ref[...] = jnp.zeros_like(gn2_ref)
        for ref in (hid, gc, gcs):
            clear_edges(ref)

    for g in range(4):
        rows = pl.ds(g * GROUP, GROUP)
        full = dot_nn(n2_ref[rows, :], fc1_ref[...]) + small_ref[10:11, :]
        back = dot_nt(g2_ref[rows, :], fc2_ref[...])
        for slab in range(slabs):
            lanes = slice(slab * 128, slab * 128 + 128)
            hid[slab, g, 2:34] = full[:, lanes].reshape(32, 8, 128)
            ga[slab, g] = back[:, lanes].reshape(32, 8, 128)

    hook(0)
    masks = edge_masks()
    for slab in range(slabs):
        lanes = pl.ds(slab * 128, 128)
        k = [jnp.broadcast_to(small_ref[n : n + 1, lanes], (8, 128)) for n in range(9)]
        bias = jnp.broadcast_to(small_ref[9:10, lanes], (8, 128))

        def forward(r, total):
            for gi in (0, 1):
                for gj in (0, 1):
                    pair = conv_cell(hid, slab, gi, gj, r, k, bias, masks)
                    acts, grads = [], []
                    for h in (0, 1):
                        x = pair[h]
                        x2 = x * x
                        half = 0.5 * jnp.tanh(x * (C0 + (C0 * C1) * x2)) + 0.5
                        value = x * half
                        slope = half + (value - value * half) * (2.0 * C0 + (6.0 * C0 * C1) * x2)
                        acts.append(value)
                        grads.append(ga[slab, 2 * gi + gj, 2 * r + h] * slope)
                        total = total + grads[-1]
                    act[group_rows(gi, gj, r), lanes] = jnp.concatenate(acts, 0).astype(BF16)
                    store_pair(gc, slab, gi, gj, r, grads)
                    store_pair(gcs, slab, gi, gj, r, shift_pair(grads, 1 - gj, *masks))
            return total

        total = lax.fori_loop(0, HALF, forward, jnp.zeros((8, 128), F32))

        def put(gi, gj, r, pair):
            ghl[group_rows(gi, gj, r), lanes] = jnp.concatenate(pair, 0).astype(BF16)

        sums = conv_back(slab, k, hid, gc, gcs, put)
        for n, value in enumerate([*sums[:9], total, sums[9]]):
            sums_ref[n : n + 1, lanes] = jnp.sum(value, axis=0, keepdims=True)
        sums_ref[11:16, lanes] = jnp.zeros((5, 128), F32)
        if slab == 0:
            hook(1)

    branch_ref[...] += dot_nn(act[...], fc2_ref[...])
    gn2_ref[...] += dot_nt(ghl[...], fc1_ref[...])
    w2g_ref[...] = dot_tn(act[...], g2_ref[...]).astype(w2g_ref.dtype)
    w1g_ref[...] = dot_nn(n2t_ref[...], ghl[...]).astype(w1g_ref.dtype)
    hook(2)

    @pl.when(step == steps - 1)
    def _():
        waves.finish()


def feed_forward(wide, narrow, n2, n2t, g2, fc1, small, part, fc2, arrays, chunks, sums_over,
                 width=256):
    tokens, model = n2.shape
    hidden = fc1.shape[1]
    slabs, steps, count = width // 128, hidden // width, len(arrays)
    padded = pltpu.VMEM((slabs, 4, 36, 8, 128), F32)
    columns = lambda rows: pl.BlockSpec((rows, width), lambda s: (0, s))
    lines = pl.BlockSpec((width, model), lambda s: (s, 0))
    anywhere = pl.BlockSpec(memory_space=pl.ANY)
    if sums_over:
        shapes = [a.shape for a in arrays]
        moved = [owned_shape(s, narrow) for s in shapes]
        extra = scatter_scratch(wide, narrow, shapes) + job_sems(wide, narrow, chunks)
        in_moved, out_moved = [once(s) for s in shapes], [once(m.shape) for m in moved]
    else:
        moved = [gathered_shape(wide, narrow, a.shape) for a in arrays]
        extra = job_sems(wide, narrow, chunks) + [pltpu.SemaphoreType.DMA((count,))]
        in_moved = out_moved = [anywhere] * count
    return pl.pallas_call(
        functools.partial(ff_kernel, wide, narrow, chunks, count, steps, sums_over),
        grid=(steps,),
        in_specs=[
            once((tokens, model)), once((model, tokens)), once((tokens, model)),
            columns(model), pl.BlockSpec((16, width), lambda s: (0, part * steps + s)), lines,
        ] + in_moved,
        out_specs=[
            once((tokens, model)), once((tokens, model)), columns(model), lines, columns(16)
        ] + out_moved,
        out_shape=[
            like((tokens, model), F32), like((tokens, model), F32),
            like((model, hidden), BF16), like((hidden, model), BF16), like((16, hidden), F32),
        ] + moved,
        scratch_shapes=[
            padded, pltpu.VMEM((slabs, 4, 32, 8, 128), F32), padded, padded,
            pltpu.VMEM((tokens, width), BF16), pltpu.VMEM((tokens, width), BF16),
        ] + extra,
        compiler_params=pltpu.CompilerParams(
            vmem_limit_bytes=56 * MIB, collective_id=4 if sums_over else 3, has_side_effects=True
        ),
        name="feed_forward",
    )(n2, n2t, g2, fc1, small, fc2, *arrays)


def flip(index, bit):
    return index + bit - 2 * bit * lax.rem(index // bit, 2)


def bits_of(count):
    return [1 << b for b in range(count.bit_length() - 1)]


def digits_of(index, wide):
    levels = wide.bit_length() - 1
    return [lax.rem(index // (1 << (levels - 1 - i)), 2) for i in range(levels)]


def static_digits(index, wide):
    levels = wide.bit_length() - 1
    return [(index >> (levels - 1 - i)) & 1 for i in range(levels)]


def at(w, n):
    return {"wide": w, "narrow": n}


def greet(places):
    barrier = pltpu.get_barrier_semaphore()
    for place in places:
        pl.semaphore_signal(barrier, inc=1, device_id=place, device_id_type=pl.DeviceIdType.MESH)
    pl.semaphore_wait(barrier, len(places))


def greet_all(place):
    barrier = pltpu.get_barrier_semaphore()
    total = place.total

    def body(k, carry):
        pl.semaphore_signal(
            barrier, inc=1, device_id=place.device(lax.rem(place.sid + k, total)),
            device_id_type=pl.DeviceIdType.MESH,
        )
        return carry

    lax.fori_loop(1, total, body, 0)
    pl.semaphore_wait(barrier, total - 1)


def remote(src, dst, send_sem, recv_sem, place):
    return pltpu.make_async_remote_copy(
        src_ref=src, dst_ref=dst, send_sem=send_sem, recv_sem=recv_sem, device_id=place,
        device_id_type=pl.DeviceIdType.MESH,
    )


class Place:
    def __init__(self, wide, narrow):
        self.wide, self.narrow = wide, narrow
        self.w, self.n = lax.axis_index("wide"), lax.axis_index("narrow")
        self.total, self.half = wide * narrow, wide * narrow // 2
        self.me = self.w * narrow + self.n
        self.core = lax.rem(self.w, 2)
        self.slot = (self.w // 2) * narrow + self.n
        self.sid = self.core * self.half + self.slot
        self.sibling = at(flip(self.w, 1), self.n)

    def device(self, sid):
        core, slot = sid // self.half, lax.rem(sid, self.half)
        return at(2 * (slot // self.narrow) + core, lax.rem(slot, self.narrow))

    def order_of(self, sid):
        core, slot = divmod(sid, self.half)
        return (2 * (slot // self.narrow) + core) * self.narrow + slot % self.narrow

    def partners(self):
        places = [at(self.w, lax.rem(self.n + k, self.narrow)) for k in range(1, self.narrow)]
        return places + [at(flip(self.w, bit), self.n) for bit in bits_of(self.wide)]

    def all_copies(self, src_of, dst, sends, recvs):
        def copy(k):
            sid = lax.rem(self.sid + k, self.total)
            return remote(src_of(sid), dst, sends.at[k], recvs.at[k], self.device(sid))

        return Exchange(copy, self.total)

    def kin_copies(self, src_of, dst, sends, recvs):
        def copy(k):
            slot = lax.rem(self.slot + k, self.half)
            return remote(src_of(slot), dst, sends.at[k], recvs.at[k],
                          self.device(self.core * self.half + slot))

        return Exchange(copy, self.half)

    def to_all(self, *refs):
        return self.all_copies(*refs).start()

    def to_kin(self, *refs):
        return self.kin_copies(*refs).start()

    def to_all_wait(self, *refs):
        self.all_copies(*refs).wait()

    def to_kin_wait(self, *refs):
        self.kin_copies(*refs).wait()


class Exchange:
    def __init__(self, copy, count):
        self.copy, self.count = copy, count

    def start(self):
        def body(k, carry):
            self.copy(k).start()
            return carry

        lax.fori_loop(1, self.count, body, 0)
        return self.wait

    def wait(self):
        def body(k, carry):
            self.copy(k).wait()
            return carry

        lax.fori_loop(1, self.count, body, 0)


def bit_sizes(wide):
    return (2,) * (wide.bit_length() - 1)


class Transfer:
    def __init__(self, place, sends, recvs, chunk, columns):
        self.p, self.sends, self.recvs, self.chunk = place, sends, recvs, chunk
        start, size = columns
        self.all = pl.ds(start, size)
        levels = len(bit_sizes(place.wide))
        far = list(range(levels - 1))
        if size % 256:
            self.parts = [(self.all, far)]
        else:
            self.parts = [(pl.ds(start, size // 2), far), (pl.ds(start + size // 2, size // 2), far[::-1])]
        self.stages = levels + 1
        self.bits = digits_of(place.w, place.wide)
        self.count = 0

    def copy(self, src, dst, place):
        slot = self.count
        self.count += 1
        return remote(src, dst, self.sends.at[self.chunk, slot], self.recvs.at[self.chunk, slot], place)

    def along(self, level):
        return at(flip(self.p.w, 1 << (len(self.bits) - 1 - level)), self.p.n)

    def in_line(self, k):
        return at(self.p.w, lax.rem(self.p.n + k, self.p.narrow))

    def copies(self, stage):
        self.count = 0
        for before in range(stage):
            self.count += len(self.make(before, True))
        return self.make(stage, False)

    def start(self, stage):
        for copy in self.copies(stage):
            copy.start()

    def finish(self):
        pass


class Gather(Transfer):
    def __init__(self, place, src, dst, sends, recvs, chunk, columns):
        super().__init__(place, sends, recvs, chunk, columns)
        self.src, self.dst = src, dst

    def make(self, stage, count_only):
        levels = len(self.bits)
        if stage == 0:
            ks = range(1, self.p.narrow)
            if count_only:
                return list(ks)
            return [
                self.copy(self.src.at[:, self.all],
                          self.dst.at[(*self.bits, self.p.n, slice(None), self.all)], self.in_line(k))
                for k in ks
            ]
        if stage == levels:
            parts = [(self.all, list(range(levels)))]
        else:
            parts = self.parts
        if count_only:
            return list(parts)
        found = []
        for columns, order in parts:
            index = list(self.bits)
            for level in order[: stage - 1]:
                index[level] = slice(None)
            part = self.dst.at[(*index, slice(None), slice(None), columns)]
            found.append(self.copy(part, part, self.along(order[stage - 1])))
        return found

    def wait(self, stage):
        for copy in self.copies(stage):
            copy.wait_recv()

    def finish(self):
        for stage in range(self.stages):
            for copy in self.copies(stage):
                copy.wait_send()


class Waves:
    def __init__(self, chunks, lag=2):
        self.chunks, self.wave, self.lag = chunks, 0, lag
        self.stages = chunks[0][0].stages
        self.count = len(chunks) + lag * self.stages

    def run(self, wave):
        for c, jobs in enumerate(self.chunks):
            stage, rest = divmod(wave - c, self.lag)
            if rest:
                continue
            for job in jobs:
                if 1 <= stage <= self.stages:
                    job.wait(stage - 1)
                if 0 <= stage < self.stages:
                    job.start(stage)

    def tick(self, times=1):
        for _ in range(times):
            if self.wave < self.count:
                self.run(self.wave)
                self.wave += 1

    def through(self, chunk):
        while self.wave <= chunk + self.lag * self.stages:
            self.tick()

    def at_hook(self, hook, hooks):
        left = self.count - 1
        for wave in range(1 + hook * left // hooks, 1 + (hook + 1) * left // hooks):
            self.run(wave)

    def finish(self):
        for jobs in self.chunks:
            for job in jobs:
                job.finish()

    def end(self):
        self.tick(self.count)
        self.finish()


def job_sems(wide, narrow, chunks):
    per = narrow - 1 + 2 * (wide.bit_length() - 1)
    return [pltpu.SemaphoreType.DMA((len(chunks), per))] * 2


def gather_jobs(place, srcs, dsts, sends, recvs, chunks, lag=2):
    return Waves([
        [Gather(place, srcs[i], dsts[i], sends, recvs, c, columns)]
        for c, (i, *columns) in enumerate(chunks)
    ], lag)


def gathered_shape(wide, narrow, shape):
    return like((*bit_sizes(wide), narrow, *shape), BF16)


def thirds(i, size):
    return [(i, t * (size // 3), size // 3) for t in range(3)]


class Scatter(Transfer):
    def __init__(self, place, src, buffers, out, sends, recvs, chunk, columns):
        super().__init__(place, sends, recvs, chunk, columns)
        self.src, self.out = src, out
        self.halves, self.line, self.got = buffers[:-2], buffers[-2], buffers[-1]
        self.rows = self.line.shape[1]
        core = len(self.bits) - 1
        self.parts = [(columns, [core] + order) for columns, order in self.parts]

    def make(self, stage, count_only):
        levels = len(self.bits)
        if stage == levels:
            ks = range(1, self.p.narrow)
            if count_only:
                return list(ks)
            return [
                self.copy(self.line.at[lax.rem(self.p.n + k, self.p.narrow), :, self.all],
                          self.got.at[k - 1, :, self.all], self.in_line(k))
                for k in ks
            ]
        parts = self.parts if stage else [(self.all, self.parts[0][1])]
        if count_only:
            return list(parts)
        found = []
        for columns, order in parts:
            source, index, kept = self.level(order, stage, True)
            into = self.halves[stage].at[(*kept, slice(None), columns)]
            found.append(self.copy(source.at[(*index, slice(None), columns)], into, self.along(order[stage])))
        return found

    def level(self, order, stage, theirs):
        source = self.src if stage == 0 else self.halves[stage - 1]
        left = [level for level in range(len(self.bits)) if level not in order[:stage]]
        bit = self.bits[order[stage]]
        bit = 1 - bit if theirs else bit
        index = [bit if level == order[stage] else slice(None) for level in left]
        return source, index, [slice(None)] * (len(left) - 1)

    def wait(self, stage):
        for copy in self.copies(stage):
            copy.wait()
        levels = len(self.bits)
        if stage == levels:
            value = self.line[self.p.n, :, self.all].astype(F32)
            for k in range(1, self.p.narrow):
                value = value + self.got[k - 1, :, self.all].astype(F32)
            self.out[:, self.all] = value
            return
        for columns, order in self.parts:
            source, index, kept = self.level(order, stage, False)
            into = self.halves[stage]
            for j in range(1 << len(kept)):
                digits = [(j >> i) & 1 for i in range(len(kept))]
                mine = [v if not isinstance(v, slice) else None for v in index]
                rest = iter(digits)
                mine = [next(rest) if v is None else v for v in mine]
                self.add(source, tuple(mine), into, tuple(digits), columns, stage == levels - 1)

    def add(self, source, mine, into, arrived, columns, last):
        if last:
            total = source[(*mine, slice(None), columns)].astype(F32) + into[
                (*arrived, slice(None), columns)
            ].astype(F32)
            for m in range(self.p.narrow):
                rows = slice(m * self.rows, (m + 1) * self.rows)
                self.line[m, :, columns] = total[rows].astype(BF16)
            return

        def body(i, carry):
            rows = pl.ds(pl.multiple_of(i * 16, 16), 16)
            into[(*arrived, rows, columns)] = (
                source[(*mine, rows, columns)].astype(F32) + into[(*arrived, rows, columns)].astype(F32)
            ).astype(BF16)
            return carry

        lax.fori_loop(0, into.shape[-2] // 16, body, 0)


def scatter_scratch(wide, narrow, shapes):
    scratch = []
    for *_, height, columns in shapes:
        for stage in range(wide.bit_length() - 1):
            scratch.append(pltpu.VMEM((*bit_sizes(wide)[stage + 1 :], height, columns), BF16))
        scratch.append(pltpu.VMEM((narrow, height // narrow, columns), BF16))
        scratch.append(pltpu.VMEM((narrow - 1, height // narrow, columns), BF16))
    return scratch


def scatter_jobs(place, srcs, outs, buffers, sends, recvs, chunks, lag=2):
    per = len(buffers) // len(srcs)
    return Waves([
        [Scatter(place, srcs[i], buffers[i * per : (i + 1) * per], outs[i], sends, recvs, c, columns)]
        for c, (i, *columns) in enumerate(chunks)
    ], lag)


def owned_shape(shape, narrow):
    return like((shape[-2] // narrow, shape[-1]), F32)


def move_lanes(tiles, moves, count):
    rows = tiles[0].shape[0]
    lane = lax.broadcasted_iota(jnp.int32, (rows, 128), 1)
    out = [jnp.zeros((rows, 128), F32) for _ in range(count)]
    for start, to, length in moves:
        while length:
            size = min(length, 128 - start % 128, 128 - to % 128)
            tile = tiles[start // 128]
            turn = (to - start) % 128
            if turn:
                tile = pltpu.roll(tile, turn, 1)
            inside = (lane >= to % 128) & (lane < to % 128 + size)
            out[to // 128] = jnp.where(inside, tile, out[to // 128])
            start, to, length = start + size, to + size, length - size
    return out


def tiles_of(values):
    return [values[:, i : i + 128] for i in range(0, values.shape[1], 128)]


def front_kernel(wide, narrow, chunks, count, own, own_ff, *refs):
    (x_ref, cot_ref, mask_ref, order_ref, cond_ref, ada_ref, bias_ref, small_ref, fc1_ref) = refs[:9]
    srcs = refs[9 : 9 + count]
    (mod_ref, sils_ref, model_ref, hidden_ref, lat_ref, gout_ref, g2_ref, normed_ref, mixed_ref,
     keep_ref, fc2b_ref, fc1b_ref) = refs[9 + count : 21 + count]
    dsts = refs[21 + count : 22 + 2 * count]
    (fc1a_ref, sil_out, got, part, sib, rows_in, smalls, send_a, recv_a, send_b, recv_b, send_c, recv_c,
     sends, recvs, local) = refs[22 + 2 * count :]
    p = Place(wide, narrow)
    mine = digits_of(p.w, wide)
    model = x_ref.shape[1]
    slabs = model // 128
    own_copies = [
        pltpu.make_async_copy(srcs[i], dsts[1 + i].at[(*mine, p.n)], local.at[i]) for i in range(count)
    ]
    for copy in own_copies:
        copy.start()
    waves = gather_jobs(p, [small_ref, fc1a_ref, *srcs], [smalls, *dsts], sends, recvs, chunks)
    cond = cond_ref[...].astype(F32)
    sil = (cond * jax.nn.sigmoid(cond)).astype(BF16).astype(F32)
    tiles = tiles_of(sil)
    for sid in range(p.total):
        d = p.order_of(sid)
        sil_out[sid] = move_lanes(tiles, [(own * d, 0, own)], 1)[0]
    greet_all(p)
    waves.tick(2)
    got[p.sid] = sil_out[p.sid]
    wait_sil = p.to_all(lambda sid: sil_out.at[sid], got.at[p.sid], send_a, recv_a)

    def arrange(t):
        rows = pl.ds(t * GROUP, GROUP)
        tokens = dot_nn(order_ref[...], x_ref[rows, :])
        unit, _ = unit_rows(tokens)
        kept = dot_nn(order_ref[...], mask_ref[rows, :])
        gout = dot_nn(order_ref[...], cot_ref[rows, :]) * jnp.concatenate([kept] * slabs, axis=1)
        for g in range(4):
            src = slice(64 * g, 64 * g + 64)
            dst = pl.ds(g * GROUP + 64 * t, 64)
            lat_ref[dst, :] = tokens[src].astype(BF16)
            gout_ref[dst, :] = gout[src].astype(BF16)
            keep_ref[dst, :] = (kept[src] - 1.0) * 1e30
            for s in range(slabs):
                tile = unit[src, s * 128 : s * 128 + 128].reshape(8, 8, 128)
                normed_ref[s, g, 2 + 8 * t : 10 + 8 * t] = tile

    arrange(0)
    wait_sil()
    sil = got[...].reshape(p.total, 128)
    sils_ref[...] = sil
    product = dot_nn(sil[:, :own].astype(BF16), ada_ref[...]) + bias_ref[...]
    for d in range(p.total):
        part[d // p.half, d % p.half] = product[d : d + 1, :]
    to_sibling = remote(part.at[1 - p.core], sib, send_b, recv_b, p.sibling)
    to_sibling.start()
    for copy in own_copies:
        copy.wait()
    smalls[(*mine, p.n)] = small_ref[...]
    waves.tick()
    arrange(1)
    to_sibling.wait()
    part[p.core] = part[p.core] + sib[...]
    rows_in[p.slot] = part[p.core, p.slot]
    wait_rows = p.to_kin(lambda slot: part.at[p.core, slot], rows_in.at[p.slot], send_c, recv_c)
    waves.tick()
    arrange(2)
    columns = tiles_of(fc1_ref[...].astype(F32))
    for h, ref in enumerate((fc1a_ref, fc1b_ref)):
        moves = [
            (own_ff * d + own_ff // 2 * h, own_ff // 2 * d, own_ff // 2) for d in range(p.total)
        ]
        ref[...] = jnp.concatenate(move_lanes(columns, moves, len(columns) // 2), axis=1).astype(BF16)
    own_fc1 = pltpu.make_async_copy(fc1a_ref, dsts[0].at[(*mine, p.n)], local.at[count])
    own_fc1.start()
    waves.tick()
    arrange(3)
    clear_edges(normed_ref)
    waves.tick()
    wait_rows()
    mod = jnp.sum(rows_in[...], axis=0)
    for i in range(6):
        mod_ref[i : i + 1, :] = mod[:, i * model : (i + 1) * model]
    own_fc1.wait()
    waves.through(0)
    pieces = [smalls[(*static_digits(d // narrow, wide), d % narrow)].astype(F32) for d in range(p.total)]
    moves = [(128 * d, own * d, own) for d in range(p.total)]
    model_ref[...] = jnp.concatenate(move_lanes([q[:16] for q in pieces], moves, slabs), axis=1)
    half, hidden = own_ff // 2, fc1_ref.shape[1]
    moves = [
        (128 * d + half * h, hidden // 2 * h + half * d, half) for d in range(p.total) for h in (0, 1)
    ]
    hidden_ref[...] = jnp.concatenate(
        move_lanes([q[16:] for q in pieces], moves, hidden // 128), axis=1
    )
    waves.tick()

    shift, scale, gate = mod_ref[0:1, :], mod_ref[1:2, :], mod_ref[5:6, :]
    total = jnp.zeros((8, model), F32)
    for g in range(4):
        rows = pl.ds(g * GROUP, GROUP)
        two = gout_ref[rows, :].astype(F32) * gate
        total = total + row_sum(two)
        g2_ref[rows, :] = two.astype(BF16)
    fc2b_ref[...] = total
    masks = edge_masks()
    for s in range(slabs):
        lanes = pl.ds(s * 128, 128)
        at_s = slice(s * 128, s * 128 + 128)
        shift8 = jnp.broadcast_to(shift[:, at_s], (8, 128))
        scale8 = jnp.broadcast_to(1.0 + scale[:, at_s], (8, 128))
        normed_ref[s, :, 2:34] = normed_ref[s, :, 2:34] * scale8 + shift8
        k = [jnp.broadcast_to(model_ref[n : n + 1, at_s], (8, 128)) for n in range(9)]
        bias = jnp.broadcast_to(model_ref[9:10, at_s], (8, 128))

        def body(r, carry):
            for gi in (0, 1):
                for gj in (0, 1):
                    pair = conv_cell(normed_ref, s, gi, gj, r, k, bias, masks)
                    mixed_ref[group_rows(gi, gj, r), lanes] = jnp.concatenate(pair, 0).astype(BF16)
            return carry

        lax.fori_loop(0, HALF, body, 0)
        waves.tick()
    waves.end()


def front(wide, narrow, x, cot, mask, order, cond, ada, bias, small, fc1, blocks, chunks):
    total = wide * narrow
    tokens, model = x.shape
    slabs, count, columns = model // 128, len(blocks), ada.shape[1]
    hidden = fc1.shape[1]
    own, own_ff = model // total, hidden // total
    inside = pl.BlockSpec(memory_space=pltpu.VMEM)
    anywhere = pl.BlockSpec(memory_space=pl.ANY)
    all_sems = pltpu.SemaphoreType.DMA((total,))
    one_sem = pltpu.SemaphoreType.DMA
    kin_sems = pltpu.SemaphoreType.DMA((total // 2,))
    return pl.pallas_call(
        functools.partial(front_kernel, wide, narrow, chunks, count, own, own_ff),
        in_specs=[inside] * 9 + [anywhere] * count,
        out_specs=[inside] * 12 + [anywhere] * (count + 1),
        out_shape=[
            like((8, model), F32), like((total, 128), F32), like((16, model), F32),
            like((16, hidden), F32), like((tokens, model), BF16), like((tokens, model), BF16),
            like((tokens, model), BF16), like((slabs, 4, 36, 8, 128), F32),
            like((tokens, model), BF16), like((tokens, 128), F32), like((8, model), F32),
            like((own, hidden // 2), BF16),
            gathered_shape(wide, narrow, (own, hidden // 2)),
        ] + [gathered_shape(wide, narrow, b.shape) for b in blocks],
        scratch_shapes=[
            pltpu.VMEM((own, hidden // 2), BF16), pltpu.VMEM((total, 1, 128), F32),
            pltpu.VMEM((total, 1, 128), F32), pltpu.VMEM((2, total // 2, 1, columns), F32),
            pltpu.VMEM((total // 2, 1, columns), F32), pltpu.VMEM((total // 2, 1, columns), F32),
            pltpu.VMEM((*bit_sizes(wide), narrow, 32, 128), BF16),
            all_sems, all_sems, one_sem, one_sem, kin_sems, kin_sems,
            *job_sems(wide, narrow, chunks), pltpu.SemaphoreType.DMA((count + 1,)),
        ],
        compiler_params=pltpu.CompilerParams(
            vmem_limit_bytes=56 * MIB, collective_id=0, has_side_effects=True
        ),
        name="front",
    )(x, cot, mask, order, cond, ada, bias, small, fc1, *blocks)


def attend_kernel(wide, narrow, chunks, count, *refs):
    mixed_ref, lat_ref, keep_ref, mod_ref, small_ref, qkv_ref, proj_ref = refs[:7]
    srcs = refs[7 : 7 + count]
    (triple_ref, probs_ref, att_ref, branch_ref, middle_ref, n2_ref,
     n2t_ref) = refs[7 + count : 14 + count]
    dsts = refs[14 + count : 14 + 2 * count]
    sends, recvs, local = refs[14 + 2 * count :]
    step = pl.program_id(0)
    p = Place(wide, narrow)
    waves = gather_jobs(p, srcs, dsts, sends, recvs, chunks)
    own_copies = [
        pltpu.make_async_copy(
            srcs[i], dsts[i].at[(*digits_of(p.w, wide), p.n)], local.at[i]
        ) for i in range(count)
    ]

    def on(when, work):
        pl.when(step == when)(work)

    def first():
        for copy in own_copies:
            copy.start()
        greet(p.partners())
        waves.run(0)
        for copy in own_copies:
            copy.wait()

    def hook(position):
        for when in range(4):
            on(when, lambda: waves.at_hook(2 * when + position, 8))

    on(0, first)
    model = lat_ref.shape[1]
    slabs = model // 128
    triple_ref[...] = dot_nn(mixed_ref[...], qkv_ref[...]).astype(BF16)
    lane = lax.broadcasted_iota(jnp.int32, (GROUP, 128), 1)
    left = lane < HEAD
    keep = jnp.concatenate([keep_ref[...]] * 2, axis=1)
    for s in range(slabs):
        q = triple_ref[:, s * 128 : s * 128 + 128]
        k = triple_ref[:, model + s * 128 : model + s * 128 + 128] * jnp.asarray(0.125, BF16)
        v = triple_ref[:, 2 * model + s * 128 : 2 * model + s * 128 + 128]
        outs = []
        for h in (0, 1):
            mine = left if h == 0 else jnp.logical_not(left)
            scores = dot_nt(jnp.where(mine, k, jnp.zeros_like(k)), q) + keep
            e = jnp.exp(scores - jnp.max(scores, axis=0, keepdims=True))
            prob = (e * (1.0 / jnp.sum(e, axis=0, keepdims=True))).astype(BF16)
            probs_ref[2 * s + h, 0] = prob
            outs.append(dot_tn(prob, v))
        att_ref[:, s * 128 : s * 128 + 128] = jnp.where(left, outs[0], outs[1]).astype(BF16)
        if s == slabs // 2 - 1:
            hook(0)
    branch = dot_nn(att_ref[...], proj_ref[...]) + small_ref[10:11, :]
    middle = lat_ref[...].astype(F32) + mod_ref[2:3, :] * branch
    unit, _ = unit_rows(middle)
    branch_ref[...] = branch
    middle_ref[...] = middle
    n2 = unit * (1.0 + mod_ref[4:5, :]) + mod_ref[3:4, :]
    n2_ref[...] = n2.astype(BF16)
    n2t_ref[...] = n2.T.astype(BF16)
    hook(1)
    on(3, waves.finish)


def attend(wide, narrow, mixed, lat, keep, mod, small, qkv, proj, blocks, chunks):
    tokens, model = lat.shape
    heads, count = model // HEAD, len(blocks)
    by_group = lambda columns: pl.BlockSpec((GROUP, columns), lambda g: (g, 0))
    anywhere = pl.BlockSpec(memory_space=pl.ANY)
    return pl.pallas_call(
        functools.partial(attend_kernel, wide, narrow, chunks, count),
        grid=(4,),
        in_specs=[
            by_group(model), by_group(model), by_group(128), whole(mod.shape),
            whole(small.shape), once(qkv.shape), once(proj.shape),
        ] + [anywhere] * count,
        out_specs=[
            by_group(3 * model), pl.BlockSpec((heads, 1, GROUP, GROUP), lambda g: (0, g, 0, 0)),
            by_group(model), by_group(model), by_group(model), by_group(model),
            pl.BlockSpec((model, GROUP), lambda g: (0, g)),
        ] + [anywhere] * count,
        out_shape=[
            like((tokens, 3 * model), BF16), like((heads, 4, GROUP, GROUP), BF16),
            like((tokens, model), BF16), like((tokens, model), F32),
            like((tokens, model), F32), like((tokens, model), BF16), like((model, tokens), BF16),
        ] + [gathered_shape(wide, narrow, b.shape) for b in blocks],
        scratch_shapes=[*job_sems(wide, narrow, chunks), pltpu.SemaphoreType.DMA((count,))],
        compiler_params=pltpu.CompilerParams(
            vmem_limit_bytes=56 * MIB, collective_id=1, has_side_effects=True
        ),
        name="attend",
    )(mixed, lat, keep, mod, small, qkv, proj, *blocks)


def back_kernel(wide, narrow, chunks, own, own_ff, *refs):
    (gn2a_ref, gn2b_ref, twoa_ref, twob_ref, middle_ref, branch_ref, gout_ref, att_ref, mixed_ref,
     q_ref, k_ref, v_ref, probs_ref, mod_ref, small_ref, proj_ref, wq_ref, wk_ref, wv_ref,
     lat_ref, normed_ref, fc2b_ref, hida_ref, hidb_ref, sils_ref, ada_ref, fc1s_ref,
     fc2s_ref) = refs[:28]
    (rows_ref, xg_ref, wgrad_ref, cond_ref, small_out, qkvg_ref, projg_ref, fc1g_ref,
     fc2g_ref) = refs[28:37]
    (ga, gmid, gmix, gmoved, sums, proj_src, qkv_src, early, late, cuts_in, hcuts, hcuts_in, part, cond_in,
     send_a, recv_a, send_b, recv_b, send_c, recv_c, send_d, recv_d, send_e, recv_e, send_f, recv_f,
     send_g, recv_g) = refs[37:65]
    buffers, (sends, recvs) = refs[65:-2], refs[-2:]
    step = pl.program_id(0)
    model = lat_ref.shape[1]
    slabs = model // 128
    last = 3 + slabs
    p = Place(wide, narrow)
    half, hidden = own_ff // 2, 2 * hida_ref.shape[1]
    waves = scatter_jobs(p, [fc1s_ref, fc2s_ref, proj_src, qkv_src],
                         [fc1g_ref, fc2g_ref, projg_ref, qkvg_ref], buffers, sends, recvs, chunks)
    gbl = xg_ref
    mine = lambda ref: ref.at[p.core, p.slot]

    @pl.when(step == 0)
    def _():
        greet_all(p)
        waves.run(0)
        waves.run(1)
        sums[...] = jnp.zeros_like(sums)
        gmix[...] = jnp.zeros_like(gmix)
        clear_edges(gmoved)
        tiles = tiles_of(hida_ref[...]) + tiles_of(hidb_ref[...])
        for sid in range(p.total):
            d = p.order_of(sid)
            moves = [(half * d, 0, half), (hidden // 2 + half * d, half, half)]
            hcuts[sid] = move_lanes(tiles, moves, 1)[0]
        hcuts_in[p.sid] = hcuts[p.sid]
        p.to_all(lambda sid: hcuts.at[sid], hcuts_in.at[p.sid], send_g, recv_g)

    @pl.when(step < 4)
    def _():
        rows = pl.ds(pl.multiple_of(step * GROUP, GROUP), GROUP)
        middle = middle_ref[...]
        two = twoa_ref[...] + twob_ref[...] + small_ref[11:12, :]
        gout = gout_ref[...].astype(F32)
        rows_ref[...] = (middle + mod_ref[5:6, :] * two).astype(BF16)
        sums[3] += row_sum(gout * two)
        unit, scale = unit_rows(middle)
        gn2 = gn2a_ref[...] + gn2b_ref[...]
        sums[1] += row_sum(gn2)
        sums[2] += row_sum(gn2 * unit)
        gm = gout + unit_back(gn2 * (1.0 + mod_ref[4:5, :]), unit, scale)
        gmid[rows, :] = gm
        sums[0] += row_sum(gm * branch_ref[...])
        gb = gm * mod_ref[2:3, :]
        sums[4] += row_sum(gb)
        low = gb.astype(BF16)
        gbl[rows, :] = low
        ga[rows, :] = dot_nt(low, proj_ref[...]).astype(BF16)

    for when, wave in ((1, 2), (1, 3), (2, 4), (3, 5)):
        pl.when(step == when)(lambda: waves.run(wave))

    @pl.when(step == 3)
    def _():
        proj_src[...] = dot_tn(att_ref[...], gbl[...]).astype(BF16).reshape(proj_src.shape)
        waves.run(6)
        for i in range(4):
            early[p.core, p.slot, :, i * model : (i + 1) * model] = jnp.sum(
                sums[i], axis=0, keepdims=True
            )
        p.to_kin(lambda slot: mine(early), mine(early), send_a, recv_a)

    @pl.when(step >= 4)
    def _():
        s = step - 4
        lane = lax.broadcasted_iota(jnp.int32, (GROUP, 128), 1)
        left = lane < HEAD
        eighth = jnp.asarray(0.125, BF16)
        lanes = pl.ds(pl.multiple_of(s * 128, 128), 128)
        weight = jnp.concatenate([wq_ref[...], wk_ref[...], wv_ref[...]], axis=1)
        grads = []
        for g in range(4):
            rows = slice(g * GROUP, (g + 1) * GROUP)
            q, k, v = q_ref[rows, :] * eighth, k_ref[rows, :] * eighth, v_ref[rows, :]
            grad = ga[rows, lanes]
            gq = gk = gv = None
            for h in (0, 1):
                keep = left if h == 0 else jnp.logical_not(left)
                only = lambda value: jnp.where(keep, value, jnp.zeros_like(value))
                p_low = probs_ref[h, g]
                prob = p_low.astype(F32)
                gh = only(grad)
                gp = dot_nt(v, gh)
                inner = jnp.sum(prob * gp, axis=0, keepdims=True)
                gs = (prob * (gp - inner)).astype(BF16)
                terms = (dot_tn(gs, only(k)), dot_nn(gs, only(q)), dot_nn(p_low, gh))
                if h == 0:
                    gq, gk, gv = terms
                else:
                    gq, gk, gv = gq + terms[0], gk + terms[1], gv + terms[2]
            grads.append(jnp.concatenate([gq, gk, gv], axis=1).astype(BF16))
            gmixed = dot_nt(grads[-1], weight)
            for t in range(slabs):
                gmix[t + 1, g, 2:34] += gmixed[:, t * 128 : t * 128 + 128].reshape(32, 8, 128)
        grad = jnp.concatenate(grads, axis=0)
        columns = pl.ds(pl.multiple_of(s * 384, 128), 384)
        found = dot_tn(mixed_ref[...], grad).astype(BF16)
        qkv_src[..., columns] = found.reshape(*qkv_src.shape[:-1], 384)

    for s in range(slabs):
        pl.when(step == 4 + s)(lambda: waves.run(7 + s))

    @pl.when(step == 6)
    def _():
        p.to_kin_wait(lambda slot: mine(early), mine(early), send_a, recv_a)
        remote(early.at[p.core], early.at[p.core], send_d, recv_d, p.sibling).start()

    @pl.when(step == last)
    def _():
        waves.wave = 7 + slabs
        masks = edge_masks()
        rows_out = []
        for s in range(slabs):
            at_s = slice(s * 128, s * 128 + 128)
            k = [jnp.broadcast_to(small_ref[n : n + 1, at_s], (8, 128)) for n in range(9)]

            def move(r, total):
                for gi in (0, 1):
                    for gj in (0, 1):
                        pair = load_pair(gmix, s + 1, gi, gj, r)
                        total = total + pair[0] + pair[1]
                        store_pair(gmoved, 0, gi, gj, r, shift_pair(pair, 1 - gj, *masks))
                return total

            total = lax.fori_loop(0, HALF, move, jnp.zeros((8, 128), F32))

            def put(gi, gj, r, pair):
                store_pair(gmix, s, gi, gj, r, pair)

            found = conv_back(0, k, normed_ref.at[s : s + 1], gmix.at[s + 1 : s + 2], gmoved, put)
            late[p.core, p.slot, :, at_s] = jnp.sum(found[9], axis=0, keepdims=True)
            column = [jnp.sum(v, axis=0, keepdims=True) for v in (*found[:9], total)]
            column.append(jnp.sum(sums[4, :, at_s], axis=0, keepdims=True))
            column.append(jnp.sum(fc2b_ref[:, at_s], axis=0, keepdims=True))
            rows_out.append(jnp.concatenate(column + [jnp.zeros((4, 128), F32)], axis=0))
            if s % 2:
                waves.tick()
        scale_sum = jnp.zeros((8, model), F32)
        for g in range(4):
            rows = pl.ds(g * GROUP, GROUP)
            unit, scale = unit_rows(lat_ref[rows, :].astype(F32))
            gn = jnp.concatenate(
                [gmix[s, g, 2:34].reshape(GROUP, 128) for s in range(slabs)], axis=1
            )
            scale_sum = scale_sum + row_sum(gn * unit)
            gmid[rows, :] = gmid[rows, :] + unit_back(gn * (1.0 + mod_ref[1:2, :]), unit, scale)
        late[p.core, p.slot, :, model:] = jnp.sum(scale_sum, axis=0, keepdims=True)
        wait_late = p.to_kin(lambda slot: mine(late), mine(late), send_c, recv_c)
        waves.tick()
        p.to_all_wait(lambda sid: hcuts.at[sid], hcuts_in.at[p.sid], send_g, recv_g)
        small_out[16:, :] = jnp.sum(hcuts_in[...], axis=0)
        cuts = hcuts
        modulation = tiles_of(late[p.core, p.slot]) + tiles_of(early[p.core, p.slot])
        share = 6 * own
        for sid in range(p.total):
            d = p.order_of(sid)
            piece = move_lanes(rows_out, [(own * d, 0, own)], 1)[0][:12]
            bias = move_lanes(modulation, [(share * d, 0, share)], -(-share // 128))
            rest = [jnp.zeros((4 - len(bias), 128), F32)]
            cuts[sid] = jnp.concatenate([piece, *bias, *rest], axis=0)
        cuts_in[p.sid] = cuts[p.sid]
        wait_cuts = p.to_all(lambda sid: cuts.at[sid], cuts_in.at[p.sid], send_b, recv_b)
        xg_ref[...] = gmid[...].astype(BF16)
        wait_late()
        swap_late = remote(late.at[p.core], late.at[p.core], send_e, recv_e, p.sibling)
        swap_late.start()
        waves.tick()
        remote(early.at[p.core], early.at[p.core], send_d, recv_d, p.sibling).wait()
        swap_late.wait()
        sil = sils_ref[:, :own].astype(BF16)
        cond = None
        for ref, start in ((late, 0), (early, 2 * model)):
            size = ref.shape[-1]
            span = slice(start, start + size)
            found = ref[...].reshape(p.total, size)
            low = found.astype(BF16)
            wgrad_ref[:, span] = dot_tn(sil, low)
            term = dot_nt(low, ada_ref[:, span])
            cond = term if cond is None else cond + term
        cond = jnp.concatenate([cond, jnp.zeros((p.total, 128 - own), F32)], axis=1)
        for sid in range(p.total):
            part[sid] = cond[sid : sid + 1, :]
        cond_in[p.me] = part[p.sid]
        wait_cond = p.to_all(lambda sid: part.at[sid], cond_in.at[p.me], send_f, recv_f)
        waves.end()
        wait_cuts()
        small_out[:16, :] = jnp.sum(cuts_in[...], axis=0)
        wait_cond()
        cond_ref[...] = cond_in[...]


def back(wide, narrow, gn2, two, middle, branch, gout, att, mixed, triple, probs, mod, small, proj, qkv,
         lat, normed, fc2b, hidden_sums, sils, ada, fc1s, fc2s):
    total = wide * narrow
    tokens, model = lat.shape
    slabs, columns = model // 128, ada.shape[1]
    hidden = 2 * hidden_sums[0].shape[1]
    own, own_ff = ada.shape[0], hidden // total
    by_group = pl.BlockSpec((GROUP, model), lambda t: (jnp.minimum(t, 3), 0))
    slab = lambda t: jnp.clip(t - 4, 0, slabs - 1)
    third = lambda rows, i: pl.BlockSpec((rows, 128), lambda t: (0, i * slabs + slab(t)))
    all_sems, kin_sems = (pltpu.SemaphoreType.DMA((n,)) for n in (total, total // 2))
    one_sem = pltpu.SemaphoreType.DMA
    padded = lambda count: pltpu.VMEM((count, 4, 36, 8, 128), F32)
    height = model // wide
    bits = bit_sizes(wide)
    shapes = [fc1s.shape, fc2s.shape, (*bits, height, model), (*bits, height, 3 * model)]
    chunks = thirds(0, hidden // 2) + thirds(1, model) + [(2, 0, model)]
    chunks += [(3, 384 * s, 384) for s in range(slabs)]
    full = lambda a: once(a.shape)
    outs = [
        like((tokens, model), BF16), like((tokens, model), BF16), like((own, columns), F32),
        like((total, 1, 128), F32), like((32, 128), F32), like((own, 3 * model), F32),
        like((own, model), F32), like((own, hidden // 2), F32), like((own_ff // 2, model), F32),
    ]
    return pl.pallas_call(
        functools.partial(back_kernel, wide, narrow, chunks, own, own_ff),
        grid=(4 + slabs,),
        in_specs=[by_group] * 7 + [full(att), full(mixed)] + [third(tokens, i) for i in range(3)] + [
            pl.BlockSpec((2, 4, GROUP, GROUP), lambda t: (slab(t), 0, 0, 0)),
            full(mod), full(small), full(proj), third(model, 0), third(model, 1), third(model, 2),
            full(lat), full(normed), full(fc2b), full(hidden_sums[0]), full(hidden_sums[1]),
            full(sils), full(ada), full(fc1s), full(fc2s),
        ],
        out_specs=[by_group] + [once(o.shape) for o in outs[1:]],
        out_shape=outs,
        scratch_shapes=[
            pltpu.VMEM((tokens, model), BF16), pltpu.VMEM((tokens, model), F32),
            padded(slabs + 1), padded(1), pltpu.VMEM((5, 8, model), F32),
            pltpu.VMEM(shapes[2], BF16), pltpu.VMEM(shapes[3], BF16),
            pltpu.VMEM((2, total // 2, 1, 4 * model), F32),
            pltpu.VMEM((2, total // 2, 1, 2 * model), F32),
            pltpu.VMEM((total, 16, 128), F32), pltpu.VMEM((total, 16, 128), F32),
            pltpu.VMEM((total, 16, 128), F32),
            pltpu.VMEM((total, 1, 128), F32), pltpu.VMEM((total, 1, 128), F32),
            kin_sems, kin_sems, all_sems, all_sems, kin_sems, kin_sems, one_sem, one_sem,
            one_sem, one_sem, all_sems, all_sems, all_sems, all_sems,
            *scatter_scratch(wide, narrow, shapes), *job_sems(wide, narrow, chunks),
        ],
        compiler_params=pltpu.CompilerParams(
            vmem_limit_bytes=63 * MIB, collective_id=2, has_side_effects=True
        ),
        name="attend_back",
    )(*gn2, *two, middle, branch, gout, att, mixed, triple, triple, triple, probs, mod,
      small, proj, qkv, qkv, qkv, lat, normed, fc2b, *hidden_sums, sils, ada, fc1s,
      fc2s)


def finish_kernel(own, own_ff, order_ref, rows_ref, grads_ref, wgrad_ref, qkvg_ref, projg_ref, fc1a_ref,
                  fc1b_ref, fc2a_ref, fc2b_ref, small_ref, cond_ref, pieces_ref,
                  out_ref, xg_ref, wgrad_out, qkv_out, proj_out, fc1_out, fc2_out, condg_out, adab_out,
                  dw1k_out, dw1b_out, projb_out, fc2b_out, dw2k_out, dw2b_out, fc1b_out):
    model = out_ref.shape[1]
    for src, dst in ((rows_ref, out_ref), (grads_ref, xg_ref)):
        block = src[...].reshape(GROUP, model)
        dst[...] = dot_tn(order_ref[...], block).astype(BF16)

    @pl.when(pl.program_id(0) == 0)
    def _():
        half, hidden, total = own_ff // 2, fc1_out.shape[1], pieces_ref.shape[0]
        wgrad_out[...] = wgrad_ref[...]
        proj_out[...] = projg_ref[...]
        for s in range(model // 128):
            for i in range(3):
                to = i * model + s * 128
                qkv_out[:, to : to + 128] = qkvg_ref[:, s * 384 + i * 128 : s * 384 + i * 128 + 128]
        moves = [
            (hidden // 2 * h + half * d, own_ff * d + half * h, half)
            for d in range(total) for h in (0, 1)
        ]
        tiles = tiles_of(fc1a_ref[...]) + tiles_of(fc1b_ref[...])
        for i, tile in enumerate(move_lanes(tiles, moves, hidden // 128)):
            fc1_out[:, i * 128 : i * 128 + 128] = tile
        fc2_out[:half, :] = fc2a_ref[...]
        fc2_out[half:, :] = fc2b_ref[...]
        tiles = [pieces_ref[d] for d in range(total)]
        moves = [(128 * d, own * d, own) for d in range(total)]
        grad = jnp.concatenate(move_lanes(tiles, moves, model // 128), axis=1)
        cond = cond_ref[...].astype(F32)
        gate = jax.nn.sigmoid(cond)
        condg_out[...] = grad * (gate + cond * gate * (1.0 - gate))
        dw1k_out[...] = small_ref[0:9, :own]
        dw2k_out[...] = small_ref[16:25, :own_ff]
        rows = ((dw1b_out, 9), (projb_out, 10), (fc2b_out, 11), (dw2b_out, 25), (fc1b_out, 26))
        for ref, row in rows:
            ref[...] = small_ref[row : row + 1, : ref.shape[1]]
        for start in range(0, 6 * own, 128):
            size = min(128, 6 * own - start)
            row = 12 + start // 128
            adab_out[:, start : start + size] = small_ref[row : row + 1, :size]


def finish(order, rows, grads, wgrad, qkvg, projg, fc1, fc2, small, cond, pieces):
    tokens, model = rows.shape
    own, hidden, own_ff = wgrad.shape[0], 2 * fc1[0].shape[1], 2 * fc2[0].shape[0]
    split = lambda value: value.reshape(4, 4, 64, model)
    block = pl.BlockSpec((4, 1, 64, model), lambda t: (0, t, 0, 0))
    lines = pl.BlockSpec((GROUP, model), lambda t: (t, 0))
    rest = [wgrad, qkvg, projg, *fc1, *fc2, small, cond, pieces]
    outs = [
        like((tokens, model), BF16), like((tokens, model), BF16), like(wgrad.shape, F32),
        like(qkvg.shape, F32), like(projg.shape, F32), like((own, hidden), F32),
        like((own_ff, model), F32), like((1, model), F32), like((1, 6 * own), F32),
        like((9, own), F32), like((1, own), F32), like((1, own), F32), like((1, own), F32),
        like((9, own_ff), F32), like((1, own_ff), F32), like((1, own_ff), F32),
    ]
    return pl.pallas_call(
        functools.partial(finish_kernel, own, own_ff),
        grid=(4,),
        in_specs=[once(order.shape), block, block] + [once(a.shape) for a in rest],
        out_specs=[lines, lines] + [once(o.shape) for o in outs[2:]],
        out_shape=outs,
        compiler_params=pltpu.CompilerParams(vmem_limit_bytes=60 * MIB),
        name="finish",
    )(order, split(rows), split(grads), *rest)


def on_device(wide, narrow, latents, condition, valid_mask, ada_weight, ada_bias, dw1_kernel, dw1_bias,
              qkv_weight, proj_weight, proj_bias, fc1_weight, fc1_bias, dw2_kernel, dw2_bias,
              fc2_weight, fc2_bias, out_cotangent):
    total = wide * narrow
    w, n = lax.axis_index("wide"), lax.axis_index("narrow")
    me = w * narrow + n
    model, hidden = latents.shape[2], fc1_weight.shape[1]
    own, own_ff = model // total, hidden // total

    bias_at = lax.dynamic_update_slice(
        jnp.zeros((1, 6 * model), F32), ada_bias.astype(F32)[None, :], (0, me * ada_bias.shape[0])
    )
    parts = [(0, dw1_kernel), (9, dw1_bias[None]), (10, proj_bias[None]), (11, fc2_bias[None]),
             (16, dw2_kernel), (25, dw2_bias[None]), (26, fc1_bias[None])]
    small = sum(
        jnp.pad(v, ((row, 32 - row - v.shape[0]), (0, 128 - v.shape[1]))) for row, v in parts
    )
    mask = jnp.broadcast_to(valid_mask[0].astype(BF16)[:, None], (latents.shape[1], 128))
    order = order_matrix()

    chunks = [(0, 0, 128)] + thirds(2, 3 * model) + [(3, 0, model)] + thirds(1, hidden // 2)
    (mod, sils, model_small, hidden_small, lat, gout, g2, normed, mixed, keep, fc2b, fc1b, fc1_one, qkv,
     proj) = front(
        wide, narrow, latents[0], out_cotangent[0], mask, order, condition, ada_weight, bias_at, small,
        fc1_weight, [qkv_weight, proj_weight], chunks,
    )
    qkv, proj = qkv.reshape(model, 3 * model), proj.reshape(model, model)
    fc2a, fc2b_rows = fc2_weight[: own_ff // 2], fc2_weight[own_ff // 2 :]
    triple, probs, att, branch, middle, n2, n2t, fc2_one = attend(
        wide, narrow, mixed, lat, keep, mod, model_small, qkv, proj, [fc2a], thirds(0, model)
    )
    chunks = thirds(0, hidden // 2) + thirds(1, model)
    as_fc1 = lambda rows: rows.reshape(model, hidden // 2)
    as_fc2 = lambda rows: rows.reshape(hidden // 2, model)
    as_lines = lambda grad: grad.reshape(*bit_sizes(wide), grad.shape[0] // wide, grad.shape[1])
    two_a, gn2_a, fc1g, fc2g, sums_a, fc1_two, fc2_two = feed_forward(
        wide, narrow, n2, n2t, g2, as_fc1(fc1_one), hidden_small, 0, as_fc2(fc2_one),
        [fc1b, fc2b_rows], chunks, False,
    )
    two_b, gn2_b, fc1h, fc2h, sums_b, fc1o, fc2o = feed_forward(
        wide, narrow, n2, n2t, g2, as_fc1(fc1_two), hidden_small, 1, as_fc2(fc2_two),
        [as_lines(fc1g), as_lines(fc2g)], chunks, True,
    )
    rows, grads, ada_wgrad, pieces, small, qkvg, projg, fc1p, fc2p = back(
        wide, narrow, (gn2_a, gn2_b), (two_a, two_b), middle, branch, gout, att, mixed, triple, probs,
        mod, model_small, proj, qkv, lat, normed, fc2b, (sums_a, sums_b), sils, ada_weight,
        as_lines(fc1h), as_lines(fc2h),
    )
    (out, xg, ada_wgrad, qkvg, projg, fc1g, fc2g, cond_grad, ada_bgrad, dw1k, dw1b, projb, fc2bg, dw2k,
     dw2b, fc1bg) = finish(
        order, rows, grads, ada_wgrad, qkvg, projg, (fc1o, fc1p), (fc2o, fc2p), small, condition, pieces
    )
    return (
        out[None], xg[None], cond_grad, ada_wgrad, ada_bgrad[0], dw1k, dw1b[0], qkvg, projg, projb[0],
        fc1g, fc1bg[0], dw2k, dw2b[0], fc2g, fc2bg[0],
    )


def solution(mesh):
    wide, narrow = mesh.shape["wide"], mesh.shape["narrow"]
    rows = lambda rank: P(AXES, *(None,) * (rank - 1))
    lanes = P(None, AXES)
    in_specs = (
        rows(3), rows(2), rows(2), rows(2), rows(1), lanes, rows(1), rows(2), rows(2), rows(1),
        rows(2), rows(1), lanes, rows(1), rows(2), rows(1), rows(3),
    )
    out_specs = (
        rows(3), rows(3), rows(2), rows(2), rows(1), lanes, rows(1), rows(2), rows(2), rows(1),
        rows(2), rows(1), lanes, rows(1), rows(2), rows(1),
    )
    return jax.shard_map(
        functools.partial(on_device, wide, narrow), mesh=mesh, in_specs=in_specs,
        out_specs=out_specs, check_vma=False,
    )
```

time: 390 us -> 309 us (0.79)
  Pallas kernels: 357 us -> 301 us
  local copies, waits for them, and re-layouts: 27.1 us -> 2.67 us
    pallas_call x1, Pallas kernels: 72.3 us -> 29.6 us  [attend(): pl.pallas_call(functools.partial(attend_kernel, wide, narrow, chunks, cou...]
    pallas_call x3 -> x4, Pallas kernels: 227 us -> 207 us  [the longest x2 110 us: feed_forward(): pl.pallas_call(functools.partial(ff_kernel, wide, narrow, chunks, count,...]
    unnamed x23 -> x2, local copies, waits for them, and re-layouts: 7.54 us -> 0.01 us
    pallas_call x1, Pallas kernels: 58.1 us -> 65.1 us  [front(): pl.pallas_call(functools.partial(front_kernel, wide, narrow, chunks, coun...]
    pad x7 -> x0, local copies, waits for them, and re-layouts: 4.7 us -> none  [on_device(): lanes = lambda rows: jnp.pad(rows, ((0, 0), (0, 128 - rows.shape[1])))]
where the time goes in v3:
time: 309 us
  Pallas kernels  301 us (97%)
  other arithmetic  3.52 us (1%)
    pallas_call x2, Pallas kernels, feed_forward(): pl.pallas_call(functools.partial(ff_kernel, wide, narrow, chunks, count,...  110 us
    pallas_call x1, Pallas kernels, back(): pl.pallas_call(functools.partial(back_kernel, wide, narrow, chunks, own,...  90.5 us
    pallas_call x1, Pallas kernels, front(): pl.pallas_call(functools.partial(front_kernel, wide, narrow, chunks, coun...  65.1 us
    pallas_call x1, Pallas kernels, attend(): pl.pallas_call(functools.partial(attend_kernel, wide, narrow, chunks, cou...  29.6 us
    pallas_call x1, Pallas kernels, finish(): pl.pallas_call(functools.partial(finish_kernel, own, own_ff), grid=(4,),...  6.18 us

profile of v3, /device:TPU:0, one launch (start us, length us, event | category | flops | bytes accessed | tf_op | source)
XLA Modules:
  0.0 308.6 jit_solution(10106554584933556224)
XLA Ops:
  0.7 0.7 broadcast_in_dim.49
  1.3 0.7 convert_reduce_fusion
  2.0 1.4 pad_add_fusion.refs_7_
  3.4 0.2 dynamic_update_slice.3.refs_6_
  3.6 0.0 copy-start
  3.6 0.7 fusion.refs_3_.order_ref
  4.4 1.6 fusion.7
  6.0 0.9 broadcast_in_dim.38.refs_2_
  6.9 0.0 copy-done
  6.9 65.1 %front.1 = (f32[8,768]{1,0:T(8,128)}, f32[32,128]{1,0:T(8,128)}, f32[16,768]{1,0:T(8,128)}, f32[16,3072]{1,0:T(8,128)}, bf16[1024,768]{1,0:T(8,128)(2,1)}, /*ind...) custom-call(bf16[1024,768]{1,0:T(8,128)(2,1)} %bitcast.42, ...), custom_call_target="tpu_custom_call" | custom-call | tf_op jit(solution)/shard_map/front/pallas_call | solution.py:837
  72.0 29.6 %attend.1 = (bf16[1024,2304]{1,0:T(8,128)(2,1)}, bf16[12,4,256,256]{3,2,1,0:T(8,128)(2,1)}, bf16[1024,768]{1,0:T(8,128)(2,1)}, f32[1024,768]{1,0:T(8,128)}, f32[...) custom-call(bf16[1024,768]{1,0:T(8,128)(2,1)} %get-tuple-element.78., ...), custom_call_target="tpu_custom_call" | custom-call | tf_op jit(solution)/shard_map/attend/pallas_call | solution.py:934
  101.6 54.8 %feed_forward.2 = (f32[1024,768]{1,0:T(8,128)}, f32[1024,768]{1,0:T(8,128)}, bf16[768,1536]{1,0:T(8,128)(2,1)}, bf16[1536,768]{1,0:T(8,128)(2,1)}, f32[16,1536]{...) custom-call(bf16[1024,768]{1,0:T(8,128)(2,1)} %get-tuple-element.85.refs_0_, ...), custom_call_target="tpu_custom_call" | custom-call | tf_op jit(solution)/shard_map/feed_forward/pallas_call | solution.py:286
  156.4 55.4 %feed_forward.3 = (f32[1024,768]{1,0:T(8,128)}, f32[1024,768]{1,0:T(8,128)}, bf16[768,1536]{1,0:T(8,128)(2,1)}, bf16[1536,768]{1,0:T(8,128)(2,1)}, f32[16,1536]{...) custom-call(bf16[1024,768]{1,0:T(8,128)(2,1)} %get-tuple-element.85.refs_0_, ...), custom_call_target="tpu_custom_call" | custom-call | tf_op jit(solution)/shard_map/feed_forward/pallas_call | solution.py:286
  211.7 90.5 %attend_back.1 = (bf16[1024,768]{1,0:T(8,128)(2,1)}, bf16[1024,768]{1,0:T(8,128)(2,1)}, f32[24,4608]{1,0:T(8,128)}, f32[32,1,128]{2,1,0:T(1,128)}, f32[32,128]{1...) custom-call(f32[1024,768]{1,0:T(8,128)} %get-tuple-element.92.refs_0_, ...), custom_call_target="tpu_custom_call" | custom-call | tf_op jit(solution)/shard_map/attend_back/pallas_call | solution.py:1184
  302.2 6.2 %finish.1 = (bf16[1024,768]{1,0:T(8,128)(2,1)}, bf16[1024,768]{1,0:T(8,128)(2,1)}, f32[24,4608]{1,0:T(8,128)}, f32[24,2304]{1,0:T(8,128)}, f32[24,768]{1,0:T(8,1...) custom-call(bf16[256,256]{1,0:T(8,128)(2,1)} %fusion.refs_3_.order_r, ...), custom_call_target="tpu_custom_call" | custom-call | tf_op jit(solution)/shard_map/finish/pallas_call | solution.py:1275
  (2 shorter events, 0.0 us)
Async XLA Ops:
  3.6 3.2 %copy-start = (f32[1,4608]{1,0:T(1,128)}, f32[1,4608]{1,0:T(1,128)S(1)}, u32[]{:S(2)}) copy-start(f32[1,4608]{1,0:T(1,128)S(1)} %dynamic_update_slice.3.refs_6_) | copy-start | bytes 55300

commit v4 on v3

--- a/solution.py
+++ b/solution.py
@@ -169,19 +169,21 @@
 
 def ff_kernel(wide, narrow, chunks, count, steps, sums_over, *refs):
     n2_ref, n2t_ref, g2_ref, fc1_ref, small_ref, fc2_ref = refs[:6]
-    srcs = refs[6 : 6 + count]
-    branch_ref, gn2_ref, w1g_ref, w2g_ref, sums_ref = refs[6 + count : 11 + count]
-    dsts = refs[11 + count : 11 + 2 * count]
-    hid, ga, gc, gcs, act, ghl = refs[11 + 2 * count : 17 + 2 * count]
+    so_far, refs = refs[6 : 6 + 2 * sums_over], refs[6 + 2 * sums_over :]
+    srcs = refs[:count]
+    branch_out, gn2_out, w1g_ref, w2g_ref, sums_ref = refs[count : 5 + count]
+    dsts, refs = refs[5 + count : 5 + 2 * count], refs[5 + 2 * count :]
+    hid, ga, gc, gcs, act, ghl, branch_ref, gn2_ref, held = refs[:9]
+    totals = (branch_ref, gn2_ref)
     step = pl.program_id(0)
     slabs = hid.shape[0]
     p = Place(wide, narrow)
     if sums_over:
-        buffers, (sends, recvs) = refs[17 + 2 * count : -2], refs[-2:]
+        buffers, (sends, recvs) = refs[9:-2], refs[-2:]
         waves = scatter_jobs(p, srcs, dsts, buffers, sends, recvs, chunks)
         own_copies = []
     else:
-        sends, recvs, local = refs[17 + 2 * count :]
+        sends, recvs, local = refs[9:]
         waves = gather_jobs(p, srcs, dsts, sends, recvs, chunks)
         own_copies = [
             pltpu.make_async_copy(
@@ -196,14 +198,14 @@
 
     @pl.when(step == 0)
     def _():
+        greet(p.partners())
         for copy in own_copies:
             copy.start()
-        greet(p.partners())
-        waves.run(0)
-        for copy in own_copies:
-            copy.wait()
-        branch_ref[...] = jnp.zeros_like(branch_ref)
-        gn2_ref[...] = jnp.zeros_like(gn2_ref)
+        for i, ref in enumerate(totals):
+            if sums_over:
+                pltpu.make_async_copy(so_far[i], ref, held.at[i]).start()
+            else:
+                ref[...] = jnp.zeros_like(ref)
         for ref in (hid, gc, gcs):
             clear_edges(ref)
 
@@ -215,6 +217,14 @@
             lanes = slice(slab * 128, slab * 128 + 128)
             hid[slab, g, 2:34] = full[:, lanes].reshape(32, 8, 128)
             ga[slab, g] = back[:, lanes].reshape(32, 8, 128)
+
+    @pl.when(step == 0)
+    def _():
+        met(len(p.partners()))
+        waves.run(0)
+        waves.run(1)
+        for copy in own_copies:
+            copy.wait()
 
     hook(0)
     masks = edge_masks()
@@ -254,8 +264,20 @@
         if slab == 0:
             hook(1)
 
+    if sums_over:
+        @pl.when(step == 0)
+        def _():
+            for i, ref in enumerate(totals):
+                pltpu.make_async_copy(so_far[i], ref, held.at[i]).wait()
+
     branch_ref[...] += dot_nn(act[...], fc2_ref[...])
     gn2_ref[...] += dot_nt(ghl[...], fc1_ref[...])
+
+    @pl.when(step == steps - 1)
+    def _():
+        for i, out in enumerate((branch_out, gn2_out)):
+            pltpu.make_async_copy(totals[i], out, held.at[i]).start()
+
     w2g_ref[...] = dot_tn(act[...], g2_ref[...]).astype(w2g_ref.dtype)
     w1g_ref[...] = dot_nn(n2t_ref[...], ghl[...]).astype(w1g_ref.dtype)
     hook(2)
@@ -263,10 +285,13 @@
     @pl.when(step == steps - 1)
     def _():
         waves.finish()
-
-
-def feed_forward(wide, narrow, n2, n2t, g2, fc1, small, part, fc2, arrays, chunks, sums_over,
+        for i, out in enumerate((branch_out, gn2_out)):
+            pltpu.make_async_copy(totals[i], out, held.at[i]).wait()
+
+
+def feed_forward(wide, narrow, n2, n2t, g2, fc1, small, part, fc2, arrays, chunks, so_far=(),
                  width=256):
+    sums_over = bool(so_far)
     tokens, model = n2.shape
     hidden = fc1.shape[1]
     slabs, steps, count = width // 128, hidden // width, len(arrays)
@@ -289,9 +314,9 @@
         in_specs=[
             once((tokens, model)), once((model, tokens)), once((tokens, model)),
             columns(model), pl.BlockSpec((16, width), lambda s: (0, part * steps + s)), lines,
-        ] + in_moved,
+        ] + [anywhere] * len(so_far) + in_moved,
         out_specs=[
-            once((tokens, model)), once((tokens, model)), columns(model), lines, columns(16)
+            anywhere, anywhere, columns(model), lines, columns(16)
         ] + out_moved,
         out_shape=[
             like((tokens, model), F32), like((tokens, model), F32),
@@ -300,12 +325,14 @@
         scratch_shapes=[
             padded, pltpu.VMEM((slabs, 4, 32, 8, 128), F32), padded, padded,
             pltpu.VMEM((tokens, width), BF16), pltpu.VMEM((tokens, width), BF16),
+            pltpu.VMEM((tokens, model), F32), pltpu.VMEM((tokens, model), F32),
+            pltpu.SemaphoreType.DMA((2,)),
         ] + extra,
         compiler_params=pltpu.CompilerParams(
             vmem_limit_bytes=56 * MIB, collective_id=4 if sums_over else 3, has_side_effects=True
         ),
         name="feed_forward",
-    )(n2, n2t, g2, fc1, small, fc2, *arrays)
+    )(n2, n2t, g2, fc1, small, fc2, *so_far, *arrays)
 
 
 def flip(index, bit):
@@ -334,7 +361,10 @@
     barrier = pltpu.get_barrier_semaphore()
     for place in places:
         pl.semaphore_signal(barrier, inc=1, device_id=place, device_id_type=pl.DeviceIdType.MESH)
-    pl.semaphore_wait(barrier, len(places))
+
+
+def met(count):
+    pl.semaphore_wait(pltpu.get_barrier_semaphore(), count)
 
 
 def greet_all(place):
@@ -349,7 +379,6 @@
         return carry
 
     lax.fori_loop(1, total, body, 0)
-    pl.semaphore_wait(barrier, total - 1)
 
 
 def remote(src, dst, send_sem, recv_sem, place):
@@ -435,16 +464,18 @@
 
 
 class Transfer:
-    def __init__(self, place, sends, recvs, chunk, columns):
+    def __init__(self, place, sends, recvs, chunk, columns, turn):
         self.p, self.sends, self.recvs, self.chunk = place, sends, recvs, chunk
         start, size = columns
         self.all = pl.ds(start, size)
         levels = len(bit_sizes(place.wide))
         far = list(range(levels - 1))
-        if size % 256:
-            self.parts = [(self.all, far)]
-        else:
-            self.parts = [(pl.ds(start, size // 2), far), (pl.ds(start + size // 2, size // 2), far[::-1])]
+        half = size // 256 * 128
+        if turn % 2:
+            far = far[::-1]
+        self.parts = [(pl.ds(start, size - half), far)]
+        if half:
+            self.parts.append((pl.ds(start + size - half, half), far[::-1]))
         self.stages = levels + 1
         self.bits = digits_of(place.w, place.wide)
         self.count = 0
@@ -470,13 +501,13 @@
         for copy in self.copies(stage):
             copy.start()
 
-    def finish(self):
+    def finish(self, stages):
         pass
 
 
 class Gather(Transfer):
-    def __init__(self, place, src, dst, sends, recvs, chunk, columns):
-        super().__init__(place, sends, recvs, chunk, columns)
+    def __init__(self, place, src, dst, sends, recvs, chunk, columns, turn):
+        super().__init__(place, sends, recvs, chunk, columns, turn)
         self.src, self.dst = src, dst
 
     def make(self, stage, count_only):
@@ -509,52 +540,63 @@
         for copy in self.copies(stage):
             copy.wait_recv()
 
-    def finish(self):
-        for stage in range(self.stages):
+    def finish(self, stages):
+        for stage in stages:
             for copy in self.copies(stage):
                 copy.wait_send()
 
 
+def steady(first, stages, lag=2):
+    return [first + lag * s for s in range(stages + 1)]
+
+
 class Waves:
-    def __init__(self, chunks, lag=2):
-        self.chunks, self.wave, self.lag = chunks, 0, lag
-        self.stages = chunks[0][0].stages
-        self.count = len(chunks) + lag * self.stages
+    def __init__(self, jobs, plan, resume=-1):
+        self.jobs, self.resume = jobs, resume
+        self.stages = jobs[0].stages
+        self.plan = plan or [steady(c, self.stages) for c in range(len(jobs))]
+        self.wave = resume + 1
+        self.last = max(waves[-1] for waves in self.plan)
 
     def run(self, wave):
-        for c, jobs in enumerate(self.chunks):
-            stage, rest = divmod(wave - c, self.lag)
-            if rest:
-                continue
-            for job in jobs:
-                if 1 <= stage <= self.stages:
+        for job, waves in zip(self.jobs, self.plan):
+            for stage, when in enumerate(waves):
+                if when != wave:
+                    continue
+                if stage and waves[stage - 1] > self.resume:
                     job.wait(stage - 1)
-                if 0 <= stage < self.stages:
+                if stage < self.stages:
                     job.start(stage)
 
     def tick(self, times=1):
         for _ in range(times):
-            if self.wave < self.count:
+            if self.wave <= self.last:
                 self.run(self.wave)
                 self.wave += 1
 
-    def through(self, chunk):
-        while self.wave <= chunk + self.lag * self.stages:
+    def through(self, wave):
+        while self.wave <= min(wave, self.last):
             self.tick()
 
     def at_hook(self, hook, hooks):
-        left = self.count - 1
-        for wave in range(1 + hook * left // hooks, 1 + (hook + 1) * left // hooks):
+        first = self.resume + 3
+        left = self.last + 1 - first
+        for wave in range(first + hook * left // hooks, first + (hook + 1) * left // hooks):
             self.run(wave)
 
-    def finish(self):
-        for jobs in self.chunks:
-            for job in jobs:
-                job.finish()
-
-    def end(self):
-        self.tick(self.count)
-        self.finish()
+    def finish(self, last=None):
+        last = self.last if last is None else last
+        for job, waves in zip(self.jobs, self.plan):
+            here = [s for s in range(self.stages) if self.resume < waves[s] <= last]
+            for stage in here:
+                if waves[stage + 1] > last:
+                    job.wait(stage)
+            job.finish(here)
+
+    def end(self, last=None):
+        last = self.last if last is None else last
+        self.through(last)
+        self.finish(last)
 
 
 def job_sems(wide, narrow, chunks):
@@ -562,11 +604,12 @@
     return [pltpu.SemaphoreType.DMA((len(chunks), per))] * 2
 
 
-def gather_jobs(place, srcs, dsts, sends, recvs, chunks, lag=2):
-    return Waves([
-        [Gather(place, srcs[i], dsts[i], sends, recvs, c, columns)]
+def gather_jobs(place, srcs, dsts, sends, recvs, chunks, plan=None, resume=-1, shift=0):
+    jobs = [
+        Gather(place, srcs[i], dsts[i], sends, recvs, c, columns, c + shift)
         for c, (i, *columns) in enumerate(chunks)
-    ], lag)
+    ]
+    return Waves(jobs, plan, resume)
 
 
 def gathered_shape(wide, narrow, shape):
@@ -579,7 +622,7 @@
 
 class Scatter(Transfer):
     def __init__(self, place, src, buffers, out, sends, recvs, chunk, columns):
-        super().__init__(place, sends, recvs, chunk, columns)
+        super().__init__(place, sends, recvs, chunk, columns, chunk)
         self.src, self.out = src, out
         self.halves, self.line, self.got = buffers[:-2], buffers[-2], buffers[-1]
         self.rows = self.line.shape[1]
@@ -645,14 +688,9 @@
                 self.line[m, :, columns] = total[rows].astype(BF16)
             return
 
-        def body(i, carry):
-            rows = pl.ds(pl.multiple_of(i * 16, 16), 16)
-            into[(*arrived, rows, columns)] = (
-                source[(*mine, rows, columns)].astype(F32) + into[(*arrived, rows, columns)].astype(F32)
-            ).astype(BF16)
-            return carry
-
-        lax.fori_loop(0, into.shape[-2] // 16, body, 0)
+        into[(*arrived, slice(None), columns)] = (
+            source[(*mine, slice(None), columns)] + into[(*arrived, slice(None), columns)]
+        )
 
 
 def scatter_scratch(wide, narrow, shapes):
@@ -665,12 +703,13 @@
     return scratch
 
 
-def scatter_jobs(place, srcs, outs, buffers, sends, recvs, chunks, lag=2):
+def scatter_jobs(place, srcs, outs, buffers, sends, recvs, chunks, plan=None):
     per = len(buffers) // len(srcs)
-    return Waves([
-        [Scatter(place, srcs[i], buffers[i * per : (i + 1) * per], outs[i], sends, recvs, c, columns)]
+    jobs = [
+        Scatter(place, srcs[i], buffers[i * per : (i + 1) * per], outs[i], sends, recvs, c, columns)
         for c, (i, *columns) in enumerate(chunks)
-    ], lag)
+    ]
+    return Waves(jobs, plan)
 
 
 def owned_shape(shape, narrow):
@@ -698,7 +737,7 @@
     return [values[:, i : i + 128] for i in range(0, values.shape[1], 128)]
 
 
-def front_kernel(wide, narrow, chunks, count, own, own_ff, *refs):
+def front_kernel(wide, narrow, chunks, plan, count, own, own_ff, *refs):
     (x_ref, cot_ref, mask_ref, order_ref, cond_ref, ada_ref, bias_ref, small_ref, fc1_ref) = refs[:9]
     srcs = refs[9 : 9 + count]
     (mod_ref, sils_ref, model_ref, hidden_ref, lat_ref, gout_ref, g2_ref, normed_ref, mixed_ref,
@@ -715,17 +754,17 @@
     ]
     for copy in own_copies:
         copy.start()
-    waves = gather_jobs(p, [small_ref, fc1a_ref, *srcs], [smalls, *dsts], sends, recvs, chunks)
+    greet_all(p)
+    waves = gather_jobs(p, [small_ref, fc1a_ref, *srcs], [smalls, *dsts], sends, recvs, chunks, plan)
+    last = waves.plan[chunks.index((3, 0, model))][-1]
     cond = cond_ref[...].astype(F32)
     sil = (cond * jax.nn.sigmoid(cond)).astype(BF16).astype(F32)
     tiles = tiles_of(sil)
     for sid in range(p.total):
         d = p.order_of(sid)
         sil_out[sid] = move_lanes(tiles, [(own * d, 0, own)], 1)[0]
-    greet_all(p)
-    waves.tick(2)
     got[p.sid] = sil_out[p.sid]
-    wait_sil = p.to_all(lambda sid: sil_out.at[sid], got.at[p.sid], send_a, recv_a)
+    smalls[(*mine, p.n)] = small_ref[...]
 
     def arrange(t):
         rows = pl.ds(t * GROUP, GROUP)
@@ -743,7 +782,14 @@
                 tile = unit[src, s * 128 : s * 128 + 128].reshape(8, 8, 128)
                 normed_ref[s, g, 2 + 8 * t : 10 + 8 * t] = tile
 
+    met(p.total - 1)
+    wait_sil = p.to_all(lambda sid: sil_out.at[sid], got.at[p.sid], send_a, recv_a)
+    waves.tick(2)
     arrange(0)
+    for copy in own_copies:
+        copy.wait()
+    waves.tick()
+    arrange(1)
     wait_sil()
     sil = got[...].reshape(p.total, 128)
     sils_ref[...] = sil
@@ -752,17 +798,16 @@
         part[d // p.half, d % p.half] = product[d : d + 1, :]
     to_sibling = remote(part.at[1 - p.core], sib, send_b, recv_b, p.sibling)
     to_sibling.start()
-    for copy in own_copies:
-        copy.wait()
-    smalls[(*mine, p.n)] = small_ref[...]
     waves.tick()
-    arrange(1)
+    arrange(2)
     to_sibling.wait()
     part[p.core] = part[p.core] + sib[...]
     rows_in[p.slot] = part[p.core, p.slot]
     wait_rows = p.to_kin(lambda slot: part.at[p.core, slot], rows_in.at[p.slot], send_c, recv_c)
     waves.tick()
-    arrange(2)
+    arrange(3)
+    clear_edges(normed_ref)
+    waves.tick()
     columns = tiles_of(fc1_ref[...].astype(F32))
     for h, ref in enumerate((fc1a_ref, fc1b_ref)):
         moves = [
@@ -771,16 +816,7 @@
         ref[...] = jnp.concatenate(move_lanes(columns, moves, len(columns) // 2), axis=1).astype(BF16)
     own_fc1 = pltpu.make_async_copy(fc1a_ref, dsts[0].at[(*mine, p.n)], local.at[count])
     own_fc1.start()
-    waves.tick()
-    arrange(3)
-    clear_edges(normed_ref)
-    waves.tick()
-    wait_rows()
-    mod = jnp.sum(rows_in[...], axis=0)
-    for i in range(6):
-        mod_ref[i : i + 1, :] = mod[:, i * model : (i + 1) * model]
-    own_fc1.wait()
-    waves.through(0)
+    waves.through(waves.plan[0][-1])
     pieces = [smalls[(*static_digits(d // narrow, wide), d % narrow)].astype(F32) for d in range(p.total)]
     moves = [(128 * d, own * d, own) for d in range(p.total)]
     model_ref[...] = jnp.concatenate(move_lanes([q[:16] for q in pieces], moves, slabs), axis=1)
@@ -791,7 +827,11 @@
     hidden_ref[...] = jnp.concatenate(
         move_lanes([q[16:] for q in pieces], moves, hidden // 128), axis=1
     )
-    waves.tick()
+    own_fc1.wait()
+    wait_rows()
+    mod = jnp.sum(rows_in[...], axis=0)
+    for i in range(6):
+        mod_ref[i : i + 1, :] = mod[:, i * model : (i + 1) * model]
 
     shift, scale, gate = mod_ref[0:1, :], mod_ref[1:2, :], mod_ref[5:6, :]
     total = jnp.zeros((8, model), F32)
@@ -819,11 +859,11 @@
             return carry
 
         lax.fori_loop(0, HALF, body, 0)
-        waves.tick()
-    waves.end()
-
-
-def front(wide, narrow, x, cot, mask, order, cond, ada, bias, small, fc1, blocks, chunks):
+        waves.through(min(waves.wave, last))
+    waves.end(last)
+
+
+def front(wide, narrow, x, cot, mask, order, cond, ada, bias, small, fc1, blocks, chunks, plan):
     total = wide * narrow
     tokens, model = x.shape
     slabs, count, columns = model // 128, len(blocks), ada.shape[1]
@@ -835,7 +875,7 @@
     one_sem = pltpu.SemaphoreType.DMA
     kin_sems = pltpu.SemaphoreType.DMA((total // 2,))
     return pl.pallas_call(
-        functools.partial(front_kernel, wide, narrow, chunks, count, own, own_ff),
+        functools.partial(front_kernel, wide, narrow, chunks, plan, count, own, own_ff),
         in_specs=[inside] * 9 + [anywhere] * count,
         out_specs=[inside] * 12 + [anywhere] * (count + 1),
         out_shape=[
@@ -861,41 +901,32 @@
     )(x, cot, mask, order, cond, ada, bias, small, fc1, *blocks)
 
 
-def attend_kernel(wide, narrow, chunks, count, *refs):
-    mixed_ref, lat_ref, keep_ref, mod_ref, small_ref, qkv_ref, proj_ref = refs[:7]
-    srcs = refs[7 : 7 + count]
-    (triple_ref, probs_ref, att_ref, branch_ref, middle_ref, n2_ref,
-     n2t_ref) = refs[7 + count : 14 + count]
-    dsts = refs[14 + count : 14 + 2 * count]
-    sends, recvs, local = refs[14 + 2 * count :]
+def attend_kernel(wide, narrow, chunks, plan, resume, shift, *refs):
+    mixed_ref, lat_ref, keep_ref, mod_ref, small_ref, qkv_ref, proj_ref, fc1_in, fc2_in = refs[:9]
+    triple_ref, probs_ref, att_ref, branch_ref, n2_ref, n2t_ref, fc1_ref, fc2_ref = refs[9:17]
+    sends, recvs = refs[17:]
     step = pl.program_id(0)
     p = Place(wide, narrow)
-    waves = gather_jobs(p, srcs, dsts, sends, recvs, chunks)
-    own_copies = [
-        pltpu.make_async_copy(
-            srcs[i], dsts[i].at[(*digits_of(p.w, wide), p.n)], local.at[i]
-        ) for i in range(count)
-    ]
+    waves = gather_jobs(p, [fc1_in, fc2_in], [fc1_ref, fc2_ref], sends, recvs, chunks, plan, resume,
+                        shift)
 
     def on(when, work):
         pl.when(step == when)(work)
-
-    def first():
-        for copy in own_copies:
-            copy.start()
-        greet(p.partners())
-        waves.run(0)
-        for copy in own_copies:
-            copy.wait()
 
     def hook(position):
         for when in range(4):
             on(when, lambda: waves.at_hook(2 * when + position, 8))
 
-    on(0, first)
+    def first():
+        met(len(p.partners()))
+        waves.run(resume + 1)
+        waves.run(resume + 2)
+
+    on(0, lambda: greet(p.partners()))
     model = lat_ref.shape[1]
     slabs = model // 128
     triple_ref[...] = dot_nn(mixed_ref[...], qkv_ref[...]).astype(BF16)
+    on(0, first)
     lane = lax.broadcasted_iota(jnp.int32, (GROUP, 128), 1)
     left = lane < HEAD
     keep = jnp.concatenate([keep_ref[...]] * 2, axis=1)
@@ -918,7 +949,6 @@
     middle = lat_ref[...].astype(F32) + mod_ref[2:3, :] * branch
     unit, _ = unit_rows(middle)
     branch_ref[...] = branch
-    middle_ref[...] = middle
     n2 = unit * (1.0 + mod_ref[4:5, :]) + mod_ref[3:4, :]
     n2_ref[...] = n2.astype(BF16)
     n2t_ref[...] = n2.T.astype(BF16)
@@ -926,46 +956,49 @@
     on(3, waves.finish)
 
 
-def attend(wide, narrow, mixed, lat, keep, mod, small, qkv, proj, blocks, chunks):
+def attend(wide, narrow, mixed, lat, keep, mod, small, qkv, proj, fc1, fc2, chunks, plan, resume, shift):
     tokens, model = lat.shape
-    heads, count = model // HEAD, len(blocks)
+    heads = model // HEAD
     by_group = lambda columns: pl.BlockSpec((GROUP, columns), lambda g: (g, 0))
     anywhere = pl.BlockSpec(memory_space=pl.ANY)
     return pl.pallas_call(
-        functools.partial(attend_kernel, wide, narrow, chunks, count),
+        functools.partial(attend_kernel, wide, narrow, chunks, plan, resume, shift),
         grid=(4,),
         in_specs=[
             by_group(model), by_group(model), by_group(128), whole(mod.shape),
-            whole(small.shape), once(qkv.shape), once(proj.shape),
-        ] + [anywhere] * count,
+            whole(small.shape), once(qkv.shape), once(proj.shape), anywhere, anywhere,
+        ],
         out_specs=[
             by_group(3 * model), pl.BlockSpec((heads, 1, GROUP, GROUP), lambda g: (0, g, 0, 0)),
-            by_group(model), by_group(model), by_group(model), by_group(model),
-            pl.BlockSpec((model, GROUP), lambda g: (0, g)),
-        ] + [anywhere] * count,
+            by_group(model), by_group(model), by_group(model),
+            pl.BlockSpec((model, GROUP), lambda g: (0, g)), anywhere, anywhere,
+        ],
         out_shape=[
             like((tokens, 3 * model), BF16), like((heads, 4, GROUP, GROUP), BF16),
             like((tokens, model), BF16), like((tokens, model), F32),
-            like((tokens, model), F32), like((tokens, model), BF16), like((model, tokens), BF16),
-        ] + [gathered_shape(wide, narrow, b.shape) for b in blocks],
-        scratch_shapes=[*job_sems(wide, narrow, chunks), pltpu.SemaphoreType.DMA((count,))],
+            like((tokens, model), BF16), like((model, tokens), BF16),
+            like(fc1.shape, BF16), like(fc2.shape, BF16),
+        ],
+        input_output_aliases={7: 6, 8: 7},
+        scratch_shapes=job_sems(wide, narrow, chunks),
         compiler_params=pltpu.CompilerParams(
             vmem_limit_bytes=56 * MIB, collective_id=1, has_side_effects=True
         ),
         name="attend",
-    )(mixed, lat, keep, mod, small, qkv, proj, *blocks)
-
-
-def back_kernel(wide, narrow, chunks, own, own_ff, *refs):
-    (gn2a_ref, gn2b_ref, twoa_ref, twob_ref, middle_ref, branch_ref, gout_ref, att_ref, mixed_ref,
+    )(mixed, lat, keep, mod, small, qkv, proj, fc1, fc2)
+
+
+def back_kernel(wide, narrow, chunks, plan, own, own_ff, *refs):
+    (gn2_ref, two_ref, branch_ref, gout_ref, att_ref, mixed_ref,
      q_ref, k_ref, v_ref, probs_ref, mod_ref, small_ref, proj_ref, wq_ref, wk_ref, wv_ref,
-     lat_ref, normed_ref, fc2b_ref, hida_ref, hidb_ref, sils_ref, ada_ref, fc1s_ref,
-     fc2s_ref) = refs[:28]
+     lat_ref, normed_hbm, fc2b_ref, hida_ref, hidb_ref, sils_ref, ada_ref, fc1s_ref,
+     fc2s_ref) = refs[:25]
     (rows_ref, xg_ref, wgrad_ref, cond_ref, small_out, qkvg_ref, projg_ref, fc1g_ref,
-     fc2g_ref) = refs[28:37]
+     fc2g_ref) = refs[25:34]
     (ga, gmid, gmix, gmoved, sums, proj_src, qkv_src, early, late, cuts_in, hcuts, hcuts_in, part, cond_in,
+     gt, normed_ref, held,
      send_a, recv_a, send_b, recv_b, send_c, recv_c, send_d, recv_d, send_e, recv_e, send_f, recv_f,
-     send_g, recv_g) = refs[37:65]
+     send_g, recv_g) = refs[34:65]
     buffers, (sends, recvs) = refs[65:-2], refs[-2:]
     step = pl.program_id(0)
     model = lat_ref.shape[1]
@@ -974,15 +1007,15 @@
     p = Place(wide, narrow)
     half, hidden = own_ff // 2, 2 * hida_ref.shape[1]
     waves = scatter_jobs(p, [fc1s_ref, fc2s_ref, proj_src, qkv_src],
-                         [fc1g_ref, fc2g_ref, projg_ref, qkvg_ref], buffers, sends, recvs, chunks)
+                         [fc1g_ref, fc2g_ref, projg_ref, qkvg_ref], buffers, sends, recvs, chunks,
+                         plan)
     gbl = xg_ref
     mine = lambda ref: ref.at[p.core, p.slot]
 
     @pl.when(step == 0)
     def _():
         greet_all(p)
-        waves.run(0)
-        waves.run(1)
+        pltpu.make_async_copy(normed_hbm, normed_ref, held).start()
         sums[...] = jnp.zeros_like(sums)
         gmix[...] = jnp.zeros_like(gmix)
         clear_edges(gmoved)
@@ -992,52 +1025,57 @@
             moves = [(half * d, 0, half), (hidden // 2 + half * d, half, half)]
             hcuts[sid] = move_lanes(tiles, moves, 1)[0]
         hcuts_in[p.sid] = hcuts[p.sid]
-        p.to_all(lambda sid: hcuts.at[sid], hcuts_in.at[p.sid], send_g, recv_g)
 
     @pl.when(step < 4)
     def _():
         rows = pl.ds(pl.multiple_of(step * GROUP, GROUP), GROUP)
-        middle = middle_ref[...]
-        two = twoa_ref[...] + twob_ref[...] + small_ref[11:12, :]
+        branch = branch_ref[...]
+        middle = lat_ref[rows, :].astype(F32) + mod_ref[2:3, :] * branch
+        two = two_ref[...] + small_ref[11:12, :]
         gout = gout_ref[...].astype(F32)
         rows_ref[...] = (middle + mod_ref[5:6, :] * two).astype(BF16)
         sums[3] += row_sum(gout * two)
         unit, scale = unit_rows(middle)
-        gn2 = gn2a_ref[...] + gn2b_ref[...]
+        gn2 = gn2_ref[...]
         sums[1] += row_sum(gn2)
         sums[2] += row_sum(gn2 * unit)
         gm = gout + unit_back(gn2 * (1.0 + mod_ref[4:5, :]), unit, scale)
         gmid[rows, :] = gm
-        sums[0] += row_sum(gm * branch_ref[...])
+        sums[0] += row_sum(gm * branch)
         gb = gm * mod_ref[2:3, :]
         sums[4] += row_sum(gb)
         low = gb.astype(BF16)
         gbl[rows, :] = low
         ga[rows, :] = dot_nt(low, proj_ref[...]).astype(BF16)
 
-    for when, wave in ((1, 2), (1, 3), (2, 4), (3, 5)):
-        pl.when(step == when)(lambda: waves.run(wave))
+    @pl.when(step == 0)
+    def _():
+        met(p.total - 1)
+        waves.run(0)
+        waves.run(1)
+        p.to_all(lambda sid: hcuts.at[sid], hcuts_in.at[p.sid], send_g, recv_g)
+
+    for when in (1, 2):
+        pl.when(step == when)(lambda: waves.run(when + 1))
 
     @pl.when(step == 3)
     def _():
         proj_src[...] = dot_tn(att_ref[...], gbl[...]).astype(BF16).reshape(proj_src.shape)
-        waves.run(6)
+        waves.run(4)
         for i in range(4):
             early[p.core, p.slot, :, i * model : (i + 1) * model] = jnp.sum(
                 sums[i], axis=0, keepdims=True
             )
         p.to_kin(lambda slot: mine(early), mine(early), send_a, recv_a)
 
-    @pl.when(step >= 4)
-    def _():
+    def attention(groups):
         s = step - 4
         lane = lax.broadcasted_iota(jnp.int32, (GROUP, 128), 1)
         left = lane < HEAD
         eighth = jnp.asarray(0.125, BF16)
         lanes = pl.ds(pl.multiple_of(s * 128, 128), 128)
         weight = jnp.concatenate([wq_ref[...], wk_ref[...], wv_ref[...]], axis=1)
-        grads = []
-        for g in range(4):
+        for g in groups:
             rows = slice(g * GROUP, (g + 1) * GROUP)
             q, k, v = q_ref[rows, :] * eighth, k_ref[rows, :] * eighth, v_ref[rows, :]
             grad = ga[rows, lanes]
@@ -1056,17 +1094,25 @@
                     gq, gk, gv = terms
                 else:
                     gq, gk, gv = gq + terms[0], gk + terms[1], gv + terms[2]
-            grads.append(jnp.concatenate([gq, gk, gv], axis=1).astype(BF16))
-            gmixed = dot_nt(grads[-1], weight)
+            found = jnp.concatenate([gq, gk, gv], axis=1).astype(BF16)
+            gt[rows, :] = found
+            gmixed = dot_nt(found, weight)
             for t in range(slabs):
                 gmix[t + 1, g, 2:34] += gmixed[:, t * 128 : t * 128 + 128].reshape(32, 8, 128)
-        grad = jnp.concatenate(grads, axis=0)
-        columns = pl.ds(pl.multiple_of(s * 384, 128), 384)
-        found = dot_tn(mixed_ref[...], grad).astype(BF16)
+
+    pl.when(step >= 4)(lambda: attention((0, 1)))
+    for s in range(slabs):
+        pl.when(step == 4 + s)(lambda: waves.run(5 + 2 * s))
+
+    @pl.when(step >= 4)
+    def _():
+        attention((2, 3))
+        columns = pl.ds(pl.multiple_of((step - 4) * 384, 128), 384)
+        found = dot_tn(mixed_ref[...], gt[...]).astype(BF16)
         qkv_src[..., columns] = found.reshape(*qkv_src.shape[:-1], 384)
 
     for s in range(slabs):
-        pl.when(step == 4 + s)(lambda: waves.run(7 + s))
+        pl.when(step == 4 + s)(lambda: waves.run(6 + 2 * s))
 
     @pl.when(step == 6)
     def _():
@@ -1075,7 +1121,8 @@
 
     @pl.when(step == last)
     def _():
-        waves.wave = 7 + slabs
+        waves.wave = 5 + 2 * slabs
+        pltpu.make_async_copy(normed_hbm, normed_ref, held).wait()
         masks = edge_masks()
         rows_out = []
         for s in range(slabs):
@@ -1157,7 +1204,7 @@
         cond_ref[...] = cond_in[...]
 
 
-def back(wide, narrow, gn2, two, middle, branch, gout, att, mixed, triple, probs, mod, small, proj, qkv,
+def back(wide, narrow, gn2, two, branch, gout, att, mixed, triple, probs, mod, small, proj, qkv,
          lat, normed, fc2b, hidden_sums, sils, ada, fc1s, fc2s):
     total = wide * narrow
     tokens, model = lat.shape
@@ -1175,6 +1222,8 @@
     shapes = [fc1s.shape, fc2s.shape, (*bits, height, model), (*bits, height, 3 * model)]
     chunks = thirds(0, hidden // 2) + thirds(1, model) + [(2, 0, model)]
     chunks += [(3, 384 * s, 384) for s in range(slabs)]
+    starts = [0, 1, 2, 3, 5, 7, 4] + [6 + 2 * s for s in range(slabs)]
+    plan = [steady(c, wide.bit_length()) for c in starts]
     full = lambda a: once(a.shape)
     outs = [
         like((tokens, model), BF16), like((tokens, model), BF16), like((own, columns), F32),
@@ -1182,12 +1231,12 @@
         like((own, model), F32), like((own, hidden // 2), F32), like((own_ff // 2, model), F32),
     ]
     return pl.pallas_call(
-        functools.partial(back_kernel, wide, narrow, chunks, own, own_ff),
+        functools.partial(back_kernel, wide, narrow, chunks, plan, own, own_ff),
         grid=(4 + slabs,),
-        in_specs=[by_group] * 7 + [full(att), full(mixed)] + [third(tokens, i) for i in range(3)] + [
+        in_specs=[by_group] * 4 + [full(att), full(mixed)] + [third(tokens, i) for i in range(3)] + [
             pl.BlockSpec((2, 4, GROUP, GROUP), lambda t: (slab(t), 0, 0, 0)),
             full(mod), full(small), full(proj), third(model, 0), third(model, 1), third(model, 2),
-            full(lat), full(normed), full(fc2b), full(hidden_sums[0]), full(hidden_sums[1]),
+            full(lat), pl.BlockSpec(memory_space=pl.ANY), full(fc2b), full(hidden_sums[0]), full(hidden_sums[1]),
             full(sils), full(ada), full(fc1s), full(fc2s),
         ],
         out_specs=[by_group] + [once(o.shape) for o in outs[1:]],
@@ -1201,6 +1250,7 @@
             pltpu.VMEM((total, 16, 128), F32), pltpu.VMEM((total, 16, 128), F32),
             pltpu.VMEM((total, 16, 128), F32),
             pltpu.VMEM((total, 1, 128), F32), pltpu.VMEM((total, 1, 128), F32),
+            pltpu.VMEM((tokens, 384), BF16), padded(slabs), one_sem,
             kin_sems, kin_sems, all_sems, all_sems, kin_sems, kin_sems, one_sem, one_sem,
             one_sem, one_sem, all_sems, all_sems, all_sems, all_sems,
             *scatter_scratch(wide, narrow, shapes), *job_sems(wide, narrow, chunks),
@@ -1209,7 +1259,7 @@
             vmem_limit_bytes=63 * MIB, collective_id=2, has_side_effects=True
         ),
         name="attend_back",
-    )(*gn2, *two, middle, branch, gout, att, mixed, triple, triple, triple, probs, mod,
+    )(gn2, two, branch, gout, att, mixed, triple, triple, triple, probs, mod,
       small, proj, qkv, qkv, qkv, lat, normed, fc2b, *hidden_sums, sils, ada, fc1s,
       fc2s)
 
@@ -1303,31 +1353,37 @@
     mask = jnp.broadcast_to(valid_mask[0].astype(BF16)[:, None], (latents.shape[1], 128))
     order = order_matrix()
 
-    chunks = [(0, 0, 128)] + thirds(2, 3 * model) + [(3, 0, model)] + thirds(1, hidden // 2)
+    fc2a, fc2b_rows = fc2_weight[: own_ff // 2], fc2_weight[own_ff // 2 :]
+    chunks = [(0, 0, 128)] + thirds(2, 3 * model) + [(3, 0, model)]
+    stages = wide.bit_length()
+    plan = [steady(c, stages) for c in range(5)]
+    needed = plan[4][-1]
+    chunks += thirds(1, hidden // 2) + thirds(4, model)
+    plan += [[6 + c] + steady(needed + 1 + c, stages - 1) for c in range(6)]
     (mod, sils, model_small, hidden_small, lat, gout, g2, normed, mixed, keep, fc2b, fc1b, fc1_one, qkv,
-     proj) = front(
+     proj, fc2_one) = front(
         wide, narrow, latents[0], out_cotangent[0], mask, order, condition, ada_weight, bias_at, small,
-        fc1_weight, [qkv_weight, proj_weight], chunks,
+        fc1_weight, [qkv_weight, proj_weight, fc2a], chunks, plan,
     )
     qkv, proj = qkv.reshape(model, 3 * model), proj.reshape(model, model)
-    fc2a, fc2b_rows = fc2_weight[: own_ff // 2], fc2_weight[own_ff // 2 :]
-    triple, probs, att, branch, middle, n2, n2t, fc2_one = attend(
-        wide, narrow, mixed, lat, keep, mod, model_small, qkv, proj, [fc2a], thirds(0, model)
+    triple, probs, att, branch, n2, n2t, fc1_one, fc2_one = attend(
+        wide, narrow, mixed, lat, keep, mod, model_small, qkv, proj, fc1_one, fc2_one,
+        thirds(0, hidden // 2) + thirds(1, model), plan[5:], needed, 5,
     )
     chunks = thirds(0, hidden // 2) + thirds(1, model)
     as_fc1 = lambda rows: rows.reshape(model, hidden // 2)
     as_fc2 = lambda rows: rows.reshape(hidden // 2, model)
     as_lines = lambda grad: grad.reshape(*bit_sizes(wide), grad.shape[0] // wide, grad.shape[1])
-    two_a, gn2_a, fc1g, fc2g, sums_a, fc1_two, fc2_two = feed_forward(
+    two, gn2, fc1g, fc2g, sums_a, fc1_two, fc2_two = feed_forward(
         wide, narrow, n2, n2t, g2, as_fc1(fc1_one), hidden_small, 0, as_fc2(fc2_one),
-        [fc1b, fc2b_rows], chunks, False,
+        [fc1b, fc2b_rows], chunks,
     )
-    two_b, gn2_b, fc1h, fc2h, sums_b, fc1o, fc2o = feed_forward(
+    two, gn2, fc1h, fc2h, sums_b, fc1o, fc2o = feed_forward(
         wide, narrow, n2, n2t, g2, as_fc1(fc1_two), hidden_small, 1, as_fc2(fc2_two),
-        [as_lines(fc1g), as_lines(fc2g)], chunks, True,
+        [as_lines(fc1g), as_lines(fc2g)], chunks, (two, gn2),
     )
     rows, grads, ada_wgrad, pieces, small, qkvg, projg, fc1p, fc2p = back(
-        wide, narrow, (gn2_a, gn2_b), (two_a, two_b), middle, branch, gout, att, mixed, triple, probs,
+        wide, narrow, gn2, two, branch, gout, att, mixed, triple, probs,
         mod, model_small, proj, qkv, lat, normed, fc2b, (sums_a, sums_b), sils, ada_weight,
         as_lines(fc1h), as_lines(fc2h),
     )

time: 309 us -> 281 us (0.909)
  Pallas kernels: 301 us -> 274 us
    pallas_call x3, Pallas kernels: 185 us -> 170 us  [the longest x1 83.4 us: back(): pl.pallas_call(functools.partial(back_kernel, wide, narrow, chunks, plan,...]
    pallas_call x2, Pallas kernels: 110 us -> 97.6 us  [feed_forward(): pl.pallas_call(functools.partial(ff_kernel, wide, narrow, chunks, count,...]
where the time goes in v4:
time: 281 us
  Pallas kernels  274 us (98%)
  other arithmetic  3.53 us (1%)
    pallas_call x2, Pallas kernels, feed_forward(): pl.pallas_call(functools.partial(ff_kernel, wide, narrow, chunks, count,...  97.6 us
    pallas_call x1, Pallas kernels, back(): pl.pallas_call(functools.partial(back_kernel, wide, narrow, chunks, plan,...  83.4 us
    pallas_call x1, Pallas kernels, front(): pl.pallas_call(functools.partial(front_kernel, wide, narrow, chunks, plan...  53 us
    pallas_call x1, Pallas kernels, attend(): pl.pallas_call(functools.partial(attend_kernel, wide, narrow, chunks, pla...  33.6 us
    pallas_call x1, Pallas kernels, finish(): pl.pallas_call(functools.partial(finish_kernel, own, own_ff), grid=(4,),...  6.18 us

profile of v4, /device:TPU:0, one launch (start us, length us, event | category | flops | bytes accessed | tf_op | source)
XLA Modules:
  0.0 280.9 jit_solution(2481287379399407379)
XLA Ops:
  0.7 0.7 broadcast_in_dim.49
  1.3 0.7 convert_reduce_fusion
  2.0 1.4 pad_add_fusion.refs_7_
  3.4 0.2 dynamic_update_slice.3.refs_6_
  3.6 0.0 copy-start
  3.6 0.8 fusion.refs_3_.order_ref
  4.4 1.6 fusion.7
  6.0 0.9 broadcast_in_dim.38.refs_2_
  6.9 0.0 copy-done
  6.9 53.0 %front.1 = (f32[8,768]{1,0:T(8,128)}, f32[32,128]{1,0:T(8,128)}, f32[16,768]{1,0:T(8,128)}, f32[16,3072]{1,0:T(8,128)}, bf16[1024,768]{1,0:T(8,128)(2,1)}, /*ind...) custom-call(bf16[1024,768]{1,0:T(8,128)(2,1)} %bitcast.42, ...), custom_call_target="tpu_custom_call" | custom-call | tf_op jit(solution)/shard_map/front/pallas_call | solution.py:877
  59.9 33.6 %attend.1 = (bf16[1024,2304]{1,0:T(8,128)(2,1)}, bf16[12,4,256,256]{3,2,1,0:T(8,128)(2,1)}, bf16[1024,768]{1,0:T(8,128)(2,1)}, f32[1024,768]{1,0:T(8,128)}, bf16...) custom-call(bf16[1024,768]{1,0:T(8,128)(2,1)} %get-tuple-element.79., ...), custom_call_target="tpu_custom_call", output_to_operand_aliasing={{6}: (7, {}), {7}: (8, {})} | custom-call | tf_op jit(solution)/shard_map/attend/pallas_call | solution.py:964
  93.5 49.9 %feed_forward.2 = (f32[1024,768]{1,0:T(8,128)}, f32[1024,768]{1,0:T(8,128)}, bf16[768,1536]{1,0:T(8,128)(2,1)}, bf16[1536,768]{1,0:T(8,128)(2,1)}, f32[16,1536]{...) custom-call(bf16[1024,768]{1,0:T(8,128)(2,1)} %get-tuple-element.88.refs_0_, ...), custom_call_target="tpu_custom_call" | custom-call | tf_op jit(solution)/shard_map/feed_forward/pallas_call | solution.py:311
  143.4 47.7 %feed_forward.3 = (f32[1024,768]{1,0:T(8,128)}, f32[1024,768]{1,0:T(8,128)}, bf16[768,1536]{1,0:T(8,128)(2,1)}, bf16[1536,768]{1,0:T(8,128)(2,1)}, f32[16,1536]{...) custom-call(bf16[1024,768]{1,0:T(8,128)(2,1)} %get-tuple-element.88.refs_0_, ...), custom_call_target="tpu_custom_call" | custom-call | tf_op jit(solution)/shard_map/feed_forward/pallas_call | solution.py:311
  191.2 83.4 %attend_back.1 = (bf16[1024,768]{1,0:T(8,128)(2,1)}, bf16[1024,768]{1,0:T(8,128)(2,1)}, f32[24,4608]{1,0:T(8,128)}, f32[32,1,128]{2,1,0:T(1,128)}, f32[32,128]{1...) custom-call(f32[1024,768]{1,0:T(8,128)} %get-tuple-element.101.refs_0_, ...), custom_call_target="tpu_custom_call" | custom-call | tf_op jit(solution)/shard_map/attend_back/pallas_call | solution.py:1233
  274.5 6.2 %finish.1 = (bf16[1024,768]{1,0:T(8,128)(2,1)}, bf16[1024,768]{1,0:T(8,128)(2,1)}, f32[24,4608]{1,0:T(8,128)}, f32[24,2304]{1,0:T(8,128)}, f32[24,768]{1,0:T(8,1...) custom-call(bf16[256,256]{1,0:T(8,128)(2,1)} %fusion.refs_3_.order_r, ...), custom_call_target="tpu_custom_call" | custom-call | tf_op jit(solution)/shard_map/finish/pallas_call | solution.py:1325
  (2 shorter events, 0.0 us)
Async XLA Ops:
  3.6 3.3 %copy-start = (f32[1,4608]{1,0:T(1,128)}, f32[1,4608]{1,0:T(1,128)S(1)}, u32[]{:S(2)}) copy-start(f32[1,4608]{1,0:T(1,128)S(1)} %dynamic_update_slice.3.refs_6_) | copy-start | bytes 55300

commit v5 on v4

--- a/solution.py
+++ b/solution.py
@@ -161,16 +161,26 @@
 
 
 def order_matrix():
-    d = jnp.arange(GROUP)
-    group, position, column = d // 64, (d % 64) // HALF, d % HALF
-    source = (2 * position + group // 2) * GRID + 2 * column + group % 2
-    return (source[:, None] == jnp.arange(GROUP)[None, :]).astype(BF16)
-
-
-def ff_kernel(wide, narrow, chunks, count, steps, sums_over, *refs):
+    d = lax.broadcasted_iota(jnp.int32, (GROUP, GROUP), 0)
+    column = lax.broadcasted_iota(jnp.int32, (GROUP, GROUP), 1)
+    group, position = d >> 6, (d >> 4) & 3
+    source = (2 * position + (group >> 1)) * GRID + 2 * (d & 15) + (group & 1)
+    return jnp.where(source == column, 1.0, 0.0).astype(BF16)
+
+
+def part_of(ref, span):
+    return ref if span is None else ref.at[pl.ds(*span)]
+
+
+def span_shape(array, span):
+    return array.shape if span is None else (span[1], *array.shape[1:])
+
+
+def ff_kernel(wide, narrow, chunks, spans, steps, sums_over, *refs):
+    count = len(spans)
     n2_ref, n2t_ref, g2_ref, fc1_ref, small_ref, fc2_ref = refs[:6]
     so_far, refs = refs[6 : 6 + 2 * sums_over], refs[6 + 2 * sums_over :]
-    srcs = refs[:count]
+    srcs = [part_of(ref, span) for ref, span in zip(refs, spans)]
     branch_out, gn2_out, w1g_ref, w2g_ref, sums_ref = refs[count : 5 + count]
     dsts, refs = refs[5 + count : 5 + 2 * count], refs[5 + 2 * count :]
     hid, ga, gc, gcs, act, ghl, branch_ref, gn2_ref, held = refs[:9]
@@ -289,7 +299,7 @@
             pltpu.make_async_copy(totals[i], out, held.at[i]).wait()
 
 
-def feed_forward(wide, narrow, n2, n2t, g2, fc1, small, part, fc2, arrays, chunks, so_far=(),
+def feed_forward(wide, narrow, n2, n2t, g2, fc1, small, part, fc2, arrays, spans, chunks, so_far=(),
                  width=256):
     sums_over = bool(so_far)
     tokens, model = n2.shape
@@ -305,11 +315,11 @@
         extra = scatter_scratch(wide, narrow, shapes) + job_sems(wide, narrow, chunks)
         in_moved, out_moved = [once(s) for s in shapes], [once(m.shape) for m in moved]
     else:
-        moved = [gathered_shape(wide, narrow, a.shape) for a in arrays]
+        moved = [gathered_shape(wide, narrow, span_shape(a, s)) for a, s in zip(arrays, spans)]
         extra = job_sems(wide, narrow, chunks) + [pltpu.SemaphoreType.DMA((count,))]
         in_moved = out_moved = [anywhere] * count
     return pl.pallas_call(
-        functools.partial(ff_kernel, wide, narrow, chunks, count, steps, sums_over),
+        functools.partial(ff_kernel, wide, narrow, chunks, spans, steps, sums_over),
         grid=(steps,),
         in_specs=[
             once((tokens, model)), once((model, tokens)), once((tokens, model)),
@@ -737,14 +747,16 @@
     return [values[:, i : i + 128] for i in range(0, values.shape[1], 128)]
 
 
-def front_kernel(wide, narrow, chunks, plan, count, own, own_ff, *refs):
-    (x_ref, cot_ref, mask_ref, order_ref, cond_ref, ada_ref, bias_ref, small_ref, fc1_ref) = refs[:9]
-    srcs = refs[9 : 9 + count]
+def front_kernel(wide, narrow, chunks, plan, spans, own, own_ff, *refs):
+    count = len(spans)
+    (x_ref, cot_ref, mask_ref, cond_ref, ada_ref, bias_ref, small_ref, fc1_ref) = refs[:8]
+    srcs, refs = refs[8 : 8 + count], refs[8 + count :]
+    srcs = [part_of(ref, span) for ref, span in zip(srcs, spans)]
     (mod_ref, sils_ref, model_ref, hidden_ref, lat_ref, gout_ref, g2_ref, normed_ref, mixed_ref,
-     keep_ref, fc2b_ref, fc1b_ref) = refs[9 + count : 21 + count]
-    dsts = refs[21 + count : 22 + 2 * count]
-    (fc1a_ref, sil_out, got, part, sib, rows_in, smalls, send_a, recv_a, send_b, recv_b, send_c, recv_c,
-     sends, recvs, local) = refs[22 + 2 * count :]
+     keep_ref, fc2b_ref, fc1b_ref) = refs[:12]
+    dsts, refs = refs[12 : 13 + count], refs[13 + count :]
+    (order_ref, fc1a_ref, sil_out, got, part, sib, rows_in, smalls, send_a, recv_a, send_b, recv_b, send_c, recv_c,
+     sends, recvs, local) = refs
     p = Place(wide, narrow)
     mine = digits_of(p.w, wide)
     model = x_ref.shape[1]
@@ -755,6 +767,7 @@
     for copy in own_copies:
         copy.start()
     greet_all(p)
+    order_ref[...] = order_matrix()
     waves = gather_jobs(p, [small_ref, fc1a_ref, *srcs], [smalls, *dsts], sends, recvs, chunks, plan)
     last = waves.plan[chunks.index((3, 0, model))][-1]
     cond = cond_ref[...].astype(F32)
@@ -770,7 +783,9 @@
         rows = pl.ds(t * GROUP, GROUP)
         tokens = dot_nn(order_ref[...], x_ref[rows, :])
         unit, _ = unit_rows(tokens)
-        kept = dot_nn(order_ref[...], mask_ref[rows, :])
+        mask = mask_ref[:, t * GROUP : (t + 1) * GROUP].astype(F32)
+        mask = (order_ref[...].astype(F32) * mask).astype(BF16)
+        kept = dot_nn(mask, jnp.ones((GROUP, 128), BF16))
         gout = dot_nn(order_ref[...], cot_ref[rows, :]) * jnp.concatenate([kept] * slabs, axis=1)
         for g in range(4):
             src = slice(64 * g, 64 * g + 64)
@@ -863,7 +878,7 @@
     waves.end(last)
 
 
-def front(wide, narrow, x, cot, mask, order, cond, ada, bias, small, fc1, blocks, chunks, plan):
+def front(wide, narrow, x, cot, mask, cond, ada, bias, small, fc1, blocks, spans, chunks, plan):
     total = wide * narrow
     tokens, model = x.shape
     slabs, count, columns = model // 128, len(blocks), ada.shape[1]
@@ -875,8 +890,8 @@
     one_sem = pltpu.SemaphoreType.DMA
     kin_sems = pltpu.SemaphoreType.DMA((total // 2,))
     return pl.pallas_call(
-        functools.partial(front_kernel, wide, narrow, chunks, plan, count, own, own_ff),
-        in_specs=[inside] * 9 + [anywhere] * count,
+        functools.partial(front_kernel, wide, narrow, chunks, plan, spans, own, own_ff),
+        in_specs=[inside] * 8 + [anywhere] * count,
         out_specs=[inside] * 12 + [anywhere] * (count + 1),
         out_shape=[
             like((8, model), F32), like((total, 128), F32), like((16, model), F32),
@@ -885,9 +900,9 @@
             like((tokens, model), BF16), like((tokens, 128), F32), like((8, model), F32),
             like((own, hidden // 2), BF16),
             gathered_shape(wide, narrow, (own, hidden // 2)),
-        ] + [gathered_shape(wide, narrow, b.shape) for b in blocks],
+        ] + [gathered_shape(wide, narrow, span_shape(b, s)) for b, s in zip(blocks, spans)],
         scratch_shapes=[
-            pltpu.VMEM((own, hidden // 2), BF16), pltpu.VMEM((total, 1, 128), F32),
+            pltpu.VMEM((GROUP, GROUP), BF16), pltpu.VMEM((own, hidden // 2), BF16), pltpu.VMEM((total, 1, 128), F32),
             pltpu.VMEM((total, 1, 128), F32), pltpu.VMEM((2, total // 2, 1, columns), F32),
             pltpu.VMEM((total // 2, 1, columns), F32), pltpu.VMEM((total // 2, 1, columns), F32),
             pltpu.VMEM((*bit_sizes(wide), narrow, 32, 128), BF16),
@@ -898,7 +913,7 @@
             vmem_limit_bytes=56 * MIB, collective_id=0, has_side_effects=True
         ),
         name="front",
-    )(x, cot, mask, order, cond, ada, bias, small, fc1, *blocks)
+    )(x, cot, mask, cond, ada, bias, small, fc1, *blocks)
 
 
 def attend_kernel(wide, narrow, chunks, plan, resume, shift, *refs):
@@ -995,11 +1010,11 @@
      fc2s_ref) = refs[:25]
     (rows_ref, xg_ref, wgrad_ref, cond_ref, small_out, qkvg_ref, projg_ref, fc1g_ref,
      fc2g_ref) = refs[25:34]
-    (ga, gmid, gmix, gmoved, sums, proj_src, qkv_src, early, late, cuts_in, hcuts, hcuts_in, part, cond_in,
+    (ga, gmid, gmix, gmoved, sums, proj_src, qkv_src, early, late, cuts, cuts_in, hcuts, hcuts_in, part, cond_in,
      gt, normed_ref, held,
      send_a, recv_a, send_b, recv_b, send_c, recv_c, send_d, recv_d, send_e, recv_e, send_f, recv_f,
-     send_g, recv_g) = refs[34:65]
-    buffers, (sends, recvs) = refs[65:-2], refs[-2:]
+     send_g, recv_g) = refs[34:66]
+    buffers, (sends, recvs) = refs[66:-2], refs[-2:]
     step = pl.program_id(0)
     model = lat_ref.shape[1]
     slabs = model // 128
@@ -1163,16 +1178,17 @@
         wait_late = p.to_kin(lambda slot: mine(late), mine(late), send_c, recv_c)
         waves.tick()
         p.to_all_wait(lambda sid: hcuts.at[sid], hcuts_in.at[p.sid], send_g, recv_g)
-        small_out[16:, :] = jnp.sum(hcuts_in[...], axis=0)
-        cuts = hcuts
+        small_out[8:, :] = jnp.sum(hcuts_in[...], axis=0)
         modulation = tiles_of(late[p.core, p.slot]) + tiles_of(early[p.core, p.slot])
-        share = 6 * own
+        third = 2 * own
         for sid in range(p.total):
             d = p.order_of(sid)
-            piece = move_lanes(rows_out, [(own * d, 0, own)], 1)[0][:12]
-            bias = move_lanes(modulation, [(share * d, 0, share)], -(-share // 128))
-            rest = [jnp.zeros((4 - len(bias), 128), F32)]
-            cuts[sid] = jnp.concatenate([piece, *bias, *rest], axis=0)
+            piece = move_lanes(rows_out, [(own * d, 0, own)], 1)[0][:8]
+            piece = piece + move_lanes(rows_out, [(own * d, 32, own)], 1)[0][8:]
+            bias = [
+                move_lanes(modulation, [(third * (3 * d + i), 64, third)], 1)[0] for i in range(3)
+            ]
+            cuts[sid] = piece + jnp.concatenate(bias + [jnp.zeros((5, 128), F32)], axis=0)
         cuts_in[p.sid] = cuts[p.sid]
         wait_cuts = p.to_all(lambda sid: cuts.at[sid], cuts_in.at[p.sid], send_b, recv_b)
         xg_ref[...] = gmid[...].astype(BF16)
@@ -1199,7 +1215,7 @@
         wait_cond = p.to_all(lambda sid: part.at[sid], cond_in.at[p.me], send_f, recv_f)
         waves.end()
         wait_cuts()
-        small_out[:16, :] = jnp.sum(cuts_in[...], axis=0)
+        small_out[:8, :] = jnp.sum(cuts_in[...], axis=0)
         wait_cond()
         cond_ref[...] = cond_in[...]
 
@@ -1222,12 +1238,12 @@
     shapes = [fc1s.shape, fc2s.shape, (*bits, height, model), (*bits, height, 3 * model)]
     chunks = thirds(0, hidden // 2) + thirds(1, model) + [(2, 0, model)]
     chunks += [(3, 384 * s, 384) for s in range(slabs)]
-    starts = [0, 1, 2, 3, 5, 7, 4] + [6 + 2 * s for s in range(slabs)]
+    starts = [0, 2, 5, 8, 11, 14, 4] + [6 + 2 * s for s in range(slabs)]
     plan = [steady(c, wide.bit_length()) for c in starts]
     full = lambda a: once(a.shape)
     outs = [
         like((tokens, model), BF16), like((tokens, model), BF16), like((own, columns), F32),
-        like((total, 1, 128), F32), like((32, 128), F32), like((own, 3 * model), F32),
+        like((total, 1, 128), F32), like((24, 128), F32), like((own, 3 * model), F32),
         like((own, model), F32), like((own, hidden // 2), F32), like((own_ff // 2, model), F32),
     ]
     return pl.pallas_call(
@@ -1247,8 +1263,8 @@
             pltpu.VMEM(shapes[2], BF16), pltpu.VMEM(shapes[3], BF16),
             pltpu.VMEM((2, total // 2, 1, 4 * model), F32),
             pltpu.VMEM((2, total // 2, 1, 2 * model), F32),
+            pltpu.VMEM((total, 8, 128), F32), pltpu.VMEM((total, 8, 128), F32),
             pltpu.VMEM((total, 16, 128), F32), pltpu.VMEM((total, 16, 128), F32),
-            pltpu.VMEM((total, 16, 128), F32),
             pltpu.VMEM((total, 1, 128), F32), pltpu.VMEM((total, 1, 128), F32),
             pltpu.VMEM((tokens, 384), BF16), padded(slabs), one_sem,
             kin_sems, kin_sems, all_sems, all_sems, kin_sems, kin_sems, one_sem, one_sem,
@@ -1264,14 +1280,15 @@
       fc2s)
 
 
-def finish_kernel(own, own_ff, order_ref, rows_ref, grads_ref, wgrad_ref, qkvg_ref, projg_ref, fc1a_ref,
+def finish_kernel(own, own_ff, rows_ref, grads_ref, wgrad_ref, qkvg_ref, projg_ref, fc1a_ref,
                   fc1b_ref, fc2a_ref, fc2b_ref, small_ref, cond_ref, pieces_ref,
                   out_ref, xg_ref, wgrad_out, qkv_out, proj_out, fc1_out, fc2_out, condg_out, adab_out,
                   dw1k_out, dw1b_out, projb_out, fc2b_out, dw2k_out, dw2b_out, fc1b_out):
     model = out_ref.shape[1]
+    order = order_matrix()
     for src, dst in ((rows_ref, out_ref), (grads_ref, xg_ref)):
         block = src[...].reshape(GROUP, model)
-        dst[...] = dot_tn(order_ref[...], block).astype(BF16)
+        dst[...] = dot_tn(order, block).astype(BF16)
 
     @pl.when(pl.program_id(0) == 0)
     def _():
@@ -1297,18 +1314,17 @@
         cond = cond_ref[...].astype(F32)
         gate = jax.nn.sigmoid(cond)
         condg_out[...] = grad * (gate + cond * gate * (1.0 - gate))
-        dw1k_out[...] = small_ref[0:9, :own]
-        dw2k_out[...] = small_ref[16:25, :own_ff]
-        rows = ((dw1b_out, 9), (projb_out, 10), (fc2b_out, 11), (dw2b_out, 25), (fc1b_out, 26))
-        for ref, row in rows:
-            ref[...] = small_ref[row : row + 1, : ref.shape[1]]
-        for start in range(0, 6 * own, 128):
-            size = min(128, 6 * own - start)
-            row = 12 + start // 128
-            adab_out[:, start : start + size] = small_ref[row : row + 1, :size]
-
-
-def finish(order, rows, grads, wgrad, qkvg, projg, fc1, fc2, small, cond, pieces):
+        dw1k_out[:8, :] = small_ref[:8, :own]
+        dw2k_out[...] = small_ref[8:17, :own_ff]
+        rows = ((dw1k_out.at[8:9], 0, 32), (dw1b_out, 1, 32), (projb_out, 2, 32), (fc2b_out, 3, 32),
+                (dw2b_out, 17, 0), (fc1b_out, 18, 0))
+        for ref, row, lane in rows:
+            ref[...] = small_ref[row : row + 1, lane : lane + ref.shape[1]]
+        for i in range(3):
+            adab_out[:, 2 * own * i : 2 * own * (i + 1)] = small_ref[i : i + 1, 64 : 64 + 2 * own]
+
+
+def finish(rows, grads, wgrad, qkvg, projg, fc1, fc2, small, cond, pieces):
     tokens, model = rows.shape
     own, hidden, own_ff = wgrad.shape[0], 2 * fc1[0].shape[1], 2 * fc2[0].shape[0]
     split = lambda value: value.reshape(4, 4, 64, model)
@@ -1325,12 +1341,12 @@
     return pl.pallas_call(
         functools.partial(finish_kernel, own, own_ff),
         grid=(4,),
-        in_specs=[once(order.shape), block, block] + [once(a.shape) for a in rest],
+        in_specs=[block, block] + [once(a.shape) for a in rest],
         out_specs=[lines, lines] + [once(o.shape) for o in outs[2:]],
         out_shape=outs,
         compiler_params=pltpu.CompilerParams(vmem_limit_bytes=60 * MIB),
         name="finish",
-    )(order, split(rows), split(grads), *rest)
+    )(split(rows), split(grads), *rest)
 
 
 def on_device(wide, narrow, latents, condition, valid_mask, ada_weight, ada_bias, dw1_kernel, dw1_bias,
@@ -1350,10 +1366,12 @@
     small = sum(
         jnp.pad(v, ((row, 32 - row - v.shape[0]), (0, 128 - v.shape[1]))) for row, v in parts
     )
-    mask = jnp.broadcast_to(valid_mask[0].astype(BF16)[:, None], (latents.shape[1], 128))
-    order = order_matrix()
-
-    fc2a, fc2b_rows = fc2_weight[: own_ff // 2], fc2_weight[own_ff // 2 :]
+    half = own_ff // 2
+    if half % 16:
+        fc2a, fc2_rows, spans = fc2_weight[:half], fc2_weight[half:], (None, None)
+    else:
+        fc2a = fc2_rows = fc2_weight
+        spans = ((0, half), (half, half))
     chunks = [(0, 0, 128)] + thirds(2, 3 * model) + [(3, 0, model)]
     stages = wide.bit_length()
     plan = [steady(c, stages) for c in range(5)]
@@ -1362,8 +1380,8 @@
     plan += [[6 + c] + steady(needed + 1 + c, stages - 1) for c in range(6)]
     (mod, sils, model_small, hidden_small, lat, gout, g2, normed, mixed, keep, fc2b, fc1b, fc1_one, qkv,
      proj, fc2_one) = front(
-        wide, narrow, latents[0], out_cotangent[0], mask, order, condition, ada_weight, bias_at, small,
-        fc1_weight, [qkv_weight, proj_weight, fc2a], chunks, plan,
+        wide, narrow, latents[0], out_cotangent[0], valid_mask, condition, ada_weight, bias_at, small,
+        fc1_weight, [qkv_weight, proj_weight, fc2a], (None, None, spans[0]), chunks, plan,
     )
     qkv, proj = qkv.reshape(model, 3 * model), proj.reshape(model, model)
     triple, probs, att, branch, n2, n2t, fc1_one, fc2_one = attend(
@@ -1376,11 +1394,11 @@
     as_lines = lambda grad: grad.reshape(*bit_sizes(wide), grad.shape[0] // wide, grad.shape[1])
     two, gn2, fc1g, fc2g, sums_a, fc1_two, fc2_two = feed_forward(
         wide, narrow, n2, n2t, g2, as_fc1(fc1_one), hidden_small, 0, as_fc2(fc2_one),
-        [fc1b, fc2b_rows], chunks,
+        [fc1b, fc2_rows], (None, spans[1]), chunks,
     )
     two, gn2, fc1h, fc2h, sums_b, fc1o, fc2o = feed_forward(
         wide, narrow, n2, n2t, g2, as_fc1(fc1_two), hidden_small, 1, as_fc2(fc2_two),
-        [as_lines(fc1g), as_lines(fc2g)], chunks, (two, gn2),
+        [as_lines(fc1g), as_lines(fc2g)], (None, None), chunks, (two, gn2),
     )
     rows, grads, ada_wgrad, pieces, small, qkvg, projg, fc1p, fc2p = back(
         wide, narrow, gn2, two, branch, gout, att, mixed, triple, probs,
@@ -1389,7 +1407,7 @@
     )
     (out, xg, ada_wgrad, qkvg, projg, fc1g, fc2g, cond_grad, ada_bgrad, dw1k, dw1b, projb, fc2bg, dw2k,
      dw2b, fc1bg) = finish(
-        order, rows, grads, ada_wgrad, qkvg, projg, (fc1o, fc1p), (fc2o, fc2p), small, condition, pieces
+        rows, grads, ada_wgrad, qkvg, projg, (fc1o, fc1p), (fc2o, fc2p), small, condition, pieces
     )
     return (
         out[None], xg[None], cond_grad, ada_wgrad, ada_bgrad[0], dw1k, dw1b[0], qkvg, projg, projb[0],

time: 281 us -> 275 us (0.979)
  Pallas kernels: 274 us -> 271 us
where the time goes in v5:
time: 275 us
  Pallas kernels  271 us (99%)
    pallas_call x2, Pallas kernels, feed_forward(): pl.pallas_call(functools.partial(ff_kernel, wide, narrow, chunks, spans,...  97.6 us
    pallas_call x1, Pallas kernels, back(): pl.pallas_call(functools.partial(back_kernel, wide, narrow, chunks, plan,...  80.6 us
    pallas_call x1, Pallas kernels, front(): pl.pallas_call(functools.partial(front_kernel, wide, narrow, chunks, plan...  53 us
    pallas_call x1, Pallas kernels, attend(): pl.pallas_call(functools.partial(attend_kernel, wide, narrow, chunks, pla...  33.6 us
    pallas_call x1, Pallas kernels, finish(): pl.pallas_call(functools.partial(finish_kernel, own, own_ff), grid=(4,),...  6.25 us

profile of v5, /device:TPU:0, one launch (start us, length us, event | category | flops | bytes accessed | tf_op | source)
XLA Modules:
  0.0 274.8 jit_solution(9915698160519305640)
XLA Ops:
  0.7 0.7 broadcast_in_dim.40
  1.3 1.4 pad_add_fusion.refs_6_
  2.7 0.2 dynamic_update_slice.3.refs_5_
  2.9 0.0 copy-start
  2.9 0.6 copy-done
  3.5 53.0 %front.1 = (f32[8,768]{1,0:T(8,128)}, f32[32,128]{1,0:T(8,128)}, f32[16,768]{1,0:T(8,128)}, f32[16,3072]{1,0:T(8,128)}, bf16[1024,768]{1,0:T(8,128)(2,1)}, /*ind...) custom-call(bf16[1024,768]{1,0:T(8,128)(2,1)} %bitcast.42, ...), custom_call_target="tpu_custom_call" | custom-call | tf_op jit(solution)/shard_map/front/pallas_call | solution.py:892
  56.5 33.6 %attend.1 = (bf16[1024,2304]{1,0:T(8,128)(2,1)}, bf16[12,4,256,256]{3,2,1,0:T(8,128)(2,1)}, bf16[1024,768]{1,0:T(8,128)(2,1)}, f32[1024,768]{1,0:T(8,128)}, bf16...) custom-call(bf16[1024,768]{1,0:T(8,128)(2,1)} %get-tuple-element.79., ...), custom_call_target="tpu_custom_call", output_to_operand_aliasing={{6}: (7, {}), {7}: (8, {})} | custom-call | tf_op jit(solution)/shard_map/attend/pallas_call | solution.py:979
  90.1 49.9 %feed_forward.2 = (f32[1024,768]{1,0:T(8,128)}, f32[1024,768]{1,0:T(8,128)}, bf16[768,1536]{1,0:T(8,128)(2,1)}, bf16[1536,768]{1,0:T(8,128)(2,1)}, f32[16,1536]{...) custom-call(bf16[1024,768]{1,0:T(8,128)(2,1)} %get-tuple-element.88.refs_0_, ...), custom_call_target="tpu_custom_call" | custom-call | tf_op jit(solution)/shard_map/feed_forward/pallas_call | solution.py:321
  140.1 47.7 %feed_forward.3 = (f32[1024,768]{1,0:T(8,128)}, f32[1024,768]{1,0:T(8,128)}, bf16[768,1536]{1,0:T(8,128)(2,1)}, bf16[1536,768]{1,0:T(8,128)(2,1)}, f32[16,1536]{...) custom-call(bf16[1024,768]{1,0:T(8,128)(2,1)} %get-tuple-element.88.refs_0_, ...), custom_call_target="tpu_custom_call" | custom-call | tf_op jit(solution)/shard_map/feed_forward/pallas_call | solution.py:321
  187.8 80.6 %attend_back.1 = (bf16[1024,768]{1,0:T(8,128)(2,1)}, bf16[1024,768]{1,0:T(8,128)(2,1)}, f32[24,4608]{1,0:T(8,128)}, f32[32,1,128]{2,1,0:T(1,128)}, f32[24,128]{1...) custom-call(f32[1024,768]{1,0:T(8,128)} %get-tuple-element.101.refs_0_, ...), custom_call_target="tpu_custom_call" | custom-call | tf_op jit(solution)/shard_map/attend_back/pallas_call | solution.py:1249
  268.4 6.3 %finish.1 = (bf16[1024,768]{1,0:T(8,128)(2,1)}, bf16[1024,768]{1,0:T(8,128)(2,1)}, f32[24,4608]{1,0:T(8,128)}, f32[24,2304]{1,0:T(8,128)}, f32[24,768]{1,0:T(8,1...) custom-call(bf16[4,4,64,768]{3,2,1,0:T(8,128)(2,1)} %bitcast.44, ...), custom_call_target="tpu_custom_call" | custom-call | tf_op jit(solution)/shard_map/finish/pallas_call | solution.py:1341
  (1 shorter events, 0.0 us)
Async XLA Ops:
  2.9 0.6 copy-start

commit v6 on v5

--- a/solution.py
+++ b/solution.py
@@ -1004,17 +1004,17 @@
 
 
 def back_kernel(wide, narrow, chunks, plan, own, own_ff, *refs):
-    (gn2_ref, two_ref, branch_ref, gout_ref, att_ref, mixed_ref,
+    (gn2_ref, two_ref, branch_ref, gout_ref, att_hbm, mixed_hbm,
      q_ref, k_ref, v_ref, probs_ref, mod_ref, small_ref, proj_ref, wq_ref, wk_ref, wv_ref,
-     lat_ref, normed_hbm, fc2b_ref, hida_ref, hidb_ref, sils_ref, ada_ref, fc1s_ref,
-     fc2s_ref) = refs[:25]
+     lat_ref, normed_hbm, fc2b_ref, hida_ref, hidb_ref, sils_ref, ada_ref, fc1s_hbm,
+     fc2s_hbm) = refs[:25]
     (rows_ref, xg_ref, wgrad_ref, cond_ref, small_out, qkvg_ref, projg_ref, fc1g_ref,
      fc2g_ref) = refs[25:34]
     (ga, gmid, gmix, gmoved, sums, proj_src, qkv_src, early, late, cuts, cuts_in, hcuts, hcuts_in, part, cond_in,
-     gt, normed_ref, held,
+     gt, normed_ref, att_ref, mixed_ref, fc1s_ref, fc2s_ref, fetched,
      send_a, recv_a, send_b, recv_b, send_c, recv_c, send_d, recv_d, send_e, recv_e, send_f, recv_f,
-     send_g, recv_g) = refs[34:66]
-    buffers, (sends, recvs) = refs[66:-2], refs[-2:]
+     send_g, recv_g) = refs[34:70]
+    buffers, (sends, recvs) = refs[70:-2], refs[-2:]
     step = pl.program_id(0)
     model = lat_ref.shape[1]
     slabs = model // 128
@@ -1025,12 +1025,16 @@
                          [fc1g_ref, fc2g_ref, projg_ref, qkvg_ref], buffers, sends, recvs, chunks,
                          plan)
     gbl = xg_ref
+    later = [(fc1s_hbm, fc1s_ref), (fc2s_hbm, fc2s_ref), (att_hbm, att_ref), (mixed_hbm, mixed_ref),
+             (normed_hbm, normed_ref)]
+    fetch = [pltpu.make_async_copy(src, dst, fetched.at[i]) for i, (src, dst) in enumerate(later)]
     mine = lambda ref: ref.at[p.core, p.slot]
 
     @pl.when(step == 0)
     def _():
         greet_all(p)
-        pltpu.make_async_copy(normed_hbm, normed_ref, held).start()
+        for copy in fetch:
+            copy.start()
         sums[...] = jnp.zeros_like(sums)
         gmix[...] = jnp.zeros_like(gmix)
         clear_edges(gmoved)
@@ -1066,6 +1070,8 @@
     @pl.when(step == 0)
     def _():
         met(p.total - 1)
+        fetch[0].wait()
+        fetch[1].wait()
         waves.run(0)
         waves.run(1)
         p.to_all(lambda sid: hcuts.at[sid], hcuts_in.at[p.sid], send_g, recv_g)
@@ -1075,6 +1081,8 @@
 
     @pl.when(step == 3)
     def _():
+        fetch[2].wait()
+        fetch[3].wait()
         proj_src[...] = dot_tn(att_ref[...], gbl[...]).astype(BF16).reshape(proj_src.shape)
         waves.run(4)
         for i in range(4):
@@ -1137,7 +1145,7 @@
     @pl.when(step == last)
     def _():
         waves.wave = 5 + 2 * slabs
-        pltpu.make_async_copy(normed_hbm, normed_ref, held).wait()
+        fetch[4].wait()
         masks = edge_masks()
         rows_out = []
         for s in range(slabs):
@@ -1241,6 +1249,7 @@
     starts = [0, 2, 5, 8, 11, 14, 4] + [6 + 2 * s for s in range(slabs)]
     plan = [steady(c, wide.bit_length()) for c in starts]
     full = lambda a: once(a.shape)
+    anywhere = pl.BlockSpec(memory_space=pl.ANY)
     outs = [
         like((tokens, model), BF16), like((tokens, model), BF16), like((own, columns), F32),
         like((total, 1, 128), F32), like((24, 128), F32), like((own, 3 * model), F32),
@@ -1249,11 +1258,11 @@
     return pl.pallas_call(
         functools.partial(back_kernel, wide, narrow, chunks, plan, own, own_ff),
         grid=(4 + slabs,),
-        in_specs=[by_group] * 4 + [full(att), full(mixed)] + [third(tokens, i) for i in range(3)] + [
+        in_specs=[by_group] * 4 + [anywhere, anywhere] + [third(tokens, i) for i in range(3)] + [
             pl.BlockSpec((2, 4, GROUP, GROUP), lambda t: (slab(t), 0, 0, 0)),
             full(mod), full(small), full(proj), third(model, 0), third(model, 1), third(model, 2),
             full(lat), pl.BlockSpec(memory_space=pl.ANY), full(fc2b), full(hidden_sums[0]), full(hidden_sums[1]),
-            full(sils), full(ada), full(fc1s), full(fc2s),
+            full(sils), full(ada), anywhere, anywhere,
         ],
         out_specs=[by_group] + [once(o.shape) for o in outs[1:]],
         out_shape=outs,
@@ -1266,7 +1275,9 @@
             pltpu.VMEM((total, 8, 128), F32), pltpu.VMEM((total, 8, 128), F32),
             pltpu.VMEM((total, 16, 128), F32), pltpu.VMEM((total, 16, 128), F32),
             pltpu.VMEM((total, 1, 128), F32), pltpu.VMEM((total, 1, 128), F32),
-            pltpu.VMEM((tokens, 384), BF16), padded(slabs), one_sem,
+            pltpu.VMEM((tokens, 384), BF16), padded(slabs),
+            pltpu.VMEM((tokens, model), BF16), pltpu.VMEM((tokens, model), BF16),
+            pltpu.VMEM(shapes[0], BF16), pltpu.VMEM(shapes[1], BF16), pltpu.SemaphoreType.DMA((5,)),
             kin_sems, kin_sems, all_sems, all_sems, kin_sems, kin_sems, one_sem, one_sem,
             one_sem, one_sem, all_sems, all_sems, all_sems, all_sems,
             *scatter_scratch(wide, narrow, shapes), *job_sems(wide, narrow, chunks),

time: 275 us -> 273 us (level)
  no operation moved by 1% of the time
where the time goes in v6:
time: 273 us
  Pallas kernels  269 us (99%)
    pallas_call x2, Pallas kernels, feed_forward(): pl.pallas_call(functools.partial(ff_kernel, wide, narrow, chunks, spans,...  97.6 us
    pallas_call x1, Pallas kernels, back(): pl.pallas_call(functools.partial(back_kernel, wide, narrow, chunks, plan,...  78.6 us
    pallas_call x1, Pallas kernels, front(): pl.pallas_call(functools.partial(front_kernel, wide, narrow, chunks, plan...  53 us
    pallas_call x1, Pallas kernels, attend(): pl.pallas_call(functools.partial(attend_kernel, wide, narrow, chunks, pla...  33.6 us
    pallas_call x1, Pallas kernels, finish(): pl.pallas_call(functools.partial(finish_kernel, own, own_ff), grid=(4,),...  6.25 us

profile of v6, /device:TPU:0, one launch (start us, length us, event | category | flops | bytes accessed | tf_op | source)
XLA Modules:
  0.0 272.8 jit_solution(3042784678500199352)
XLA Ops:
  0.7 0.7 broadcast_in_dim.40
  1.3 1.4 pad_add_fusion.refs_6_
  2.7 0.2 dynamic_update_slice.3.refs_5_
  2.9 0.0 copy-start
  2.9 0.6 copy-done
  3.5 53.0 %front.1 = (f32[8,768]{1,0:T(8,128)}, f32[32,128]{1,0:T(8,128)}, f32[16,768]{1,0:T(8,128)}, f32[16,3072]{1,0:T(8,128)}, bf16[1024,768]{1,0:T(8,128)(2,1)}, /*ind...) custom-call(bf16[1024,768]{1,0:T(8,128)(2,1)} %bitcast.42, ...), custom_call_target="tpu_custom_call" | custom-call | tf_op jit(solution)/shard_map/front/pallas_call | solution.py:892
  56.5 33.6 %attend.1 = (bf16[1024,2304]{1,0:T(8,128)(2,1)}, bf16[12,4,256,256]{3,2,1,0:T(8,128)(2,1)}, bf16[1024,768]{1,0:T(8,128)(2,1)}, f32[1024,768]{1,0:T(8,128)}, bf16...) custom-call(bf16[1024,768]{1,0:T(8,128)(2,1)} %get-tuple-element.79., ...), custom_call_target="tpu_custom_call", output_to_operand_aliasing={{6}: (7, {}), {7}: (8, {})} | custom-call | tf_op jit(solution)/shard_map/attend/pallas_call | solution.py:979
  90.1 49.9 %feed_forward.2 = (f32[1024,768]{1,0:T(8,128)}, f32[1024,768]{1,0:T(8,128)}, bf16[768,1536]{1,0:T(8,128)(2,1)}, bf16[1536,768]{1,0:T(8,128)(2,1)}, f32[16,1536]{...) custom-call(bf16[1024,768]{1,0:T(8,128)(2,1)} %get-tuple-element.88.refs_0_, ...), custom_call_target="tpu_custom_call" | custom-call | tf_op jit(solution)/shard_map/feed_forward/pallas_call | solution.py:321
  140.1 47.7 %feed_forward.3 = (f32[1024,768]{1,0:T(8,128)}, f32[1024,768]{1,0:T(8,128)}, bf16[768,1536]{1,0:T(8,128)(2,1)}, bf16[1536,768]{1,0:T(8,128)(2,1)}, f32[16,1536]{...) custom-call(bf16[1024,768]{1,0:T(8,128)(2,1)} %get-tuple-element.88.refs_0_, ...), custom_call_target="tpu_custom_call" | custom-call | tf_op jit(solution)/shard_map/feed_forward/pallas_call | solution.py:321
  187.8 78.6 %attend_back.1 = (bf16[1024,768]{1,0:T(8,128)(2,1)}, bf16[1024,768]{1,0:T(8,128)(2,1)}, f32[24,4608]{1,0:T(8,128)}, f32[32,1,128]{2,1,0:T(1,128)}, f32[24,128]{1...) custom-call(f32[1024,768]{1,0:T(8,128)} %get-tuple-element.101.refs_0_, ...), custom_call_target="tpu_custom_call" | custom-call | tf_op jit(solution)/shard_map/attend_back/pallas_call | solution.py:1258
  266.4 6.3 %finish.1 = (bf16[1024,768]{1,0:T(8,128)(2,1)}, bf16[1024,768]{1,0:T(8,128)(2,1)}, f32[24,4608]{1,0:T(8,128)}, f32[24,2304]{1,0:T(8,128)}, f32[24,768]{1,0:T(8,1...) custom-call(bf16[4,4,64,768]{3,2,1,0:T(8,128)(2,1)} %bitcast.44, ...), custom_call_target="tpu_custom_call" | custom-call | tf_op jit(solution)/shard_map/finish/pallas_call | solution.py:1352
  (1 shorter events, 0.0 us)
Async XLA Ops:
  2.9 0.6 copy-start

commit v7 on v6

--- a/solution.py
+++ b/solution.py
@@ -1246,7 +1246,7 @@
     shapes = [fc1s.shape, fc2s.shape, (*bits, height, model), (*bits, height, 3 * model)]
     chunks = thirds(0, hidden // 2) + thirds(1, model) + [(2, 0, model)]
     chunks += [(3, 384 * s, 384) for s in range(slabs)]
-    starts = [0, 2, 5, 8, 11, 14, 4] + [6 + 2 * s for s in range(slabs)]
+    starts = [0, 3, 7, 9, 11, 13, 4] + [6 + 2 * s for s in range(slabs)]
     plan = [steady(c, wide.bit_length()) for c in starts]
     full = lambda a: once(a.shape)
     anywhere = pl.BlockSpec(memory_space=pl.ANY)

time: 273 us -> 272 us (level)
  no operation moved by 1% of the time
where the time goes in v7:
time: 272 us; the launch traced here: 271 us
  Pallas kernels  268 us (99%)
    pallas_call x2, Pallas kernels, feed_forward(): pl.pallas_call(functools.partial(ff_kernel, wide, narrow, chunks, spans,...  97.6 us
    pallas_call x1, Pallas kernels, back(): pl.pallas_call(functools.partial(back_kernel, wide, narrow, chunks, plan,...  77.3 us
    pallas_call x1, Pallas kernels, front(): pl.pallas_call(functools.partial(front_kernel, wide, narrow, chunks, plan...  53 us
    pallas_call x1, Pallas kernels, attend(): pl.pallas_call(functools.partial(attend_kernel, wide, narrow, chunks, pla...  33.6 us
    pallas_call x1, Pallas kernels, finish(): pl.pallas_call(functools.partial(finish_kernel, own, own_ff), grid=(4,),...  6.25 us

profile of v7, /device:TPU:0, one launch (start us, length us, event | category | flops | bytes accessed | tf_op | source)
XLA Modules:
  0.0 271.5 jit_solution(939445685294874513)
XLA Ops:
  0.7 0.7 broadcast_in_dim.40
  1.3 1.4 pad_add_fusion.refs_6_
  2.7 0.2 dynamic_update_slice.3.refs_5_
  2.9 0.0 copy-start
  2.9 0.6 copy-done
  3.5 53.0 %front.1 = (f32[8,768]{1,0:T(8,128)}, f32[32,128]{1,0:T(8,128)}, f32[16,768]{1,0:T(8,128)}, f32[16,3072]{1,0:T(8,128)}, bf16[1024,768]{1,0:T(8,128)(2,1)}, /*ind...) custom-call(bf16[1024,768]{1,0:T(8,128)(2,1)} %bitcast.42, ...), custom_call_target="tpu_custom_call" | custom-call | tf_op jit(solution)/shard_map/front/pallas_call | solution.py:892
  56.5 33.6 %attend.1 = (bf16[1024,2304]{1,0:T(8,128)(2,1)}, bf16[12,4,256,256]{3,2,1,0:T(8,128)(2,1)}, bf16[1024,768]{1,0:T(8,128)(2,1)}, f32[1024,768]{1,0:T(8,128)}, bf16...) custom-call(bf16[1024,768]{1,0:T(8,128)(2,1)} %get-tuple-element.79., ...), custom_call_target="tpu_custom_call", output_to_operand_aliasing={{6}: (7, {}), {7}: (8, {})} | custom-call | tf_op jit(solution)/shard_map/attend/pallas_call | solution.py:979
  90.1 49.9 %feed_forward.2 = (f32[1024,768]{1,0:T(8,128)}, f32[1024,768]{1,0:T(8,128)}, bf16[768,1536]{1,0:T(8,128)(2,1)}, bf16[1536,768]{1,0:T(8,128)(2,1)}, f32[16,1536]{...) custom-call(bf16[1024,768]{1,0:T(8,128)(2,1)} %get-tuple-element.88.refs_0_, ...), custom_call_target="tpu_custom_call" | custom-call | tf_op jit(solution)/shard_map/feed_forward/pallas_call | solution.py:321
  140.1 47.7 %feed_forward.3 = (f32[1024,768]{1,0:T(8,128)}, f32[1024,768]{1,0:T(8,128)}, bf16[768,1536]{1,0:T(8,128)(2,1)}, bf16[1536,768]{1,0:T(8,128)(2,1)}, f32[16,1536]{...) custom-call(bf16[1024,768]{1,0:T(8,128)(2,1)} %get-tuple-element.88.refs_0_, ...), custom_call_target="tpu_custom_call" | custom-call | tf_op jit(solution)/shard_map/feed_forward/pallas_call | solution.py:321
  187.8 77.3 %attend_back.1 = (bf16[1024,768]{1,0:T(8,128)(2,1)}, bf16[1024,768]{1,0:T(8,128)(2,1)}, f32[24,4608]{1,0:T(8,128)}, f32[32,1,128]{2,1,0:T(1,128)}, f32[24,128]{1...) custom-call(f32[1024,768]{1,0:T(8,128)} %get-tuple-element.101.refs_0_, ...), custom_call_target="tpu_custom_call" | custom-call | tf_op jit(solution)/shard_map/attend_back/pallas_call | solution.py:1258
  265.1 6.3 %finish.1 = (bf16[1024,768]{1,0:T(8,128)(2,1)}, bf16[1024,768]{1,0:T(8,128)(2,1)}, f32[24,4608]{1,0:T(8,128)}, f32[24,2304]{1,0:T(8,128)}, f32[24,768]{1,0:T(8,1...) custom-call(bf16[4,4,64,768]{3,2,1,0:T(8,128)(2,1)} %bitcast.44, ...), custom_call_target="tpu_custom_call" | custom-call | tf_op jit(solution)/shard_map/finish/pallas_call | solution.py:1352
  (1 shorter events, 0.0 us)
Async XLA Ops:
  2.9 0.6 copy-start
